TPU v7x, 256 devices: a whole 4x4x8 slice. The times are simulated.
256 devices in a mesh: gx: 8 (over z_hi, x), gz: 32 (over z_lo, y, core).
Axes of the slice: x: 4, y: 4, z: 8 (z_hi: 2, z_lo: 4; z = z_hi * 4 + z_lo), core: 2. Of those that a mesh axis runs over, the one named last changes fastest.
Arguments:
- tokens: bfloat16 [64, 8, 256, 768], P('gx', None, 'gz'), may hold values from -6 to 6
- body_mask: int32 [64, 8, 256], P('gx', None, 'gz'), may hold values 0 or 1
- cotangent: bfloat16 [64, 8, 256, 768], P('gx', None, 'gz'), may hold values from -6 to 6
- input_proj: bfloat16 [768, 1152], replicated, may hold values from -2 to 6
- output_proj: bfloat16 [384, 768], replicated, may hold values from -0.3125 to 0.3125
- coarse_proj: bfloat16 [768, 768], replicated, may hold values from -0.21875 to 0.21875
Outputs:
- block_out: bfloat16 [64, 8, 256, 768], P('gx', None, 'gz')
- token_grad: bfloat16 [64, 8, 256, 768], P('gx', None, 'gz')
- input_grad: float32 [768, 1152], P(('gx', 'gz'))
- output_grad: float32 [384, 768], P(None, ('gx', 'gz'))
- coarse_grad: float32 [768, 768], P(('gx', 'gz'))
All inputs are finite; a program needn't handle non-finite values. No bound on the sum of `body_mask` on one device may be relied on, other than what follows from the above.
Results may differ from a plain program's by a relative error of at most 0.015.
The roundings to bfloat16 on the way count: a program that leaves them out, or rounds other values in their place, can miss the bound.
Values may be sent and summed in bfloat16 or wider, within the bound.
No kernel may reach another device: no remote copies, remote signals or barrier semaphores. Data moves between devices by JAX's collectives and lax.ppermute only.
A program may use at most 128 MiB of HBM per device.

v0:
```python
import functools

import jax
import jax.numpy as jnp
from jax import lax
from jax.experimental import pallas as pl
from jax.experimental.pallas import tpu as pltpu
from jax.sharding import Mesh
from jax.sharding import PartitionSpec as P

HEAD = 64
PAIR = 2 * HEAD
CHUNK = 256
HIDDEN = -1e30
GX = ("zh", "x")
GZ = ("zl", "y", "core")
ALL = GX + GZ
bf16 = jnp.bfloat16
f32 = jnp.float32


def dot(left, right):
    return jnp.dot(left, right, preferred_element_type=f32)


def dot_nt(left, right):
    return lax.dot_general(left, right, (((1,), (1,)), ((), ())), preferred_element_type=f32)


def call(kernel, outs, *args, scratch=(), flops=0, size=0):
    return pl.pallas_call(
        kernel,
        out_shape=[jax.ShapeDtypeStruct(s, d) for s, d in outs],
        scratch_shapes=list(scratch),
        compiler_params=pltpu.CompilerParams(vmem_limit_bytes=40 * 2**20),
        cost_estimate=pl.CostEstimate(flops=flops, bytes_accessed=size, transcendentals=0),
    )(*args)


def normalize(values):
    centre = values - jnp.mean(values, axis=-1, keepdims=True)
    inv_std = lax.rsqrt(jnp.mean(centre * centre, axis=-1, keepdims=True) + 1e-05)
    return centre * inv_std, inv_std


def low_rows(shape):
    return lax.broadcasted_iota(jnp.int32, shape, 1) < shape[1] // 2


def split_z(rows):
    m, z, d = rows.shape[0] // 2, rows.shape[1], rows.shape[2]
    pairs = rows.reshape(m, 2, z, d)
    a, b = pairs[:, 0], pairs[:, 1]
    low = low_rows(a.shape)
    lower = jnp.where(low, a, pltpu.roll(b, z // 2, 1))
    upper = jnp.where(low, pltpu.roll(a, z // 2, 1), b)
    return lower.reshape(m * z, d), upper.reshape(m * z, d)


def join_z(lower, upper):
    m, d = lower.shape[0] // 8, lower.shape[1]
    lower, upper = lower.reshape(m, 8, d), upper.reshape(m, 8, d)
    low = low_rows(lower.shape)
    a = jnp.where(low, lower, pltpu.roll(upper, 4, 1))
    b = jnp.where(low, pltpu.roll(lower, 4, 1), upper)
    return jnp.stack([a, b], axis=1).reshape(2 * m, 8, d)


def x_half(ref, half):
    x, y, z, d = ref.shape
    rows = ref[half * (x // 2) : (half + 1) * (x // 2)].astype(f32)
    return rows.reshape(x // 2 * y, z, d)


def prepare(tok_ref, cot_ref, wo_ref, wc_ref, both_ref, right_ref, up_ref, own_ref, coarse_ref):
    d = tok_ref.shape[3]
    total = jnp.zeros((1, d), f32)
    cells = 1
    for n in tok_ref.shape[:3]:
        cells *= n
    for half, refs in ((0, (both_ref, right_ref)), (1, (up_ref, own_ref))):
        normed, _ = normalize(x_half(tok_ref, half))
        total += jnp.sum(jnp.sum(normed, axis=0), axis=0, keepdims=True)
        for ref, part in zip(refs, split_z(normed)):
            ref[:, :d] = part.astype(bf16)
        for ref, part in zip(refs, split_z(x_half(cot_ref, half))):
            ref[:, d:] = dot_nt(part.astype(bf16), wo_ref[...]).astype(bf16)
    pooled = jnp.broadcast_to((total / cells).astype(bf16), (coarse_ref.shape[0], d))
    coarse_ref[:, :d] = pooled
    coarse_ref[:, d:] = dot(pooled, wc_ref[...]).astype(bf16)


def turn_cot(cot_ref, src_ref, out_ref):
    d = cot_ref.shape[3]
    parts = []
    for half in (0, 1):
        parts += [p.astype(bf16) for p in split_z(x_half(cot_ref, half))]
    perm = picks(src_ref, d)
    n = parts[0].shape[0]
    for i, part in enumerate(parts):
        out_ref[:, i * n : (i + 1) * n] = dot_nt(perm, part).astype(bf16)


def picks(src_ref, d):
    columns = lax.broadcasted_iota(jnp.int32, (d, d), 1)
    return jnp.where(columns == src_ref[...], 1.0, 0.0).astype(bf16)


def head_of(pair, half):
    lanes = lax.broadcasted_iota(jnp.int32, pair.shape, 1)
    return jnp.where((lanes < HEAD) == (half == 0), pair, jnp.zeros_like(pair))


def attend(own_ref, up_ref, right_ref, both_ref, wi_ref, kv_ref, mask_ref,
           a0_ref, a1_ref, a2_ref, a3_ref, q_ref, k_ref, v_ref, m_ref, l_ref, out_ref):
    d, width = wi_ref.shape
    inner = width // 3
    n = own_ref.shape[0]
    tokens = 4 * n
    for i, ref in enumerate((own_ref, up_ref, right_ref, both_ref)):
        packed = dot(ref[:, :d], wi_ref[...])
        rows = slice(i * n, (i + 1) * n)
        q_ref[rows] = packed[:, :inner].astype(bf16) * bf16(0.125)
        k_ref[rows] = packed[:, inner : 2 * inner].astype(bf16)
        v_ref[rows] = packed[:, 2 * inner :].astype(bf16)
    k_ref[tokens:] = kv_ref[:, d : d + inner]
    v_ref[tokens:] = kv_ref[:, d + inner :]
    eye = jnp.where(
        lax.broadcasted_iota(jnp.int32, (PAIR, PAIR), 0)
        == lax.broadcasted_iota(jnp.int32, (PAIR, PAIR), 1), 1.0, 0.0).astype(bf16)
    chunks = tokens // CHUNK
    m_ref[...] = jnp.zeros_like(m_ref)
    l_ref[...] = jnp.zeros_like(l_ref)

    def step(i, _):
        lanes = pl.ds(pl.multiple_of(i // chunks * PAIR, PAIR), PAIR)
        rows = pl.ds(pl.multiple_of(i % chunks * CHUNK, CHUNK), CHUNK)
        keys = k_ref[:, lanes]
        vals_t = dot_nt(eye, v_ref[:, lanes]).astype(bf16)
        query = q_ref[rows, lanes]
        found = []
        for half in range(2):
            s = dot_nt(keys, head_of(query, half)) + mask_ref[...]
            top = jnp.max(s, axis=0, keepdims=True)
            e = jnp.exp(s - top)
            inv = 1.0 / jnp.sum(e, axis=0, keepdims=True)
            weight = (e * inv).astype(bf16)
            found.append(dot(vals_t[half * HEAD : (half + 1) * HEAD], weight))
            m_ref[pl.ds(2 * i + half, 1)] = top
            l_ref[pl.ds(2 * i + half, 1)] = inv
        out_ref[rows, lanes] = jnp.concatenate(found, axis=0).T.astype(bf16)
        return 0

    lax.fori_loop(0, inner // PAIR * chunks, step, 0)
    for i, ref in enumerate((a0_ref, a1_ref, a2_ref, a3_ref)):
        ref[...] = out_ref[i * n : (i + 1) * n]


def attend_back(own_ref, up_ref, right_ref, both_ref, wi_ref, mask_ref, q_ref, k_ref, v_ref, m_ref, l_ref,
                d0_ref, d1_ref, d2_ref, d3_ref, grad_ref, coarse_ref, g_ref, dk_ref, dv_ref):
    d, width = wi_ref.shape
    inner = width // 3
    n = own_ref.shape[0]
    tokens = 4 * n
    for i, ref in enumerate((own_ref, up_ref, right_ref, both_ref)):
        g_ref[i * n : (i + 1) * n] = ref[:, d:]
    eye = jnp.where(
        lax.broadcasted_iota(jnp.int32, (PAIR, PAIR), 0)
        == lax.broadcasted_iota(jnp.int32, (PAIR, PAIR), 1), 1.0, 0.0).astype(bf16)
    chunks = tokens // CHUNK
    dk_ref[...] = jnp.zeros_like(dk_ref)
    dv_ref[...] = jnp.zeros_like(dv_ref)

    def step(i, _):
        lanes = pl.ds(pl.multiple_of(i // chunks * PAIR, PAIR), PAIR)
        rows = pl.ds(pl.multiple_of(i % chunks * CHUNK, CHUNK), CHUNK)
        keys = k_ref[:, lanes]
        vals = v_ref[:, lanes]
        keys_t = dot_nt(eye, keys).astype(bf16)
        found = []
        dv = dv_ref[:, lanes]
        dk = dk_ref[:, lanes]
        for half in range(2):
            query = head_of(q_ref[rows, lanes], half)
            g = head_of(g_ref[rows, lanes], half)
            s = dot_nt(keys, query) + mask_ref[...]
            prob = jnp.exp(s - m_ref[pl.ds(2 * i + half, 1)]) * l_ref[pl.ds(2 * i + half, 1)]
            dv += dot(prob.astype(bf16), g)
            spread = prob * dot_nt(vals, g)
            centre = jnp.sum(spread, axis=0, keepdims=True)
            score = (spread - prob * centre).astype(bf16)
            dk += dot(score, query)
            found.append(dot(keys_t[half * HEAD : (half + 1) * HEAD], score))
        dv_ref[:, lanes] = dv
        dk_ref[:, lanes] = dk
        grad_ref[rows, lanes] = (jnp.concatenate(found, axis=0).T * 0.125).astype(bf16)
        return 0

    lax.fori_loop(0, inner // PAIR * chunks, step, 0)
    grad_ref[:, inner : 2 * inner] = dk_ref[:tokens].astype(bf16)
    grad_ref[:, 2 * inner :] = dv_ref[:tokens].astype(bf16)
    coarse_ref[:, :inner] = dk_ref[tokens:].astype(bf16)
    coarse_ref[:, inner:] = dv_ref[tokens:].astype(bf16)
    for i, ref in enumerate((d0_ref, d1_ref, d2_ref, d3_ref)):
        ref[...] = dot_nt(grad_ref[i * n : (i + 1) * n], wi_ref[...]).astype(bf16)


def weight_grads(own_ref, up_ref, right_ref, both_ref, src_ref, grad_ref, cot_ref,
                 b0_ref, b1_ref, b2_ref, b3_ref, keep_ref, send_ref, turned_ref, att_ref):
    d = src_ref.shape[0]
    n = own_ref.shape[0]
    width = grad_ref.shape[1]
    perm = picks(src_ref, d)
    for i, ref in enumerate((own_ref, up_ref, right_ref, both_ref)):
        turned_ref[:, i * n : (i + 1) * n] = dot_nt(perm, ref[:, :d]).astype(bf16)
    for i, ref in enumerate((b0_ref, b1_ref, b2_ref, b3_ref)):
        att_ref[i * n : (i + 1) * n] = ref[...]
    for ref, rows in ((keep_ref, slice(0, d // 2)), (send_ref, slice(d // 2, d))):
        ref[:, :width] = dot(turned_ref[rows], grad_ref[...]).astype(bf16)
        ref[:, width:] = dot(cot_ref[rows], att_ref[...]).astype(bf16)


def block_result(tok_ref, b0_ref, b1_ref, b2_ref, b3_ref, wo_ref, out_ref):
    x = tok_ref.shape[0]
    for half, refs in ((0, (b0_ref, b1_ref)), (1, (b2_ref, b3_ref))):
        branch = [dot(ref[...], wo_ref[...]).astype(bf16).astype(f32) for ref in refs]
        total = x_half(tok_ref, half) + join_z(*branch)
        out_ref[half * (x // 2) : (half + 1) * (x // 2)] = total.astype(bf16).reshape(
            (x // 2,) + out_ref.shape[1:])


def coarse_total(parts_ref, wc_ref, rows_ref, pooled_ref):
    total = jnp.sum(parts_ref[...].astype(f32), axis=0, keepdims=True).astype(bf16)
    rows_ref[...] = jnp.broadcast_to(total, rows_ref.shape)
    pooled_ref[...] = dot_nt(jnp.broadcast_to(total, (8, total.shape[1])), wc_ref[...])


def token_result(tok_ref, cot_ref, b0_ref, b1_ref, b2_ref, b3_ref, pooled_ref, out_ref):
    x, y, z, d = tok_ref.shape
    pooled = (pooled_ref[0:1] / float(x * y * z))[None]
    for half, refs in ((0, (b0_ref, b1_ref)), (1, (b2_ref, b3_ref))):
        normed, inv_std = normalize(x_half(tok_ref, half))
        grad = join_z(*[ref[...].astype(f32) for ref in refs]) + pooled
        first = jnp.mean(grad, axis=-1, keepdims=True)
        second = jnp.mean(grad * normed, axis=-1, keepdims=True)
        total = x_half(cot_ref, half) + inv_std * (grad - first - normed * second)
        out_ref[half * (x // 2) : (half + 1) * (x // 2)] = total.astype(bf16).reshape(
            (x // 2,) + out_ref.shape[1:])


def moved(block, dx, dz):
    nx, nz = lax.axis_size(GX), lax.axis_size(GZ)
    route = [
        (a * nz + c, ((a + dx) % nx) * nz + (c + dz) % nz)
        for a in range(nx)
        for c in range(nz)
    ]
    return lax.ppermute(block, ALL, route)


def mask_quads(a):
    x, y, z = a.shape
    a = jnp.moveaxis(a.reshape(2, x // 2, y, 2, z // 2), 3, 1)
    return a.reshape(2, 2, 1, x * y * z // 4)


def returned(own, up, right, both):
    return moved(both, 1, 1), moved(right, 1, 0), moved(up, 0, 1), own


def body(tokens, body_mask, cotangent, w_in, w_out, w_coarse):
    x, y, z, d = tokens.shape
    size = x * y * z
    n = size // 4
    inner = w_out.shape[0]
    coarse = lax.axis_size(GZ)
    columns = lax.axis_size(GX)
    devices = columns * coarse
    per = d // devices
    core = lax.axis_index("core")

    quads = mask_quads(body_mask)
    masks = [quads[1, 1], moved(quads[1, 0], 0, -1), moved(quads[0, 1], -1, 0), moved(quads[0, 0], -1, -1)]
    live = jnp.concatenate(masks + [jnp.ones((1, coarse), jnp.int32)], axis=1)
    mask = jnp.where(live > 0, 0.0, HIDDEN).reshape(size + coarse, 1)

    wide = (n, d + inner)
    both, right, up, own, far = call(
        prepare, [(wide, bf16)] * 4 + [((coarse, 2 * d), bf16)], tokens, cotangent, w_out, w_coarse,
        flops=4 * size * d * inner, size=10 * size * d)
    up, right, both = moved(up, 0, -1), moved(right, -1, 0), moved(both, -1, -1)
    far = lax.all_to_all(far, GZ, 0, 0, tiled=True)
    pooled = far[:, :d]

    row = jnp.arange(d, dtype=jnp.int32)
    half = row // (d // 2)
    rest = row % (d // 2)
    src = (rest // per * 2 + (half + core) % 2) * per + rest % per
    src = src.reshape(d, 1)
    (cot_turned,) = call(turn_cot, [((d, size), bf16)], cotangent, src, flops=2 * size * d * d, size=4 * size * d)

    slim = (n, inner)
    a0, a1, a2, a3, q, k, v, top, inv = call(
        attend,
        [(slim, bf16)] * 4
        + [((size, inner), bf16), ((size + coarse, inner), bf16), ((size + coarse, inner), bf16)]
        + [((16, CHUNK), f32)] * 2,
        own, up, right, both, w_in, far, mask,
        scratch=[pltpu.VMEM((size, inner), bf16)], flops=6 * size * d * inner + 8 * size * size * inner, size=8 * size * d)
    b0, b1, b2, b3 = returned(a0, a1, a2, a3)

    d0, d1, d2, d3, grad, coarse_part = call(
        attend_back,
        [((n, d), bf16)] * 4 + [((size, 3 * inner), bf16), ((coarse, 2 * inner), bf16)],
        own, up, right, both, w_in, mask, q, k, v, top, inv,
        scratch=[pltpu.VMEM((size, inner), bf16)] + [pltpu.VMEM((size + coarse, inner), f32)] * 2,
        flops=6 * size * d * inner + 16 * size * size * inner, size=10 * size * d)
    e0, e1, e2, e3 = returned(d0, d1, d2, d3)
    parts = lax.all_to_all(coarse_part, GZ, 0, 0, tiled=True)

    keep, send = call(
        weight_grads, [((d // 2, 4 * inner), bf16)] * 2,
        own, up, right, both, src, grad, cot_turned, b0, b1, b2, b3,
        scratch=[pltpu.VMEM((d, size), bf16), pltpu.VMEM((size, inner), bf16)],
        flops=12 * size * d * inner, size=10 * size * d)
    other = lax.ppermute(send, "core", [(0, 1), (1, 0)])
    chips = devices // 2
    chip_sum = (keep.astype(f32) + other.astype(f32)).astype(bf16).reshape(chips, per, 4 * inner)
    got = lax.all_to_all(chip_sum, GX + ("zl", "y"), 0, 0)

    (block_out,) = call(
        block_result, [(tokens.shape, bf16)], tokens, b0, b1, b2, b3, w_out, flops=2 * size * d * inner, size=6 * size * d)

    rows, grad_pooled = call(
        coarse_total, [((coarse, 2 * inner), bf16), ((8, d), f32)], parts, w_coarse, size=2 * d * d)
    grads_far = lax.all_to_all(rows, GZ, 0, 0, tiled=True)
    picked = lax.dynamic_slice_in_dim(
        pooled.reshape(coarse, columns, d // columns), lax.axis_index(GZ) * per, per, axis=2)
    share = jnp.einsum("mcj,me->cje", picked, grads_far, preferred_element_type=f32)
    coarse_grad = jnp.sum(lax.all_to_all(share, GX, 0, 0), axis=0)

    (token_grad,) = call(
        token_result, [(tokens.shape, bf16)], tokens, cotangent, e0, e1, e2, e3, grad_pooled, size=8 * size * d)

    summed = jnp.sum(got.astype(f32), axis=0)
    input_grad = summed[:, : 3 * inner]
    output_grad = summed[:, 3 * inner :].T
    return (block_out, token_grad, input_grad, output_grad, coarse_grad)


def solution(mesh):
    fine = Mesh(mesh.devices.reshape(2, 4, 4, 4, 2), ALL)
    grid = P(GX, None, GZ, None)
    return jax.shard_map(
        body,
        mesh=fine,
        in_specs=(grid, P(GX, None, GZ), grid, P(), P(), P()),
        out_specs=(grid, grid, P(ALL, None), P(None, ALL), P(ALL, None)),
        check_vma=False,
    )
```

profile of v0, /device:TPU:1, one launch (start us, length us, event | category | flops | bytes accessed | tf_op | source)
XLA Modules:
  0.0 215.4 jit_solution(8602668938229942011)
XLA Ops:
  1.8 3.3 %collective-permute-start.3 = (s32[1,128]{1,0:T(1,128)S(1)}, s32[1,128]{1,0:T(1,128)S(1)}, u32[]{:S(2)}, u32[]{:S(2)}) collective-permute-start(s32[1,128]{1,0:T(1,128)S(1)} %get-tuple-element.55), channel_id=1, source_target_pairs={{0,31},{1,0},{2,1},{3,2},{4,3},{5,4},{6,5},{7,6},{8,7},{9,8},{10,9... | collective-permute-start | bytes 1544 | tf_op jit(solution)/shard_map/ppermute | solution.py:258
  5.1 7.4 %collective-permute-start.4 = (s32[1,128]{1,0:T(1,128)S(1)}, s32[1,128]{1,0:T(1,128)S(1)}, u32[]{:S(2)}, u32[]{:S(2)}) collective-permute-start(s32[1,128]{1,0:T(1,128)S(1)} %get-tuple-element.54), channel_id=1, source_target_pairs={{0,224},{1,225},{2,226},{3,227},{4,228},{5,229},{6,230},{7,231},{8... | collective-permute-start | bytes 1544 | tf_op jit(solution)/shard_map/ppermute | solution.py:258
  12.4 4.5 %collective-permute-start.5 = (s32[1,128]{1,0:T(1,128)S(1)}, s32[1,128]{1,0:T(1,128)S(1)}, u32[]{:S(2)}, u32[]{:S(2)}) collective-permute-start(s32[1,128]{1,0:T(1,128)S(1)} %get-tuple-element.53), channel_id=1, source_target_pairs={{0,255},{1,224},{2,225},{3,226},{4,227},{5,228},{6,229},{7,230},{8... | collective-permute-start | bytes 1544 | tf_op jit(solution)/shard_map/ppermute | solution.py:258
  21.6 1.9 shard_map.101
  25.3 3.6 %all-to-all-start = ((bf16[32,2,768]{2,1,0:T(2,128)(2,1)}), bf16[32,2,768]{2,1,0:T(2,128)(2,1)S(1)}, u32[]{:S(2)}, u32[]{:S(2)}) async-start(bf16[32,2,768]{2,1,0:T(2,128)(2,1)} %reshape.252), calls=%async_computation | async-start | bytes 196608 | tf_op jit(solution)/shard_map/all_to_all | solution.py:292
  32.8 6.0 %collective-permute-start.2 = (bf16[128,1152]{1,0:T(8,128)(2,1)S(1)}, bf16[128,1152]{1,0:T(8,128)(2,1)S(1)}, u32[]{:S(2)}, u32[]{:S(2)}) collective-permute-start(bf16[128,1152]{1,0:T(8,128)(2,1)S(1)} %get-tuple-element.32), channel_id=1, source_target_pairs={{0,255},{1,224},{2,225},{3,226},{4,227},{5,228},{6,229},{7,230},{8... | collective-permute-start | bytes 884744 | tf_op jit(solution)/shard_map/ppermute | solution.py:258
  39.2 17.9 %collective-permute-done.2.both_ref = bf16[128,1152]{1,0:T(8,128)(2,1)S(1)} collective-permute-done((bf16[128,1152]{1,0:T(8,128)(2,1)S(1)}, bf16[128,1152]{1,0:T(8,128)(2,1)S(1)}, u32[]{:S(2)}, u32[]{:S(2)}) %collective-permute-start.2) | collective-permute-done | bytes 294944 | tf_op jit(solution)/shard_map/ppermute | solution.py:258
  58.7 8.9 %shard_map.102 = (bf16[128,384]{1,0:T(8,128)(2,1)S(1)}, bf16[128,384]{1,0:T(8,128)(2,1)S(1)}, bf16[128,384]{1,0:T(8,128)(2,1)S(1)}, bf16[128,384]{1,0:T(8,128)(2...) custom-call(bf16[128,1152]{1,0:T(8,128)(2,1)S(1)} %get-tuple-element, ...), custom_call_target="tpu_custom_call" | custom-call | flops 1711276032 | bytes 3145728 | tf_op jit(solution)/shard_map/pallas_call | solution.py:31
  68.1 11.0 %shard_map.104 = (bf16[128,768]{1,0:T(8,128)(2,1)S(1)}, bf16[128,768]{1,0:T(8,128)(2,1)S(1)}, bf16[128,768]{1,0:T(8,128)(2,1)S(1)}, bf16[128,768]{1,0:T(8,128)(2...) custom-call(bf16[128,1152]{1,0:T(8,128)(2,1)S(1)} %get-tuple-element.29.own_ref, ...), custom_call_target="tpu_custom_call" | custom-call | flops 2516582400 | bytes 3932160 | tf_op jit(solution)/shard_map/pallas_call | solution.py:31
  85.9 3.9 %shard_map.108 = (bf16[384,1536]{1,0:T(8,128)(2,1)S(1)}, bf16[384,1536]{1,0:T(8,128)(2,1)}) custom-call(bf16[128,1152]{1,0:T(8,128)(2,1)S(1)} %copy-done.25, bf16[128,1152]{1,0:T(8,128)(2,1)S(1)} %copy-done.27, bf16[128,1152]{1,0:T(8,128)(2,1)S(1)} %copy-done.29, bf16[128,1152]{1,0:T(8,128)(2,1)S(1)} %copy-done.31, s32[768,1]{1,0:T(8,128)S(1)} %fusion.4.src_ref, ...), custom_call_target="tpu_custom_call" | custom-call | flops 1811939328 | bytes 3932160 | tf_op jit(solution)/shard_map/pallas_call | solution.py:31
  89.8 3.1 %collective-permute-start.12 = (bf16[384,1536]{1,0:T(8,128)(2,1)}, bf16[384,1536]{1,0:T(8,128)(2,1)}, u32[]{:S(2)}, u32[]{:S(2)}) collective-permute-start(bf16[384,1536]{1,0:T(8,128)(2,1)} %get-tuple-element.51), channel_id=1, source_target_pairs={{0,1},{1,0},{2,3},{3,2},{4,5},{5,4},{6,7},{7,6},{8,9},{9,8},{10,11... | collective-permute-start | bytes 3538952 | tf_op jit(solution)/shard_map/ppermute | solution.py:326
  95.0 7.4 %all-to-all-start.1 = ((bf16[32,2,384]{2,1,0:T(2,128)(2,1)}), bf16[32,2,384]{2,1,0:T(2,128)(2,1)S(1)}, u32[]{:S(2)}, u32[]{:S(2)}) async-start(bf16[32,2,384]{2,1,0:T(2,128)(2,1)} %reshape.254), calls=%async_computation.1 | async-start | bytes 98304 | tf_op jit(solution)/shard_map/all_to_all | solution.py:319
  103.4 6.7 %all-to-all-done.1 = bf16[32,2,384]{2,1,0:T(2,128)(2,1)S(1)} async-done(((bf16[32,2,384]{2,1,0:T(2,128)(2,1)}), bf16[32,2,384]{2,1,0:T(2,128)(2,1)S(1)}, u32[]{:S(2)}, u32[]{:S(2)}) %all-to-all-start.1) | async-done | bytes 49184 | tf_op jit(solution)/shard_map/all_to_all | solution.py:319
  112.0 3.9 %all-to-all-start.3 = ((bf16[32,2,384]{2,1,0:T(2,128)(2,1)}), bf16[32,2,384]{2,1,0:T(2,128)(2,1)S(1)}, u32[]{:S(2)}, u32[]{:S(2)}) async-start(bf16[32,2,384]{2,1,0:T(2,128)(2,1)} %reshape.256), calls=%async_computation.3 | async-start | bytes 98304 | tf_op jit(solution)/shard_map/all_to_all | solution.py:336
  116.2 7.6 %all-to-all-done.3 = bf16[32,2,384]{2,1,0:T(2,128)(2,1)S(1)} async-done(((bf16[32,2,384]{2,1,0:T(2,128)(2,1)}), bf16[32,2,384]{2,1,0:T(2,128)(2,1)S(1)}, u32[]{:S(2)}, u32[]{:S(2)}) %all-to-all-start.3) | async-done | bytes 49184 | tf_op jit(solution)/shard_map/all_to_all | solution.py:336
  124.6 10.9 %all-to-all-start.4 = ((f32[8,3,768]{2,1,0:T(4,128)}), f32[8,3,768]{2,1,0:T(4,128)S(1)}, u32[]{:S(2)}, u32[]{:S(2)}) async-start(f32[8,3,768]{2,1,0:T(4,128)} %copy.57), calls=%async_computation.4 | async-start | bytes 196608 | tf_op jit(solution)/shard_map/all_to_all | solution.py:340
  137.0 2.1 reshape.248
  139.1 5.5 %all-to-all-done.4 = f32[8,3,768]{2,1,0:T(4,128)S(1)} async-done(((f32[8,3,768]{2,1,0:T(4,128)}), f32[8,3,768]{2,1,0:T(4,128)S(1)}, u32[]{:S(2)}, u32[]{:S(2)}) %all-to-all-start.4) | async-done | bytes 73760 | tf_op jit(solution)/shard_map/all_to_all | solution.py:340
  144.6 7.3 %all-to-all-start.2 = ((bf16[128,3,1536]{2,1,0:T(4,128)(2,1)}), bf16[128,3,1536]{2,1,0:T(4,128)(2,1)}, u32[]{:S(2)}, u32[]{:S(2)}) async-start(bf16[128,3,1536]{2,1,0:T(4,128)(2,1)} %reshape.248), calls=%async_computation.2 | async-start | bytes 3145728 | tf_op jit(solution)/shard_map/all_to_all | solution.py:329
  152.5 3.5 %collective-permute-start.11 = (bf16[128,768]{1,0:T(8,128)(2,1)S(1)}, bf16[128,768]{1,0:T(8,128)(2,1)S(1)}, u32[]{:S(2)}, u32[]{:S(2)}) collective-permute-start(bf16[128,768]{1,0:T(8,128)(2,1)S(1)} %copy-done.35), channel_id=1, source_target_pairs={{0,1},{1,2},{2,3},{3,4},{4,5},{5,6},{6,7},{7,8},{8,9},{9,10},{10,1... | collective-permute-start | bytes 589832 | tf_op jit(solution)/shard_map/ppermute | solution.py:258
  158.9 37.4 %collective-permute-done.10.b1_ref = bf16[128,768]{1,0:T(8,128)(2,1)S(1)} collective-permute-done((bf16[128,768]{1,0:T(8,128)(2,1)S(1)}, bf16[128,768]{1,0:T(8,128)(2,1)S(1)}, u32[]{:S(2)}, u32[]{:S(2)}) %collective-permute-start.10) | collective-permute-done | bytes 196640 | tf_op jit(solution)/shard_map/ppermute | solution.py:258
  196.3 13.1 %collective-permute-done.9.b0_ref = bf16[128,768]{1,0:T(8,128)(2,1)S(1)} collective-permute-done((bf16[128,768]{1,0:T(8,128)(2,1)S(1)}, bf16[128,768]{1,0:T(8,128)(2,1)S(1)}, u32[]{:S(2)}, u32[]{:S(2)}) %collective-permute-start.9) | collective-permute-done | bytes 196640 | tf_op jit(solution)/shard_map/ppermute | solution.py:258
  209.4 2.1 shard_map.106
  212.1 2.1 convert_reduce_fusion
  (137 shorter events, 33.3 us)
Async XLA Ops:
  1.8 31.0 %collective-permute-start.3 = (s32[1,128]{1,0:T(1,128)S(1)}, s32[1,128]{1,0:T(1,128)S(1)}, u32[]{:S(2)}, u32[]{:S(2)}) collective-permute-start(s32[1,128]{1,0:T(1,128)S(1)} %get-tuple-element.55), channel_id=1, source_target_pairs={{0,31},{1,0},{2,1},{3,2},{4,3},{5,4},{6,5},{7,6},{8,7},{9,8},{10,9... | collective-permute-start | bytes 1544 | tf_op jit(solution)/shard_map/ppermute | solution.py:258
  5.1 33.7 %collective-permute-start.4 = (s32[1,128]{1,0:T(1,128)S(1)}, s32[1,128]{1,0:T(1,128)S(1)}, u32[]{:S(2)}, u32[]{:S(2)}) collective-permute-start(s32[1,128]{1,0:T(1,128)S(1)} %get-tuple-element.54), channel_id=1, source_target_pairs={{0,224},{1,225},{2,226},{3,227},{4,228},{5,229},{6,230},{7,231},{8... | collective-permute-start | bytes 1544 | tf_op jit(solution)/shard_map/ppermute | solution.py:258
  12.4 26.3 %collective-permute-start.5 = (s32[1,128]{1,0:T(1,128)S(1)}, s32[1,128]{1,0:T(1,128)S(1)}, u32[]{:S(2)}, u32[]{:S(2)}) collective-permute-start(s32[1,128]{1,0:T(1,128)S(1)} %get-tuple-element.53), channel_id=1, source_target_pairs={{0,255},{1,224},{2,225},{3,226},{4,227},{5,228},{6,229},{7,230},{8... | collective-permute-start | bytes 1544 | tf_op jit(solution)/shard_map/ppermute | solution.py:258
  23.4 44.6 %copy-start.24 = (bf16[128,1152]{1,0:T(8,128)(2,1)}, bf16[128,1152]{1,0:T(8,128)(2,1)S(1)}, u32[]{:S(2)}) copy-start(bf16[128,1152]{1,0:T(8,128)(2,1)S(1)} %get-tuple-element.29.own_ref) | copy-start | bytes 884740
  25.3 13.7 %all-to-all-start = ((bf16[32,2,768]{2,1,0:T(2,128)(2,1)}), bf16[32,2,768]{2,1,0:T(2,128)(2,1)S(1)}, u32[]{:S(2)}, u32[]{:S(2)}) async-start(bf16[32,2,768]{2,1,0:T(2,128)(2,1)} %reshape.252), calls=%async_computation | async-start | bytes 196608 | tf_op jit(solution)/shard_map/all_to_all | solution.py:292
  29.0 10.2 %collective-permute-start = (bf16[128,1152]{1,0:T(8,128)(2,1)}, bf16[128,1152]{1,0:T(8,128)(2,1)S(1)}, u32[]{:S(2)}, u32[]{:S(2)}) collective-permute-start(bf16[128,1152]{1,0:T(8,128)(2,1)} %get-tuple-element.30), channel_id=1, source_target_pairs={{0,31},{1,0},{2,1},{3,2},{4,3},{5,4},{6,5},{7,6},{8,7},{9,8},{10,9... | collective-permute-start | bytes 884744 | tf_op jit(solution)/shard_map/ppermute | solution.py:258
  29.1 10.1 %collective-permute-start.1 = (bf16[128,1152]{1,0:T(8,128)(2,1)S(1)}, bf16[128,1152]{1,0:T(8,128)(2,1)S(1)}, u32[]{:S(2)}, u32[]{:S(2)}) collective-permute-start(bf16[128,1152]{1,0:T(8,128)(2,1)S(1)} %get-tuple-element.31), channel_id=1, source_target_pairs={{0,224},{1,225},{2,226},{3,227},{4,228},{5,229},{6,230},{7,231},{8... | collective-permute-start | bytes 884744 | tf_op jit(solution)/shard_map/ppermute | solution.py:258
  32.8 24.3 %collective-permute-start.2 = (bf16[128,1152]{1,0:T(8,128)(2,1)S(1)}, bf16[128,1152]{1,0:T(8,128)(2,1)S(1)}, u32[]{:S(2)}, u32[]{:S(2)}) collective-permute-start(bf16[128,1152]{1,0:T(8,128)(2,1)S(1)} %get-tuple-element.32), channel_id=1, source_target_pairs={{0,255},{1,224},{2,225},{3,226},{4,227},{5,228},{6,229},{7,230},{8... | collective-permute-start | bytes 884744 | tf_op jit(solution)/shard_map/ppermute | solution.py:258
  39.2 28.4 %copy-start.8 = (bf16[32,1,1536]{2,0,1:T(8,128)(2,1)}, bf16[32,1,1536]{2,0,1:T(8,128)(2,1)S(1)}, u32[]{:S(2)}) copy-start(bf16[32,1,1536]{2,0,1:T(8,128)(2,1)S(1)} %copy.68) | copy-start | bytes 294916
  39.2 28.9 %copy-start.26 = (bf16[128,1152]{1,0:T(8,128)(2,1)}, bf16[128,1152]{1,0:T(8,128)(2,1)S(1)}, u32[]{:S(2)}) copy-start(bf16[128,1152]{1,0:T(8,128)(2,1)S(1)} %collective-permute-done.up_ref) | copy-start | bytes 884740
  39.2 28.9 %copy-start.28 = (bf16[128,1152]{1,0:T(8,128)(2,1)}, bf16[128,1152]{1,0:T(8,128)(2,1)S(1)}, u32[]{:S(2)}) copy-start(bf16[128,1152]{1,0:T(8,128)(2,1)S(1)} %collective-permute-done.1.right_ref) | copy-start | bytes 884740
  67.6 14.3 %collective-permute-start.6 = (bf16[128,384]{1,0:T(8,128)(2,1)S(1)}, bf16[128,384]{1,0:T(8,128)(2,1)S(1)}, u32[]{:S(2)}, u32[]{:S(2)}) collective-permute-start(bf16[128,384]{1,0:T(8,128)(2,1)S(1)} %get-tuple-element.34), channel_id=1, source_target_pairs={{0,33},{1,34},{2,35},{3,36},{4,37},{5,38},{6,39},{7,40},{8,41},{9,... | collective-permute-start | bytes 294920 | tf_op jit(solution)/shard_map/ppermute | solution.py:258
  67.7 14.2 %collective-permute-start.7 = (bf16[128,384]{1,0:T(8,128)(2,1)S(1)}, bf16[128,384]{1,0:T(8,128)(2,1)S(1)}, u32[]{:S(2)}, u32[]{:S(2)}) collective-permute-start(bf16[128,384]{1,0:T(8,128)(2,1)S(1)} %get-tuple-element.35), channel_id=1, source_target_pairs={{0,32},{1,33},{2,34},{3,35},{4,36},{5,37},{6,38},{7,39},{8,40},{9,... | collective-permute-start | bytes 294920 | tf_op jit(solution)/shard_map/ppermute | solution.py:258
  68.0 13.9 %collective-permute-start.8 = (bf16[128,384]{1,0:T(8,128)(2,1)S(1)}, bf16[128,384]{1,0:T(8,128)(2,1)S(1)}, u32[]{:S(2)}, u32[]{:S(2)}) collective-permute-start(bf16[128,384]{1,0:T(8,128)(2,1)S(1)} %get-tuple-element.36), channel_id=1, source_target_pairs={{0,1},{1,2},{2,3},{3,4},{4,5},{5,6},{6,7},{7,8},{8,9},{9,10},{10,1... | collective-permute-start | bytes 294920 | tf_op jit(solution)/shard_map/ppermute | solution.py:258
  89.8 45.6 %collective-permute-start.12 = (bf16[384,1536]{1,0:T(8,128)(2,1)}, bf16[384,1536]{1,0:T(8,128)(2,1)}, u32[]{:S(2)}, u32[]{:S(2)}) collective-permute-start(bf16[384,1536]{1,0:T(8,128)(2,1)} %get-tuple-element.51), channel_id=1, source_target_pairs={{0,1},{1,0},{2,3},{3,2},{4,5},{5,4},{6,7},{7,6},{8,9},{9,8},{10,11... | collective-permute-start | bytes 3538952 | tf_op jit(solution)/shard_map/ppermute | solution.py:326
  95.0 15.1 %all-to-all-start.1 = ((bf16[32,2,384]{2,1,0:T(2,128)(2,1)}), bf16[32,2,384]{2,1,0:T(2,128)(2,1)S(1)}, u32[]{:S(2)}, u32[]{:S(2)}) async-start(bf16[32,2,384]{2,1,0:T(2,128)(2,1)} %reshape.254), calls=%async_computation.1 | async-start | bytes 98304 | tf_op jit(solution)/shard_map/all_to_all | solution.py:319
  112.0 11.7 %all-to-all-start.3 = ((bf16[32,2,384]{2,1,0:T(2,128)(2,1)}), bf16[32,2,384]{2,1,0:T(2,128)(2,1)S(1)}, u32[]{:S(2)}, u32[]{:S(2)}) async-start(bf16[32,2,384]{2,1,0:T(2,128)(2,1)} %reshape.256), calls=%async_computation.3 | async-start | bytes 98304 | tf_op jit(solution)/shard_map/all_to_all | solution.py:336
  124.6 20.1 %all-to-all-start.4 = ((f32[8,3,768]{2,1,0:T(4,128)}), f32[8,3,768]{2,1,0:T(4,128)S(1)}, u32[]{:S(2)}, u32[]{:S(2)}) async-start(f32[8,3,768]{2,1,0:T(4,128)} %copy.57), calls=%async_computation.4 | async-start | bytes 196608 | tf_op jit(solution)/shard_map/all_to_all | solution.py:340
  144.6 67.5 %all-to-all-start.2 = ((bf16[128,3,1536]{2,1,0:T(4,128)(2,1)}), bf16[128,3,1536]{2,1,0:T(4,128)(2,1)}, u32[]{:S(2)}, u32[]{:S(2)}) async-start(bf16[128,3,1536]{2,1,0:T(4,128)(2,1)} %reshape.248), calls=%async_computation.2 | async-start | bytes 3145728 | tf_op jit(solution)/shard_map/all_to_all | solution.py:329
  151.9 44.4 %collective-permute-start.10 = (bf16[128,768]{1,0:T(8,128)(2,1)S(1)}, bf16[128,768]{1,0:T(8,128)(2,1)S(1)}, u32[]{:S(2)}, u32[]{:S(2)}) collective-permute-start(bf16[128,768]{1,0:T(8,128)(2,1)S(1)} %copy-done.37), channel_id=1, source_target_pairs={{0,32},{1,33},{2,34},{3,35},{4,36},{5,37},{6,38},{7,39},{8,40},{9,... | collective-permute-start | bytes 589832 | tf_op jit(solution)/shard_map/ppermute | solution.py:258
  152.5 43.8 %collective-permute-start.11 = (bf16[128,768]{1,0:T(8,128)(2,1)S(1)}, bf16[128,768]{1,0:T(8,128)(2,1)S(1)}, u32[]{:S(2)}, u32[]{:S(2)}) collective-permute-start(bf16[128,768]{1,0:T(8,128)(2,1)S(1)} %copy-done.35), channel_id=1, source_target_pairs={{0,1},{1,2},{2,3},{3,4},{4,5},{5,6},{6,7},{7,8},{8,9},{9,10},{10,1... | collective-permute-start | bytes 589832 | tf_op jit(solution)/shard_map/ppermute | solution.py:258
  155.9 53.5 %copy-start.10 = (bf16[128,768]{1,0:T(8,128)(2,1)S(1)}, bf16[128,768]{1,0:T(8,128)(2,1)}, u32[]{:S(2)}) copy-start(bf16[128,768]{1,0:T(8,128)(2,1)} %copy-done.9) | copy-start | bytes 589828
  156.0 53.5 %copy-start.21 = (f32[8,768]{1,0:T(8,128)S(1)}, f32[8,768]{1,0:T(8,128)}, u32[]{:S(2)}) copy-start(f32[8,768]{1,0:T(8,128)} %copy-done.20) | copy-start | bytes 73732
  156.0 53.5 %collective-permute-start.9 = (bf16[128,768]{1,0:T(8,128)(2,1)S(1)}, bf16[128,768]{1,0:T(8,128)(2,1)S(1)}, u32[]{:S(2)}, u32[]{:S(2)}) collective-permute-start(bf16[128,768]{1,0:T(8,128)(2,1)S(1)} %copy-done.33), channel_id=1, source_target_pairs={{0,33},{1,34},{2,35},{3,36},{4,37},{5,38},{6,39},{7,40},{8,41},{9,... | collective-permute-start | bytes 589832 | tf_op jit(solution)/shard_map/ppermute | solution.py:258
  (34 other events, 305.9 us)
where the time goes:
time: 216 us; the launch traced here: 215 us
  waiting for transfers between devices  88.3 us (41%)
  starting transfers between devices  63.9 us (30%)
  Pallas kernels  31.2 us (14%)
  local copies, waits for them, and re-layouts  22.8 us (11%)
  other arithmetic  7.84 us (4%)
    ppermute x12, waiting for transfers between devices, moved(): return lax.ppermute(block, ALL, route)  68.5 us
    pallas_call x8, Pallas kernels, call(): pl.pallas_call(kernel, out_shape=[jax.ShapeDtypeStruct(s, d) for s, d in...  31.2 us
    ppermute x12, starting transfers between devices, moved(): return lax.ppermute(block, ALL, route)  27.7 us
    unnamed x94, local copies, waits for them, and re-layouts  16.8 us
    all_to_all x1, starting transfers between devices, body(): coarse_grad = jnp.sum(lax.all_to_all(share, GX, 0, 0), axis=0)  10.9 us
    all_to_all x1, waiting for transfers between devices, body(): grads_far = lax.all_to_all(rows, GZ, 0, 0, tiled=True)  7.56 us
    all_to_all x1, starting transfers between devices, body(): parts = lax.all_to_all(coarse_part, GZ, 0, 0, tiled=True)  7.44 us
    all_to_all x1, starting transfers between devices, body(): got = lax.all_to_all(chip_sum, GX + ('zl', 'y'), 0, 0)  7.26 us
  transfers between devices with their start and end apart: 18, of which 7 were waited for; matrix products, arithmetic and copies ran while one was open for 6% of the time, Pallas kernels for 9%

commit v1 on v0

--- a/solution.py
+++ b/solution.py
@@ -27,13 +27,16 @@
     return lax.dot_general(left, right, (((1,), (1,)), ((), ())), preferred_element_type=f32)
 
 
-def call(kernel, outs, *args, scratch=(), flops=0, size=0):
+def call(kernel, outs, *args, scratch=(), far=(), scalars=(), grant=16):
     return pl.pallas_call(
         kernel,
         out_shape=[jax.ShapeDtypeStruct(s, d) for s, d in outs],
+        in_specs=[
+            pl.BlockSpec(memory_space=pltpu.HBM if i in far else pltpu.SMEM if i in scalars else pltpu.VMEM) for i in range(len(args))
+        ],
         scratch_shapes=list(scratch),
-        compiler_params=pltpu.CompilerParams(vmem_limit_bytes=40 * 2**20),
-        cost_estimate=pl.CostEstimate(flops=flops, bytes_accessed=size, transcendentals=0),
+        compiler_params=pltpu.CompilerParams(vmem_limit_bytes=grant * 2**20),
+        cost_estimate=pl.CostEstimate(flops=1, bytes_accessed=1, transcendentals=0),
     )(*args)
 
 
@@ -72,19 +75,45 @@
     return rows.reshape(x // 2 * y, z, d)
 
 
-def prepare(tok_ref, cot_ref, wo_ref, wc_ref, both_ref, right_ref, up_ref, own_ref, coarse_ref):
-    d = tok_ref.shape[3]
+def columns_of(mask):
+    m, z = mask.shape
+    rows = jnp.broadcast_to(mask[:, None, :], (m, z, z))
+    shape = (m, z, z)
+    same = lax.broadcasted_iota(jnp.int32, shape, 1) == lax.broadcasted_iota(jnp.int32, shape, 2)
+    column = jnp.sum(jnp.where(same, rows, 0.0), axis=2, keepdims=True)
+    return jnp.broadcast_to(column, (m, z, 128))
+
+
+def prepare(*refs):
+    sources, mask_ref, refs = refs[:4], refs[4], refs[5:]
+    outs, held, sems = refs[:5], refs[5:9], refs[9]
+    both_ref, right_ref, up_ref, own_ref, coarse_ref = outs
+    tok_ref, cot_ref, wo_ref, wc_ref = held
+    copies = [pltpu.make_async_copy(a, b, sems.at[i]) for i, (a, b) in enumerate(zip(sources, held))]
+    for copy in copies:
+        copy.start()
+    copies[0].wait()
+    inner, d = wo_ref.shape
     total = jnp.zeros((1, d), f32)
     cells = 1
     for n in tok_ref.shape[:3]:
         cells *= n
-    for half, refs in ((0, (both_ref, right_ref)), (1, (up_ref, own_ref))):
+    halves = ((0, (both_ref, right_ref)), (1, (up_ref, own_ref)))
+    for half, refs in halves:
         normed, _ = normalize(x_half(tok_ref, half))
         total += jnp.sum(jnp.sum(normed, axis=0), axis=0, keepdims=True)
         for ref, part in zip(refs, split_z(normed)):
             ref[:, :d] = part.astype(bf16)
+        x, y, z = mask_ref.shape
+        cells_in = mask_ref[half * (x // 2) : (half + 1) * (x // 2)].astype(f32)
+        for ref, part in zip(refs, split_z(columns_of(cells_in.reshape(x // 2 * y, z)))):
+            ref[:, d + inner :] = part.astype(bf16)
+    copies[1].wait()
+    copies[2].wait()
+    for half, refs in halves:
         for ref, part in zip(refs, split_z(x_half(cot_ref, half))):
-            ref[:, d:] = dot_nt(part.astype(bf16), wo_ref[...]).astype(bf16)
+            ref[:, d : d + inner] = dot_nt(part.astype(bf16), wo_ref[...]).astype(bf16)
+    copies[3].wait()
     pooled = jnp.broadcast_to((total / cells).astype(bf16), (coarse_ref.shape[0], d))
     coarse_ref[:, :d] = pooled
     coarse_ref[:, d:] = dot(pooled, wc_ref[...]).astype(bf16)
@@ -111,8 +140,16 @@
     return jnp.where((lanes < HEAD) == (half == 0), pair, jnp.zeros_like(pair))
 
 
-def attend(own_ref, up_ref, right_ref, both_ref, wi_ref, kv_ref, mask_ref,
-           a0_ref, a1_ref, a2_ref, a3_ref, q_ref, k_ref, v_ref, m_ref, l_ref, out_ref):
+def hide(mask_ref, refs, start):
+    n = refs[0].shape[0]
+    for i, ref in enumerate(refs):
+        seen = ref[:, start:].astype(f32)
+        mask_ref[i * n : (i + 1) * n] = jnp.where(seen > 0.5, 0.0, HIDDEN)
+    mask_ref[4 * n :] = jnp.zeros((mask_ref.shape[0] - 4 * n, mask_ref.shape[1]), f32)
+
+
+def attend(own_ref, up_ref, right_ref, both_ref, wi_ref, kv_ref,
+           a0_ref, a1_ref, a2_ref, a3_ref, q_ref, k_ref, v_ref, m_ref, l_ref, out_ref, mask_ref):
     d, width = wi_ref.shape
     inner = width // 3
     n = own_ref.shape[0]
@@ -123,6 +160,7 @@
         q_ref[rows] = packed[:, :inner].astype(bf16) * bf16(0.125)
         k_ref[rows] = packed[:, inner : 2 * inner].astype(bf16)
         v_ref[rows] = packed[:, 2 * inner :].astype(bf16)
+    hide(mask_ref, (own_ref, up_ref, right_ref, both_ref), d + inner)
     k_ref[tokens:] = kv_ref[:, d : d + inner]
     v_ref[tokens:] = kv_ref[:, d + inner :]
     eye = jnp.where(
@@ -140,7 +178,7 @@
         query = q_ref[rows, lanes]
         found = []
         for half in range(2):
-            s = dot_nt(keys, head_of(query, half)) + mask_ref[...]
+            s = dot_nt(keys, head_of(query, half)) + jnp.concatenate([mask_ref[...]] * 2, axis=1)
             top = jnp.max(s, axis=0, keepdims=True)
             e = jnp.exp(s - top)
             inv = 1.0 / jnp.sum(e, axis=0, keepdims=True)
@@ -156,14 +194,15 @@
         ref[...] = out_ref[i * n : (i + 1) * n]
 
 
-def attend_back(own_ref, up_ref, right_ref, both_ref, wi_ref, mask_ref, q_ref, k_ref, v_ref, m_ref, l_ref,
-                d0_ref, d1_ref, d2_ref, d3_ref, grad_ref, coarse_ref, g_ref, dk_ref, dv_ref):
+def attend_back(own_ref, up_ref, right_ref, both_ref, wi_ref, q_ref, k_ref, v_ref, m_ref, l_ref,
+                d0_ref, d1_ref, d2_ref, d3_ref, grad_ref, coarse_ref, g_ref, dk_ref, dv_ref, mask_ref):
     d, width = wi_ref.shape
     inner = width // 3
     n = own_ref.shape[0]
     tokens = 4 * n
     for i, ref in enumerate((own_ref, up_ref, right_ref, both_ref)):
-        g_ref[i * n : (i + 1) * n] = ref[:, d:]
+        g_ref[i * n : (i + 1) * n] = ref[:, d : d + inner]
+    hide(mask_ref, (own_ref, up_ref, right_ref, both_ref), d + inner)
     eye = jnp.where(
         lax.broadcasted_iota(jnp.int32, (PAIR, PAIR), 0)
         == lax.broadcasted_iota(jnp.int32, (PAIR, PAIR), 1), 1.0, 0.0).astype(bf16)
@@ -183,7 +222,7 @@
         for half in range(2):
             query = head_of(q_ref[rows, lanes], half)
             g = head_of(g_ref[rows, lanes], half)
-            s = dot_nt(keys, query) + mask_ref[...]
+            s = dot_nt(keys, query) + jnp.concatenate([mask_ref[...]] * 2, axis=1)
             prob = jnp.exp(s - m_ref[pl.ds(2 * i + half, 1)]) * l_ref[pl.ds(2 * i + half, 1)]
             dv += dot(prob.astype(bf16), g)
             spread = prob * dot_nt(vals, g)
@@ -199,8 +238,13 @@
     lax.fori_loop(0, inner // PAIR * chunks, step, 0)
     grad_ref[:, inner : 2 * inner] = dk_ref[:tokens].astype(bf16)
     grad_ref[:, 2 * inner :] = dv_ref[:tokens].astype(bf16)
-    coarse_ref[:, :inner] = dk_ref[tokens:].astype(bf16)
-    coarse_ref[:, inner:] = dv_ref[tokens:].astype(bf16)
+    peers = coarse_ref.shape[0]
+    part = jnp.concatenate([dk_ref[tokens:].astype(bf16), dv_ref[tokens:].astype(bf16)], axis=1)
+    chip = lax.broadcasted_iota(jnp.int32, (peers, peers), 0) // 2 * 2
+    token = lax.broadcasted_iota(jnp.int32, (peers, peers), 1)
+    for i in range(2):
+        pick = jnp.where(token == chip + i, 1.0, 0.0).astype(bf16)
+        coarse_ref[:, i * 2 * inner : (i + 1) * 2 * inner] = dot(pick, part).astype(bf16)
     for i, ref in enumerate((d0_ref, d1_ref, d2_ref, d3_ref)):
         ref[...] = dot_nt(grad_ref[i * n : (i + 1) * n], wi_ref[...]).astype(bf16)
 
@@ -229,10 +273,48 @@
             (x // 2,) + out_ref.shape[1:])
 
 
-def coarse_total(parts_ref, wc_ref, rows_ref, pooled_ref):
+def coarse_total(parts_ref, wc_ref, core_ref, pair_ref, pooled_ref):
+    d = wc_ref.shape[0]
     total = jnp.sum(parts_ref[...].astype(f32), axis=0, keepdims=True).astype(bf16)
-    rows_ref[...] = jnp.broadcast_to(total, rows_ref.shape)
-    pooled_ref[...] = dot_nt(jnp.broadcast_to(total, (8, total.shape[1])), wc_ref[...])
+    pair_ref[...] = total
+    row = jnp.where(core_ref[0, 0] == 0, total[:, :d], total[:, d:])
+    pooled_ref[...] = dot_nt(jnp.broadcast_to(row, (8, d)), wc_ref[...])
+
+
+def assemble(keep_ref, other_ref, pair_ref, picked_ref, out_ref):
+    plane, rows, width = out_ref.shape
+    rows -= 8
+    line = lax.broadcasted_iota(jnp.int32, (8, width), 0)
+    lanes = picked_ref.shape[1]
+    for i in range(plane):
+        part = slice(i * rows, (i + 1) * rows)
+        out_ref[i, :rows] = (keep_ref[part].astype(f32) + other_ref[part].astype(f32)).astype(bf16)
+        extra = jnp.where(line == 0, pair_ref[...].astype(f32), 0.0)
+        out_ref[i, rows:] = extra.astype(bf16)
+        seen = jnp.where(line[:, :lanes] == 1, picked_ref[i : i + 1].astype(f32), extra[:, :lanes])
+        out_ref[i, rows:, :lanes] = seen.astype(bf16)
+
+
+def plane_sums(in_ref, out_ref):
+    plane, rows, width = in_ref.shape
+    rows -= 8
+    deep = out_ref.shape[0]
+    half = width // 2
+    total = jnp.sum(in_ref[:, :rows].astype(f32), axis=0)
+    extra = in_ref[:, rows:].astype(f32)
+    line = lax.broadcasted_iota(jnp.int32, extra.shape, 1)
+    grads = jnp.sum(jnp.where(line == 0, extra, 0.0), axis=1).astype(bf16)
+    picked = jnp.sum(jnp.where(line == 1, extra, 0.0), axis=1)[:, :256].astype(bf16)
+    coarse = jnp.zeros((128, half), f32)
+    for i in range(2):
+        coarse += lax.dot_general(
+            picked[:, i * 128 : (i + 1) * 128], grads[:, i * half : (i + 1) * half],
+            (((0,), (0,)), ((), ())), preferred_element_type=f32)
+    step = out_ref.shape[1] // (rows // deep)
+    for j in range(rows // deep):
+        part = slice(j * deep, (j + 1) * deep)
+        out_ref[:, j * step : j * step + width] = total[part].astype(bf16)
+        out_ref[:, j * step + width : (j + 1) * step] = coarse[part].astype(bf16)
 
 
 def token_result(tok_ref, cot_ref, b0_ref, b1_ref, b2_ref, b3_ref, pooled_ref, out_ref):
@@ -258,12 +340,6 @@
     return lax.ppermute(block, ALL, route)
 
 
-def mask_quads(a):
-    x, y, z = a.shape
-    a = jnp.moveaxis(a.reshape(2, x // 2, y, 2, z // 2), 3, 1)
-    return a.reshape(2, 2, 1, x * y * z // 4)
-
-
 def returned(own, up, right, both):
     return moved(both, 1, 1), moved(right, 1, 0), moved(up, 0, 1), own
 
@@ -279,25 +355,29 @@
     per = d // devices
     core = lax.axis_index("core")
 
-    quads = mask_quads(body_mask)
-    masks = [quads[1, 1], moved(quads[1, 0], 0, -1), moved(quads[0, 1], -1, 0), moved(quads[0, 0], -1, -1)]
-    live = jnp.concatenate(masks + [jnp.ones((1, coarse), jnp.int32)], axis=1)
-    mask = jnp.where(live > 0, 0.0, HIDDEN).reshape(size + coarse, 1)
-
-    wide = (n, d + inner)
+    wide = (n, d + inner + 128)
     both, right, up, own, far = call(
-        prepare, [(wide, bf16)] * 4 + [((coarse, 2 * d), bf16)], tokens, cotangent, w_out, w_coarse,
-        flops=4 * size * d * inner, size=10 * size * d)
+        prepare, [(wide, bf16)] * 4 + [((coarse, 2 * d), bf16)], tokens, cotangent, w_out, w_coarse, body_mask,
+        far=range(4),
+        grant=60,
+        scratch=[pltpu.VMEM(a.shape, bf16) for a in (tokens, cotangent, w_out, w_coarse)] + [pltpu.SemaphoreType.DMA((4,))])
     up, right, both = moved(up, 0, -1), moved(right, -1, 0), moved(both, -1, -1)
     far = lax.all_to_all(far, GZ, 0, 0, tiled=True)
-    pooled = far[:, :d]
+
+    zh, nx, zl, ny, cores = (lax.axis_size(a) for a in ALL)
+    plane, deep = nx * ny, zh * zl
+    mine = lax.dynamic_slice_in_dim(far, lax.axis_index(GZ) // cores * cores, cores, axis=0)[:, :d]
+    mine = mine.reshape(cores, zh, nx, zl, ny, cores, per)
+    mine = lax.dynamic_index_in_dim(mine, core, axis=5, keepdims=False)
+    mine = jnp.transpose(mine, (2, 4, 0, 5, 1, 3)).reshape(plane, cores, per * deep)
+    picked = jnp.pad(mine, ((0, 0), (0, 0), (0, 128 - per * deep))).reshape(plane, cores * 128)
 
     row = jnp.arange(d, dtype=jnp.int32)
-    half = row // (d // 2)
-    rest = row % (d // 2)
-    src = (rest // per * 2 + (half + core) % 2) * per + rest % per
-    src = src.reshape(d, 1)
-    (cot_turned,) = call(turn_cot, [((d, size), bf16)], cotangent, src, flops=2 * size * d * d, size=4 * size * d)
+    half, rest = row // (d // 2), row % (d // 2)
+    chip, j, depth = rest // (per * deep), rest % (per * deep) // deep, rest % deep
+    device = ((depth // zl * nx + chip // ny) * zl + depth % zl) * ny + chip % ny
+    src = ((device * cores + (half + core) % cores) * per + j).reshape(d, 1)
+    (cot_turned,) = call(turn_cot, [((d, size), bf16)], cotangent, src)
 
     slim = (n, inner)
     a0, a1, a2, a3, q, k, v, top, inv = call(
@@ -305,46 +385,42 @@
         [(slim, bf16)] * 4
         + [((size, inner), bf16), ((size + coarse, inner), bf16), ((size + coarse, inner), bf16)]
         + [((16, CHUNK), f32)] * 2,
-        own, up, right, both, w_in, far, mask,
-        scratch=[pltpu.VMEM((size, inner), bf16)], flops=6 * size * d * inner + 8 * size * size * inner, size=8 * size * d)
+        own, up, right, both, w_in, far,
+        scratch=[pltpu.VMEM((size, inner), bf16), pltpu.VMEM((size + coarse, 128), f32)])
     b0, b1, b2, b3 = returned(a0, a1, a2, a3)
 
     d0, d1, d2, d3, grad, coarse_part = call(
         attend_back,
-        [((n, d), bf16)] * 4 + [((size, 3 * inner), bf16), ((coarse, 2 * inner), bf16)],
-        own, up, right, both, w_in, mask, q, k, v, top, inv,
-        scratch=[pltpu.VMEM((size, inner), bf16)] + [pltpu.VMEM((size + coarse, inner), f32)] * 2,
-        flops=6 * size * d * inner + 16 * size * size * inner, size=10 * size * d)
+        [((n, d), bf16)] * 4 + [((size, 3 * inner), bf16), ((coarse, 4 * inner), bf16)],
+        own, up, right, both, w_in, q, k, v, top, inv,
+        scratch=[pltpu.VMEM((size, inner), bf16)] + [pltpu.VMEM((size + coarse, inner), f32)] * 2
+        + [pltpu.VMEM((size + coarse, 128), f32)])
     e0, e1, e2, e3 = returned(d0, d1, d2, d3)
     parts = lax.all_to_all(coarse_part, GZ, 0, 0, tiled=True)
 
+    grad, e2 = lax.optimization_barrier((grad, e2))
     keep, send = call(
         weight_grads, [((d // 2, 4 * inner), bf16)] * 2,
         own, up, right, both, src, grad, cot_turned, b0, b1, b2, b3,
-        scratch=[pltpu.VMEM((d, size), bf16), pltpu.VMEM((size, inner), bf16)],
-        flops=12 * size * d * inner, size=10 * size * d)
+        scratch=[pltpu.VMEM((d, size), bf16), pltpu.VMEM((size, inner), bf16)])
     other = lax.ppermute(send, "core", [(0, 1), (1, 0)])
-    chips = devices // 2
-    chip_sum = (keep.astype(f32) + other.astype(f32)).astype(bf16).reshape(chips, per, 4 * inner)
-    got = lax.all_to_all(chip_sum, GX + ("zl", "y"), 0, 0)
-
-    (block_out,) = call(
-        block_result, [(tokens.shape, bf16)], tokens, b0, b1, b2, b3, w_out, flops=2 * size * d * inner, size=6 * size * d)
-
-    rows, grad_pooled = call(
-        coarse_total, [((coarse, 2 * inner), bf16), ((8, d), f32)], parts, w_coarse, size=2 * d * d)
-    grads_far = lax.all_to_all(rows, GZ, 0, 0, tiled=True)
-    picked = lax.dynamic_slice_in_dim(
-        pooled.reshape(coarse, columns, d // columns), lax.axis_index(GZ) * per, per, axis=2)
-    share = jnp.einsum("mcj,me->cje", picked, grads_far, preferred_element_type=f32)
-    coarse_grad = jnp.sum(lax.all_to_all(share, GX, 0, 0), axis=0)
-
-    (token_grad,) = call(
-        token_result, [(tokens.shape, bf16)], tokens, cotangent, e0, e1, e2, e3, grad_pooled, size=8 * size * d)
-
-    summed = jnp.sum(got.astype(f32), axis=0)
+    pair, grad_pooled = call(
+        coarse_total, [((1, 4 * inner), bf16), ((8, d), f32)], parts, w_coarse, core.reshape(1, 1), scalars=(2,))
+
+    (packet,) = call(
+        assemble, [((plane, per * deep + 8, 4 * inner), bf16)], keep, other, pair, picked)
+    packet, e0, e1, e2 = lax.optimization_barrier((packet, e0, e1, e2))
+    packet = lax.all_to_all(packet, ("x", "y"), 0, 0, tiled=True)
+    (slab,) = call(plane_sums, [((deep, per * 6 * inner), bf16)], packet)
+    slab = lax.all_to_all(slab, ("zh", "zl"), 0, 0, tiled=True)
+
+    (block_out,) = call(block_result, [(tokens.shape, bf16)], tokens, b0, b1, b2, b3, w_out)
+    (token_grad,) = call(token_result, [(tokens.shape, bf16)], tokens, cotangent, e0, e1, e2, e3, grad_pooled)
+
+    summed = jnp.sum(slab.astype(f32), axis=0).reshape(per, 6 * inner)
     input_grad = summed[:, : 3 * inner]
-    output_grad = summed[:, 3 * inner :].T
+    output_grad = summed[:, 3 * inner : 4 * inner].T
+    coarse_grad = summed[:, 4 * inner :]
     return (block_out, token_grad, input_grad, output_grad, coarse_grad)
 
 

time: 216 us -> 171 us (0.79)
  waiting for transfers between devices: 88.3 us -> 57.2 us
  starting transfers between devices: 63.9 us -> 33.4 us
  blocking collectives: 0 us -> 25.6 us
  local copies, waits for them, and re-layouts: 22.8 us -> 11.5 us
  Pallas kernels: 31.2 us -> 36.2 us
  other arithmetic: 7.84 us -> 4.89 us
    ppermute x12 -> x9, waiting for transfers between devices: 68.5 us -> 23.4 us  [moved(): return lax.ppermute(block, ALL, route)]
    all_to_all x0 -> x1, blocking collectives: none -> 25.6 us  [body(): packet = lax.all_to_all(packet, ('x', 'y'), 0, 0, tiled=True)]
    all_to_all x1, waiting for transfers between devices: 0.01 us -> 23.5 us  [body(): far = lax.all_to_all(far, GZ, 0, 0, tiled=True)]
    all_to_all x3 -> x1, starting transfers between devices: 22 us -> 3.36 us  [body(): slab = lax.all_to_all(slab, ('zh', 'zl'), 0, 0, tiled=True)]
    ppermute x12 -> x9, starting transfers between devices: 27.7 us -> 16.7 us  [moved(): return lax.ppermute(block, ALL, route)]
    unnamed x94 -> x64, local copies, waits for them, and re-layouts: 16.8 us -> 7.55 us
    all_to_all x3 -> x1, waiting for transfers between devices: 13.1 us -> 3.99 us  [body(): slab = lax.all_to_all(slab, ('zh', 'zl'), 0, 0, tiled=True)]
    pallas_call x8 -> x10, Pallas kernels: 31.2 us -> 36.2 us  [call(): pl.pallas_call(kernel, out_shape=[jax.ShapeDtypeStruct(s, d) for s, d in...]
  transfers between devices with their start and end apart: 18 -> 13, of which waited for: 7 -> 7; matrix products, arithmetic and copies ran while one was open for 6% -> 5% of each run, Pallas kernels for 9% -> 4%
where the time goes in v1:
time: 171 us; the launch traced here: 170 us
  waiting for transfers between devices  57.2 us (33%)
  Pallas kernels  36.2 us (21%)
  starting transfers between devices  33.4 us (20%)
  blocking collectives  25.6 us (15%)
  local copies, waits for them, and re-layouts  11.5 us (7%)
  other arithmetic  4.89 us (3%)
    pallas_call x10, Pallas kernels, call(): pl.pallas_call(kernel, out_shape=[jax.ShapeDtypeStruct(s, d) for s, d in...  36.2 us
    all_to_all x1, blocking collectives, body(): packet = lax.all_to_all(packet, ('x', 'y'), 0, 0, tiled=True)  25.6 us
    all_to_all x1, waiting for transfers between devices, body(): far = lax.all_to_all(far, GZ, 0, 0, tiled=True)  23.5 us
    ppermute x9, waiting for transfers between devices, moved(): return lax.ppermute(block, ALL, route)  23.4 us
    ppermute x9, starting transfers between devices, moved(): return lax.ppermute(block, ALL, route)  16.7 us
    all_to_all x1, starting transfers between devices, body(): parts = lax.all_to_all(coarse_part, GZ, 0, 0, tiled=True)  8.39 us
    unnamed x64, local copies, waits for them, and re-layouts  7.55 us
    all_to_all x1, waiting for transfers between devices, body(): parts = lax.all_to_all(coarse_part, GZ, 0, 0, tiled=True)  6.3 us
  transfers between devices with their start and end apart: 13, of which 7 were waited for; matrix products, arithmetic and copies ran while one was open for 5% of the time, Pallas kernels for 4%

profile of v1, /device:TPU:1, one launch (start us, length us, event | category | flops | bytes accessed | tf_op | source)
XLA Modules:
  0.0 169.9 jit_solution(14605019973502560692)
XLA Ops:
  0.6 4.7 %shard_map.101 = (bf16[128,1280]{1,0:T(8,128)(2,1)}, bf16[128,1280]{1,0:T(8,128)(2,1)}, bf16[128,1280]{1,0:T(8,128)(2,1)}, bf16[128,1280]{1,0:T(8,128)(2,1)}, bf16[32,1536]{1,0:T(8,128)(2,1)}) custom-call(bf16[8,8,8,768]{3,2,1,0:T(8,128)(2,1)} %tok_ref.3, bf16[8,8,8,768]{3,2,1,0:T(8,128)(2,1)} %cot_ref.3, bf16[384,768]{1,0:T(8,128)(2,1)} %wo_ref.1, ...), custom_call_target="tpu_custom_call" | custom-call | flops 1 | bytes 1 | tf_op jit(solution)/shard_map/pallas_call | solution.py:31
  5.4 3.3 %collective-permute-start = (bf16[128,1280]{1,0:T(8,128)(2,1)}, bf16[128,1280]{1,0:T(8,128)(2,1)S(1)}, u32[]{:S(2)}, u32[]{:S(2)}) collective-permute-start(bf16[128,1280]{1,0:T(8,128)(2,1)} %get-tuple-element.36), channel_id=1, source_target_pairs={{0,31},{1,0},{2,1},{3,2},{4,3},{5,4},{6,5},{7,6},{8,7},{9,8},{10,9... | collective-permute-start | bytes 983048 | tf_op jit(solution)/shard_map/ppermute | solution.py:340
  8.7 7.4 %collective-permute-start.1 = (bf16[128,1280]{1,0:T(8,128)(2,1)}, bf16[128,1280]{1,0:T(8,128)(2,1)S(1)}, u32[]{:S(2)}, u32[]{:S(2)}) collective-permute-start(bf16[128,1280]{1,0:T(8,128)(2,1)} %get-tuple-element.37), channel_id=1, source_target_pairs={{0,224},{1,225},{2,226},{3,227},{4,228},{5,229},{6,230},{7,231},{8... | collective-permute-start | bytes 983048 | tf_op jit(solution)/shard_map/ppermute | solution.py:340
  16.0 4.5 %collective-permute-start.2 = (bf16[128,1280]{1,0:T(8,128)(2,1)}, bf16[128,1280]{1,0:T(8,128)(2,1)S(1)}, u32[]{:S(2)}, u32[]{:S(2)}) collective-permute-start(bf16[128,1280]{1,0:T(8,128)(2,1)} %get-tuple-element.38), channel_id=1, source_target_pairs={{0,255},{1,224},{2,225},{3,226},{4,227},{5,228},{6,229},{7,230},{8... | collective-permute-start | bytes 983048 | tf_op jit(solution)/shard_map/ppermute | solution.py:340
  21.1 1.6 reduce.1
  23.3 3.6 %all-to-all-start = ((bf16[32,2,768]{2,1,0:T(2,128)(2,1)}), bf16[32,2,768]{2,1,0:T(2,128)(2,1)S(1)}, u32[]{:S(2)}, u32[]{:S(2)}) async-start(bf16[32,2,768]{2,1,0:T(2,128)(2,1)} %reshape.394), calls=%async_computation | async-start | bytes 196608 | tf_op jit(solution)/shard_map/all_to_all | solution.py:365
  27.0 23.5 %all-to-all-done = bf16[32,2,768]{2,1,0:T(2,128)(2,1)S(1)} async-done(((bf16[32,2,768]{2,1,0:T(2,128)(2,1)}), bf16[32,2,768]{2,1,0:T(2,128)(2,1)S(1)}, u32[]{:S(2)}, u32[]{:S(2)}) %all-to-all-start) | async-done | bytes 98336 | tf_op jit(solution)/shard_map/all_to_all | solution.py:365
  50.6 8.9 %shard_map.102 = (bf16[128,384]{1,0:T(8,128)(2,1)S(1)}, bf16[128,384]{1,0:T(8,128)(2,1)S(1)}, bf16[128,384]{1,0:T(8,128)(2,1)S(1)}, bf16[128,384]{1,0:T(8,128)(2...) custom-call(bf16[128,1280]{1,0:T(8,128)(2,1)S(1)} %copy-done.4, ...), custom_call_target="tpu_custom_call" | custom-call | flops 1 | bytes 1 | tf_op jit(solution)/shard_map/pallas_call | solution.py:31
  60.6 11.1 %shard_map.104 = (bf16[128,768]{1,0:T(8,128)(2,1)S(1)}, bf16[128,768]{1,0:T(8,128)(2,1)S(1)}, bf16[128,768]{1,0:T(8,128)(2,1)S(1)}, bf16[128,768]{1,0:T(8,128)(2...) custom-call(bf16[128,1280]{1,0:T(8,128)(2,1)S(1)} %copy-done.4, ...), custom_call_target="tpu_custom_call" | custom-call | flops 1 | bytes 1 | tf_op jit(solution)/shard_map/pallas_call | solution.py:31
  73.7 1.8 %fusion.11.src_ref = s32[768,1]{1,0:T(8,128)S(1)} fusion(s32[]{:T(128)} %axis_index.36), kind=kLoop, calls=%fused_computation.37 | loop fusion | flops 84480 | bytes 3076 | tf_op jit(solution)/shard_map/add | solution.py:379
  75.5 1.4 shard_map.105.cot_ref
  77.6 6.6 %collective-permute-done.3.b0_ref = bf16[128,384]{1,0:T(8,128)(2,1)S(1)} collective-permute-done((bf16[128,384]{1,0:T(8,128)(2,1)S(1)}, bf16[128,384]{1,0:T(8,128)(2,1)S(1)}, u32[]{:S(2)}, u32[]{:S(2)}) %collective-permute-start.3) | collective-permute-done | bytes 98336 | tf_op jit(solution)/shard_map/ppermute | solution.py:340
  84.2 2.8 %collective-permute-done.4.b1_ref = bf16[128,384]{1,0:T(8,128)(2,1)S(1)} collective-permute-done((bf16[128,384]{1,0:T(8,128)(2,1)S(1)}, bf16[128,384]{1,0:T(8,128)(2,1)S(1)}, u32[]{:S(2)}, u32[]{:S(2)}) %collective-permute-start.4) | collective-permute-done | bytes 98336 | tf_op jit(solution)/shard_map/ppermute | solution.py:340
  87.0 3.9 %shard_map.106 = (bf16[384,1536]{1,0:T(8,128)(2,1)S(1)}, bf16[384,1536]{1,0:T(8,128)(2,1)}) custom-call(bf16[128,1280]{1,0:T(8,128)(2,1)S(1)} %copy-done.4, bf16[128,1280]{1,0:T(8,128)(2,1)S(1)} %collective-permute-done.up_ref, bf16[128,1280]{1,0:T(8,128)(2,1)S(1)} %collective-permute-done.1.right_ref, bf16[128,1280]{1,0:T(8,128)(2,1)S(1)} %copy-done.6, ...), custom_call_target="tpu_custom_call" | custom-call | flops 1 | bytes 1 | tf_op jit(solution)/shard_map/pallas_call | solution.py:31
  94.5 8.4 %all-to-all-start.1 = ((bf16[32,2,768]{2,1,0:T(2,128)(2,1)}), bf16[32,2,768]{2,1,0:T(2,128)(2,1)S(1)}, u32[]{:S(2)}, u32[]{:S(2)}) async-start(bf16[32,2,768]{2,1,0:T(2,128)(2,1)} %reshape.396), calls=%async_computation.1 | async-start | bytes 196608 | tf_op jit(solution)/shard_map/all_to_all | solution.py:399
  105.3 6.3 %all-to-all-done.1 = bf16[32,2,768]{2,1,0:T(2,128)(2,1)S(1)} async-done(((bf16[32,2,768]{2,1,0:T(2,128)(2,1)}), bf16[32,2,768]{2,1,0:T(2,128)(2,1)S(1)}, u32[]{:S(2)}, u32[]{:S(2)}) %all-to-all-start.1) | async-done | bytes 98336 | tf_op jit(solution)/shard_map/all_to_all | solution.py:399
  112.2 1.3 copy-done.9
  113.5 1.6 shard_map.108
  115.8 13.3 %collective-permute-done.9.b1_ref = bf16[128,768]{1,0:T(8,128)(2,1)S(1)} collective-permute-done((bf16[128,768]{1,0:T(8,128)(2,1)S(1)}, bf16[128,768]{1,0:T(8,128)(2,1)S(1)}, u32[]{:S(2)}, u32[]{:S(2)}) %collective-permute-start.9) | collective-permute-done | bytes 196640 | tf_op jit(solution)/shard_map/ppermute | solution.py:340
  129.1 25.6 %all_to_all.36.in_ref = bf16[16,32,1536]{2,1,0:T(8,128)(2,1)S(1)} all-to-all(bf16[16,32,1536]{2,1,0:T(8,128)(2,1)S(1)} %shard_map.108), channel_id=1, replica_groups=mesh['zh'=2,'x'=4,'zl'=4,'y'=4,'core'=2] {'x','y'}, dimensions={0} | all-to-all | bytes 3145728 | tf_op jit(solution)/shard_map/all_to_all | solution.py:413
  156.6 3.4 %all-to-all-start.3 = ((bf16[8,2,3456]{2,1,0:T(2,128)(2,1)}), bf16[8,2,3456]{2,1,0:T(2,128)(2,1)S(1)}, u32[]{:S(2)}, u32[]{:S(2)}) async-start(bf16[8,2,3456]{2,1,0:T(2,128)(2,1)} %reshape.398), calls=%async_computation.3 | async-start | bytes 221184 | tf_op jit(solution)/shard_map/all_to_all | solution.py:415
  160.1 1.6 shard_map.103
  161.7 2.1 %shard_map.109 = bf16[8,8,8,768]{3,2,1,0:T(8,128)(2,1)} custom-call(bf16[8,8,8,768]{3,2,1,0:T(8,128)(2,1)S(1)} %copy-done.1, bf16[8,8,8,768]{3,2,1,0:T(8,128)(2,1)S(1)} %copy-done.2, bf16[128,768]{1,0:T(8,128)(2,1)S(1)} %collective-permute-done.8.b0_ref, bf16[128,768]{1,0:T(8,128)(2,1)S(1)} %collective-permute-done.9.b1_ref, ...), custom_call_target="tpu_custom_call" | custom-call | flops 1 | bytes 1 | tf_op jit(solution)/shard_map/pallas_call | solution.py:31
  163.8 4.0 %all-to-all-done.3 = bf16[8,2,3456]{2,1,0:T(2,128)(2,1)S(1)} async-done(((bf16[8,2,3456]{2,1,0:T(2,128)(2,1)}), bf16[8,2,3456]{2,1,0:T(2,128)(2,1)S(1)}, u32[]{:S(2)}, u32[]{:S(2)}) %all-to-all-start.3) | async-done | bytes 110624 | tf_op jit(solution)/shard_map/all_to_all | solution.py:415
  (93 shorter events, 16.3 us)
Async XLA Ops:
  0.6 50.0 %copy-start = (bf16[768,1152]{1,0:T(8,128)(2,1)S(1)}, bf16[768,1152]{1,0:T(8,128)(2,1)}, u32[]{:S(2)}) copy-start(bf16[768,1152]{1,0:T(8,128)(2,1)} %wi_ref.3) | copy-start | bytes 5308420
  5.4 45.3 %copy-start.4 = (bf16[128,1280]{1,0:T(8,128)(2,1)S(1)}, bf16[128,1280]{1,0:T(8,128)(2,1)}, u32[]{:S(2)}) copy-start(bf16[128,1280]{1,0:T(8,128)(2,1)} %get-tuple-element.35.own_ref) | copy-start | bytes 983044
  5.4 45.2 %collective-permute-start = (bf16[128,1280]{1,0:T(8,128)(2,1)}, bf16[128,1280]{1,0:T(8,128)(2,1)S(1)}, u32[]{:S(2)}, u32[]{:S(2)}) collective-permute-start(bf16[128,1280]{1,0:T(8,128)(2,1)} %get-tuple-element.36), channel_id=1, source_target_pairs={{0,31},{1,0},{2,1},{3,2},{4,3},{5,4},{6,5},{7,6},{8,7},{9,8},{10,9... | collective-permute-start | bytes 983048 | tf_op jit(solution)/shard_map/ppermute | solution.py:340
  8.7 41.9 %collective-permute-start.1 = (bf16[128,1280]{1,0:T(8,128)(2,1)}, bf16[128,1280]{1,0:T(8,128)(2,1)S(1)}, u32[]{:S(2)}, u32[]{:S(2)}) collective-permute-start(bf16[128,1280]{1,0:T(8,128)(2,1)} %get-tuple-element.37), channel_id=1, source_target_pairs={{0,224},{1,225},{2,226},{3,227},{4,228},{5,229},{6,230},{7,231},{8... | collective-permute-start | bytes 983048 | tf_op jit(solution)/shard_map/ppermute | solution.py:340
  16.0 34.5 %collective-permute-start.2 = (bf16[128,1280]{1,0:T(8,128)(2,1)}, bf16[128,1280]{1,0:T(8,128)(2,1)S(1)}, u32[]{:S(2)}, u32[]{:S(2)}) collective-permute-start(bf16[128,1280]{1,0:T(8,128)(2,1)} %get-tuple-element.38), channel_id=1, source_target_pairs={{0,255},{1,224},{2,225},{3,226},{4,227},{5,228},{6,229},{7,230},{8... | collective-permute-start | bytes 983048 | tf_op jit(solution)/shard_map/ppermute | solution.py:340
  23.3 27.1 %all-to-all-start = ((bf16[32,2,768]{2,1,0:T(2,128)(2,1)}), bf16[32,2,768]{2,1,0:T(2,128)(2,1)S(1)}, u32[]{:S(2)}, u32[]{:S(2)}) async-start(bf16[32,2,768]{2,1,0:T(2,128)(2,1)} %reshape.394), calls=%async_computation | async-start | bytes 196608 | tf_op jit(solution)/shard_map/all_to_all | solution.py:365
  50.5 9.0 %copy-start.25 = (bf16[32,1,1536]{2,1,0:T(2,128)(2,1)}, bf16[32,1,1536]{2,1,0:T(2,128)(2,1)S(1)}, u32[]{:S(2)}) copy-start(bf16[32,1,1536]{2,1,0:T(2,128)(2,1)S(1)} %reshape.395) | copy-start | bytes 294916
  50.6 8.9 %copy-start.5 = (bf16[128,1280]{1,0:T(8,128)(2,1)}, bf16[128,1280]{1,0:T(8,128)(2,1)S(1)}, u32[]{:S(2)}) copy-start(bf16[128,1280]{1,0:T(8,128)(2,1)S(1)} %collective-permute-done.2.both_ref) | copy-start | bytes 983044
  59.5 27.4 %copy-start.10 = (bf16[128,384]{1,0:T(8,128)(2,1)}, bf16[128,384]{1,0:T(8,128)(2,1)S(1)}, u32[]{:S(2)}) copy-start(bf16[128,384]{1,0:T(8,128)(2,1)S(1)} %get-tuple-element.43.b3_ref) | copy-start | bytes 294916
  60.6 14.9 %copy-start.2 = (bf16[8,8,8,768]{3,2,1,0:T(8,128)(2,1)S(1)}, bf16[8,8,8,768]{3,2,1,0:T(8,128)(2,1)}, u32[]{:S(2)}) copy-start(bf16[8,8,8,768]{3,2,1,0:T(8,128)(2,1)} %cot_ref.3) | copy-start | bytes 2359300
  72.3 4.6 %collective-permute-start.6 = (bf16[128,768]{1,0:T(8,128)(2,1)S(1)}, bf16[128,768]{1,0:T(8,128)(2,1)S(1)}, u32[]{:S(2)}, u32[]{:S(2)}) collective-permute-start(bf16[128,768]{1,0:T(8,128)(2,1)S(1)} %get-tuple-element.50), channel_id=1, source_target_pairs={{0,1},{1,2},{2,3},{3,4},{4,5},{5,6},{6,7},{7,8},{8,9},{9,10},{10,1... | collective-permute-start | bytes 589832 | tf_op jit(solution)/shard_map/ppermute | solution.py:340
  73.0 11.2 %collective-permute-start.3 = (bf16[128,384]{1,0:T(8,128)(2,1)S(1)}, bf16[128,384]{1,0:T(8,128)(2,1)S(1)}, u32[]{:S(2)}, u32[]{:S(2)}) collective-permute-start(bf16[128,384]{1,0:T(8,128)(2,1)S(1)} %get-tuple-element.40), channel_id=1, source_target_pairs={{0,33},{1,34},{2,35},{3,36},{4,37},{5,38},{6,39},{7,40},{8,41},{9,... | collective-permute-start | bytes 294920 | tf_op jit(solution)/shard_map/ppermute | solution.py:340
  73.0 14.0 %collective-permute-start.4 = (bf16[128,384]{1,0:T(8,128)(2,1)S(1)}, bf16[128,384]{1,0:T(8,128)(2,1)S(1)}, u32[]{:S(2)}, u32[]{:S(2)}) collective-permute-start(bf16[128,384]{1,0:T(8,128)(2,1)S(1)} %get-tuple-element.41), channel_id=1, source_target_pairs={{0,32},{1,33},{2,34},{3,35},{4,36},{5,37},{6,38},{7,39},{8,40},{9,... | collective-permute-start | bytes 294920 | tf_op jit(solution)/shard_map/ppermute | solution.py:340
  73.0 14.0 %collective-permute-start.5 = (bf16[128,384]{1,0:T(8,128)(2,1)S(1)}, bf16[128,384]{1,0:T(8,128)(2,1)S(1)}, u32[]{:S(2)}, u32[]{:S(2)}) collective-permute-start(bf16[128,384]{1,0:T(8,128)(2,1)S(1)} %get-tuple-element.42), channel_id=1, source_target_pairs={{0,1},{1,2},{2,3},{3,4},{4,5},{5,6},{6,7},{7,8},{8,9},{9,10},{10,1... | collective-permute-start | bytes 294920 | tf_op jit(solution)/shard_map/ppermute | solution.py:340
  87.0 6.2 %copy-start.21 = (bf16[32,1536]{1,0:T(8,128)(2,1)S(1)}, bf16[32,1536]{1,0:T(8,128)(2,1)}, u32[]{:S(2)}) copy-start(bf16[32,1536]{1,0:T(8,128)(2,1)} %copy-done.20) | copy-start | bytes 294916
  87.0 16.0 %copy-start.23 = (bf16[128,768]{1,0:T(8,128)(2,1)S(1)}, bf16[128,768]{1,0:T(8,128)(2,1)}, u32[]{:S(2)}) copy-start(bf16[128,768]{1,0:T(8,128)(2,1)} %copy-done.22) | copy-start | bytes 589828
  91.9 19.8 %copy-start.3 = (bf16[768,768]{1,0:T(8,128)(2,1)S(1)}, bf16[768,768]{1,0:T(8,128)(2,1)}, u32[]{:S(2)}) copy-start(bf16[768,768]{1,0:T(8,128)(2,1)} %wc_ref.1) | copy-start | bytes 3538948
  91.9 20.2 %collective-permute-start.7 = (bf16[384,1536]{1,0:T(8,128)(2,1)}, bf16[384,1536]{1,0:T(8,128)(2,1)}, u32[]{:S(2)}, u32[]{:S(2)}) collective-permute-start(bf16[384,1536]{1,0:T(8,128)(2,1)} %get-tuple-element.53), channel_id=1, source_target_pairs={{0,1},{1,0},{2,3},{3,2},{4,5},{5,4},{6,7},{7,6},{8,9},{9,8},{10,11... | collective-permute-start | bytes 3538952 | tf_op jit(solution)/shard_map/ppermute | solution.py:406
  94.5 17.1 %all-to-all-start.1 = ((bf16[32,2,768]{2,1,0:T(2,128)(2,1)}), bf16[32,2,768]{2,1,0:T(2,128)(2,1)S(1)}, u32[]{:S(2)}, u32[]{:S(2)}) async-start(bf16[32,2,768]{2,1,0:T(2,128)(2,1)} %reshape.396), calls=%async_computation.1 | async-start | bytes 196608 | tf_op jit(solution)/shard_map/all_to_all | solution.py:399
  102.9 12.9 %collective-permute-start.8 = (bf16[128,768]{1,0:T(8,128)(2,1)}, bf16[128,768]{1,0:T(8,128)(2,1)S(1)}, u32[]{:S(2)}, u32[]{:S(2)}) collective-permute-start(bf16[128,768]{1,0:T(8,128)(2,1)} %copy-done.24), channel_id=1, source_target_pairs={{0,33},{1,34},{2,35},{3,36},{4,37},{5,38},{6,39},{7,40},{8,41},{9,... | collective-permute-start | bytes 589832 | tf_op jit(solution)/shard_map/ppermute | solution.py:340
  103.0 26.1 %collective-permute-start.9 = (bf16[128,768]{1,0:T(8,128)(2,1)S(1)}, bf16[128,768]{1,0:T(8,128)(2,1)S(1)}, u32[]{:S(2)}, u32[]{:S(2)}) collective-permute-start(bf16[128,768]{1,0:T(8,128)(2,1)S(1)} %copy-done.23), channel_id=1, source_target_pairs={{0,32},{1,33},{2,34},{3,35},{4,36},{5,37},{6,38},{7,39},{8,40},{9,... | collective-permute-start | bytes 589832 | tf_op jit(solution)/shard_map/ppermute | solution.py:340
  154.7 5.3 %copy-start.13 = (bf16[128,384]{1,0:T(8,128)(2,1)S(1)}, bf16[128,384]{1,0:T(8,128)(2,1)}, u32[]{:S(2)}) copy-start(bf16[128,384]{1,0:T(8,128)(2,1)} %copy-done.12) | copy-start | bytes 294916
  154.7 5.3 %copy-start.15 = (bf16[128,384]{1,0:T(8,128)(2,1)S(1)}, bf16[128,384]{1,0:T(8,128)(2,1)}, u32[]{:S(2)}) copy-start(bf16[128,384]{1,0:T(8,128)(2,1)} %copy-done.14) | copy-start | bytes 294916
  156.6 11.1 %all-to-all-start.3 = ((bf16[8,2,3456]{2,1,0:T(2,128)(2,1)}), bf16[8,2,3456]{2,1,0:T(2,128)(2,1)S(1)}, u32[]{:S(2)}, u32[]{:S(2)}) async-start(bf16[8,2,3456]{2,1,0:T(2,128)(2,1)} %reshape.398), calls=%async_computation.3 | async-start | bytes 221184 | tf_op jit(solution)/shard_map/all_to_all | solution.py:415
  (15 other events, 41.6 us)

commit v2 on v1

--- a/solution.py
+++ b/solution.py
@@ -19,12 +19,12 @@
 f32 = jnp.float32
 
 
-def dot(left, right):
-    return jnp.dot(left, right, preferred_element_type=f32)
-
-
-def dot_nt(left, right):
-    return lax.dot_general(left, right, (((1,), (1,)), ((), ())), preferred_element_type=f32)
+def dot(left, side):
+    return jnp.dot(left, side, preferred_element_type=f32)
+
+
+def dot_nt(left, side):
+    return lax.dot_general(left, side, (((1,), (1,)), ((), ())), preferred_element_type=f32)
 
 
 def call(kernel, outs, *args, scratch=(), far=(), scalars=(), grant=16):
@@ -69,10 +69,14 @@
     return jnp.stack([a, b], axis=1).reshape(2 * m, 8, d)
 
 
-def x_half(ref, half):
+def halves(core_ref, x):
+    far = core_ref[0, 0] * (x // 2)
+    return far, x // 2 - far
+
+
+def x_half(ref, start):
     x, y, z, d = ref.shape
-    rows = ref[half * (x // 2) : (half + 1) * (x // 2)].astype(f32)
-    return rows.reshape(x // 2 * y, z, d)
+    return ref[pl.ds(start, x // 2)].astype(f32).reshape(x // 2 * y, z, d)
 
 
 def columns_of(mask):
@@ -85,9 +89,9 @@
 
 
 def prepare(*refs):
-    sources, mask_ref, refs = refs[:4], refs[4], refs[5:]
+    sources, mask_ref, core_ref, refs = refs[:4], refs[4], refs[5], refs[6:]
     outs, held, sems = refs[:5], refs[5:9], refs[9]
-    both_ref, right_ref, up_ref, own_ref, coarse_ref = outs
+    up_ref, side_ref, both_ref, own_ref, coarse_ref = outs
     tok_ref, cot_ref, wo_ref, wc_ref = held
     copies = [pltpu.make_async_copy(a, b, sems.at[i]) for i, (a, b) in enumerate(zip(sources, held))]
     for copy in copies:
@@ -98,32 +102,33 @@
     cells = 1
     for n in tok_ref.shape[:3]:
         cells *= n
-    halves = ((0, (both_ref, right_ref)), (1, (up_ref, own_ref)))
-    for half, refs in halves:
-        normed, _ = normalize(x_half(tok_ref, half))
+    away, home = halves(core_ref, tok_ref.shape[0])
+    places = ((away, (up_ref, side_ref)), (home, (both_ref, own_ref)))
+    for start, refs in places:
+        normed, _ = normalize(x_half(tok_ref, start))
         total += jnp.sum(jnp.sum(normed, axis=0), axis=0, keepdims=True)
         for ref, part in zip(refs, split_z(normed)):
             ref[:, :d] = part.astype(bf16)
         x, y, z = mask_ref.shape
-        cells_in = mask_ref[half * (x // 2) : (half + 1) * (x // 2)].astype(f32)
+        cells_in = mask_ref[pl.ds(start, x // 2)].astype(f32)
         for ref, part in zip(refs, split_z(columns_of(cells_in.reshape(x // 2 * y, z)))):
             ref[:, d + inner :] = part.astype(bf16)
     copies[1].wait()
     copies[2].wait()
-    for half, refs in halves:
-        for ref, part in zip(refs, split_z(x_half(cot_ref, half))):
+    for start, refs in places:
+        for ref, part in zip(refs, split_z(x_half(cot_ref, start))):
             ref[:, d : d + inner] = dot_nt(part.astype(bf16), wo_ref[...]).astype(bf16)
     copies[3].wait()
-    pooled = jnp.broadcast_to((total / cells).astype(bf16), (coarse_ref.shape[0], d))
+    pooled = (total / cells).astype(bf16)
     coarse_ref[:, :d] = pooled
-    coarse_ref[:, d:] = dot(pooled, wc_ref[...]).astype(bf16)
-
-
-def turn_cot(cot_ref, src_ref, out_ref):
+    coarse_ref[:, d:] = dot(jnp.broadcast_to(pooled, (8, d)), wc_ref[...])[:1].astype(bf16)
+
+
+def turn_cot(cot_ref, src_ref, core_ref, out_ref):
     d = cot_ref.shape[3]
     parts = []
-    for half in (0, 1):
-        parts += [p.astype(bf16) for p in split_z(x_half(cot_ref, half))]
+    for start in halves(core_ref, cot_ref.shape[0]):
+        parts += [p.astype(bf16) for p in split_z(x_half(cot_ref, start))]
     perm = picks(src_ref, d)
     n = parts[0].shape[0]
     for i, part in enumerate(parts):
@@ -148,21 +153,21 @@
     mask_ref[4 * n :] = jnp.zeros((mask_ref.shape[0] - 4 * n, mask_ref.shape[1]), f32)
 
 
-def attend(own_ref, up_ref, right_ref, both_ref, wi_ref, kv_ref,
+def attend(own_ref, up_ref, side_ref, both_ref, wi_ref, kv_ref,
            a0_ref, a1_ref, a2_ref, a3_ref, q_ref, k_ref, v_ref, m_ref, l_ref, out_ref, mask_ref):
     d, width = wi_ref.shape
     inner = width // 3
     n = own_ref.shape[0]
     tokens = 4 * n
-    for i, ref in enumerate((own_ref, up_ref, right_ref, both_ref)):
+    for i, ref in enumerate((own_ref, up_ref, side_ref, both_ref)):
         packed = dot(ref[:, :d], wi_ref[...])
         rows = slice(i * n, (i + 1) * n)
         q_ref[rows] = packed[:, :inner].astype(bf16) * bf16(0.125)
         k_ref[rows] = packed[:, inner : 2 * inner].astype(bf16)
         v_ref[rows] = packed[:, 2 * inner :].astype(bf16)
-    hide(mask_ref, (own_ref, up_ref, right_ref, both_ref), d + inner)
-    k_ref[tokens:] = kv_ref[:, d : d + inner]
-    v_ref[tokens:] = kv_ref[:, d + inner :]
+    hide(mask_ref, (own_ref, up_ref, side_ref, both_ref), d + inner)
+    k_ref[tokens:] = kv_ref[:, :inner]
+    v_ref[tokens:] = kv_ref[:, inner:]
     eye = jnp.where(
         lax.broadcasted_iota(jnp.int32, (PAIR, PAIR), 0)
         == lax.broadcasted_iota(jnp.int32, (PAIR, PAIR), 1), 1.0, 0.0).astype(bf16)
@@ -194,15 +199,15 @@
         ref[...] = out_ref[i * n : (i + 1) * n]
 
 
-def attend_back(own_ref, up_ref, right_ref, both_ref, wi_ref, q_ref, k_ref, v_ref, m_ref, l_ref,
+def attend_back(own_ref, up_ref, side_ref, both_ref, wi_ref, q_ref, k_ref, v_ref, m_ref, l_ref,
                 d0_ref, d1_ref, d2_ref, d3_ref, grad_ref, coarse_ref, g_ref, dk_ref, dv_ref, mask_ref):
     d, width = wi_ref.shape
     inner = width // 3
     n = own_ref.shape[0]
     tokens = 4 * n
-    for i, ref in enumerate((own_ref, up_ref, right_ref, both_ref)):
+    for i, ref in enumerate((own_ref, up_ref, side_ref, both_ref)):
         g_ref[i * n : (i + 1) * n] = ref[:, d : d + inner]
-    hide(mask_ref, (own_ref, up_ref, right_ref, both_ref), d + inner)
+    hide(mask_ref, (own_ref, up_ref, side_ref, both_ref), d + inner)
     eye = jnp.where(
         lax.broadcasted_iota(jnp.int32, (PAIR, PAIR), 0)
         == lax.broadcasted_iota(jnp.int32, (PAIR, PAIR), 1), 1.0, 0.0).astype(bf16)
@@ -249,13 +254,13 @@
         ref[...] = dot_nt(grad_ref[i * n : (i + 1) * n], wi_ref[...]).astype(bf16)
 
 
-def weight_grads(own_ref, up_ref, right_ref, both_ref, src_ref, grad_ref, cot_ref,
+def weight_grads(own_ref, up_ref, side_ref, both_ref, src_ref, grad_ref, cot_ref,
                  b0_ref, b1_ref, b2_ref, b3_ref, keep_ref, send_ref, turned_ref, att_ref):
     d = src_ref.shape[0]
     n = own_ref.shape[0]
     width = grad_ref.shape[1]
     perm = picks(src_ref, d)
-    for i, ref in enumerate((own_ref, up_ref, right_ref, both_ref)):
+    for i, ref in enumerate((own_ref, up_ref, side_ref, both_ref)):
         turned_ref[:, i * n : (i + 1) * n] = dot_nt(perm, ref[:, :d]).astype(bf16)
     for i, ref in enumerate((b0_ref, b1_ref, b2_ref, b3_ref)):
         att_ref[i * n : (i + 1) * n] = ref[...]
@@ -264,21 +269,23 @@
         ref[:, width:] = dot(cot_ref[rows], att_ref[...]).astype(bf16)
 
 
-def block_result(tok_ref, b0_ref, b1_ref, b2_ref, b3_ref, wo_ref, out_ref):
+def block_result(tok_ref, b0_ref, b1_ref, b2_ref, b3_ref, wo_ref, core_ref, out_ref):
     x = tok_ref.shape[0]
-    for half, refs in ((0, (b0_ref, b1_ref)), (1, (b2_ref, b3_ref))):
+    for start, refs in zip(halves(core_ref, x), ((b0_ref, b1_ref), (b2_ref, b3_ref))):
         branch = [dot(ref[...], wo_ref[...]).astype(bf16).astype(f32) for ref in refs]
-        total = x_half(tok_ref, half) + join_z(*branch)
-        out_ref[half * (x // 2) : (half + 1) * (x // 2)] = total.astype(bf16).reshape(
+        total = x_half(tok_ref, start) + join_z(*branch)
+        out_ref[pl.ds(start, x // 2)] = total.astype(bf16).reshape(
             (x // 2,) + out_ref.shape[1:])
 
 
-def coarse_total(parts_ref, wc_ref, core_ref, pair_ref, pooled_ref):
-    d = wc_ref.shape[0]
-    total = jnp.sum(parts_ref[...].astype(f32), axis=0, keepdims=True).astype(bf16)
-    pair_ref[...] = total
-    row = jnp.where(core_ref[0, 0] == 0, total[:, :d], total[:, d:])
-    pooled_ref[...] = dot_nt(jnp.broadcast_to(row, (8, d)), wc_ref[...])
+def coarse_total(parts_ref, core_ref, pair_ref, here_ref, there_ref):
+    d = parts_ref.shape[1] // 2
+    parts = parts_ref[...].astype(f32)
+    even = lax.broadcasted_iota(jnp.int32, parts.shape, 0) % 2 == 0
+    for i, ref in ((0, here_ref), (1, there_ref)):
+        total = jnp.sum(jnp.where(even == (i == 0), parts, 0.0), axis=0, keepdims=True)
+        pair_ref[pl.ds(i, 1)] = total
+        ref[...] = jnp.where(core_ref[0, 0] == 0, total[:, :d], total[:, d:])
 
 
 def assemble(keep_ref, other_ref, pair_ref, picked_ref, out_ref):
@@ -289,9 +296,9 @@
     for i in range(plane):
         part = slice(i * rows, (i + 1) * rows)
         out_ref[i, :rows] = (keep_ref[part].astype(f32) + other_ref[part].astype(f32)).astype(bf16)
-        extra = jnp.where(line == 0, pair_ref[...].astype(f32), 0.0)
+        extra = jnp.where(line == 0, pair_ref[0:1], jnp.where(line == 1, pair_ref[1:2], 0.0))
         out_ref[i, rows:] = extra.astype(bf16)
-        seen = jnp.where(line[:, :lanes] == 1, picked_ref[i : i + 1].astype(f32), extra[:, :lanes])
+        seen = jnp.where(line[:, :lanes] == 2, picked_ref[i : i + 1].astype(f32), extra[:, :lanes])
         out_ref[i, rows:, :lanes] = seen.astype(bf16)
 
 
@@ -303,12 +310,13 @@
     total = jnp.sum(in_ref[:, :rows].astype(f32), axis=0)
     extra = in_ref[:, rows:].astype(f32)
     line = lax.broadcasted_iota(jnp.int32, extra.shape, 1)
-    grads = jnp.sum(jnp.where(line == 0, extra, 0.0), axis=1).astype(bf16)
-    picked = jnp.sum(jnp.where(line == 1, extra, 0.0), axis=1)[:, :256].astype(bf16)
+    picked = jnp.sum(jnp.where(line == 2, extra, 0.0), axis=1)[:, :512].astype(bf16)
     coarse = jnp.zeros((128, half), f32)
-    for i in range(2):
+    for i in range(4):
+        if i % 2 == 0:
+            grads = jnp.sum(jnp.where(line == i // 2, extra, 0.0), axis=1).astype(bf16)
         coarse += lax.dot_general(
-            picked[:, i * 128 : (i + 1) * 128], grads[:, i * half : (i + 1) * half],
+            picked[:, i * 128 : (i + 1) * 128], grads[:, i % 2 * half : (i % 2 + 1) * half],
             (((0,), (0,)), ((), ())), preferred_element_type=f32)
     step = out_ref.shape[1] // (rows // deep)
     for j in range(rows // deep):
@@ -317,31 +325,47 @@
         out_ref[:, j * step + width : (j + 1) * step] = coarse[part].astype(bf16)
 
 
-def token_result(tok_ref, cot_ref, b0_ref, b1_ref, b2_ref, b3_ref, pooled_ref, out_ref):
+def token_result(tok_ref, cot_ref, b0_ref, b1_ref, b2_ref, b3_ref, here_ref, next_ref, wc_ref, core_ref, out_ref):
     x, y, z, d = tok_ref.shape
-    pooled = (pooled_ref[0:1] / float(x * y * z))[None]
-    for half, refs in ((0, (b0_ref, b1_ref)), (1, (b2_ref, b3_ref))):
-        normed, inv_std = normalize(x_half(tok_ref, half))
+    coarse = (here_ref[...] + next_ref[...]).astype(bf16)
+    pooled = dot_nt(jnp.broadcast_to(coarse, (8, d)), wc_ref[...])[0:1]
+    pooled = (pooled / float(x * y * z))[None]
+    for start, refs in zip(halves(core_ref, x), ((b0_ref, b1_ref), (b2_ref, b3_ref))):
+        normed, inv_std = normalize(x_half(tok_ref, start))
         grad = join_z(*[ref[...].astype(f32) for ref in refs]) + pooled
         first = jnp.mean(grad, axis=-1, keepdims=True)
         second = jnp.mean(grad * normed, axis=-1, keepdims=True)
-        total = x_half(cot_ref, half) + inv_std * (grad - first - normed * second)
-        out_ref[half * (x // 2) : (half + 1) * (x // 2)] = total.astype(bf16).reshape(
+        total = x_half(cot_ref, start) + inv_std * (grad - first - normed * second)
+        out_ref[pl.ds(start, x // 2)] = total.astype(bf16).reshape(
             (x // 2,) + out_ref.shape[1:])
 
 
-def moved(block, dx, dz):
+def passed(block, step, back=False):
     nx, nz = lax.axis_size(GX), lax.axis_size(GZ)
-    route = [
-        (a * nz + c, ((a + dx) % nx) * nz + (c + dz) % nz)
-        for a in range(nx)
-        for c in range(nz)
-    ]
+    route = []
+    for a in range(nx):
+        for c in range(nz):
+            to_a, to_c = step(a, c)
+            route.append((a * nz + c, to_a % nx * nz + to_c % nz))
+    if back:
+        route = [(b, a) for a, b in route]
     return lax.ppermute(block, ALL, route)
 
 
-def returned(own, up, right, both):
-    return moved(both, 1, 1), moved(right, 1, 0), moved(up, 0, 1), own
+def to_up(a, c):
+    return a, c - 1
+
+
+def to_side(a, c):
+    return (a - 1, c) if c % 2 == 0 else (a + 1, c)
+
+
+def to_both(a, c):
+    return (a - 1, c - 1) if c % 2 else (a + 1, c - 1)
+
+
+def returned(own, up, side, both):
+    return passed(up, to_up, True), passed(side, to_side, True), passed(both, to_both, True), own
 
 
 def body(tokens, body_mask, cotangent, w_in, w_out, w_coarse):
@@ -356,28 +380,37 @@
     core = lax.axis_index("core")
 
     wide = (n, d + inner + 128)
-    both, right, up, own, far = call(
-        prepare, [(wide, bf16)] * 4 + [((coarse, 2 * d), bf16)], tokens, cotangent, w_out, w_coarse, body_mask,
+    place = core.reshape(1, 1)
+    up, side, both, own, row = call(
+        prepare, [(wide, bf16)] * 4 + [((1, 2 * d), bf16)], tokens, cotangent, w_out, w_coarse, body_mask, place,
         far=range(4),
+        scalars=(5,),
         grant=60,
         scratch=[pltpu.VMEM(a.shape, bf16) for a in (tokens, cotangent, w_out, w_coarse)] + [pltpu.SemaphoreType.DMA((4,))])
-    up, right, both = moved(up, 0, -1), moved(right, -1, 0), moved(both, -1, -1)
-    far = lax.all_to_all(far, GZ, 0, 0, tiled=True)
+    before = passed(row, lambda a, c: (a + 1, c))
+    up, side, both = passed(up, to_up), passed(side, to_side), passed(both, to_both)
+
+    odd = lax.broadcasted_iota(jnp.int32, (coarse, 1), 0) % 2 == 1
+    shared = jnp.broadcast_to(jnp.concatenate([row[:, :d], before[:, :d]], axis=1), (coarse, 2 * d))
+    kv = jnp.where(odd, before[:, d:], row[:, d:])
+    far = lax.all_to_all(jnp.concatenate([shared, kv], axis=1), GZ, 0, 0, tiled=True)
+    kv = far[:, 2 * d :]
 
     zh, nx, zl, ny, cores = (lax.axis_size(a) for a in ALL)
     plane, deep = nx * ny, zh * zl
-    mine = lax.dynamic_slice_in_dim(far, lax.axis_index(GZ) // cores * cores, cores, axis=0)[:, :d]
-    mine = mine.reshape(cores, zh, nx, zl, ny, cores, per)
-    mine = lax.dynamic_index_in_dim(mine, core, axis=5, keepdims=False)
-    mine = jnp.transpose(mine, (2, 4, 0, 5, 1, 3)).reshape(plane, cores, per * deep)
-    picked = jnp.pad(mine, ((0, 0), (0, 0), (0, 128 - per * deep))).reshape(plane, cores * 128)
+    mine = lax.dynamic_slice_in_dim(far, lax.axis_index(GZ) // cores * cores, cores, axis=0)[:, : 2 * d]
+    mine = mine.reshape(cores, 2, zh, nx, zl, ny, cores, per)
+    mine = lax.dynamic_index_in_dim(mine, core, axis=6, keepdims=False)
+    mine = jnp.transpose(mine, (3, 5, 1, 0, 6, 2, 4)).reshape(plane, 2 * cores, per * deep)
+    picked = jnp.pad(mine, ((0, 0), (0, 0), (0, 128 - per * deep))).reshape(plane, 2 * cores * 128)
 
     row = jnp.arange(d, dtype=jnp.int32)
     half, rest = row // (d // 2), row % (d // 2)
     chip, j, depth = rest // (per * deep), rest % (per * deep) // deep, rest % deep
     device = ((depth // zl * nx + chip // ny) * zl + depth % zl) * ny + chip % ny
     src = ((device * cores + (half + core) % cores) * per + j).reshape(d, 1)
-    (cot_turned,) = call(turn_cot, [((d, size), bf16)], cotangent, src)
+    (cot_turned,) = call(turn_cot, [((d, size), bf16)], cotangent, src, place, scalars=(2,))
+    kv, cot_turned = lax.optimization_barrier((kv, cot_turned))
 
     slim = (n, inner)
     a0, a1, a2, a3, q, k, v, top, inv = call(
@@ -385,27 +418,28 @@
         [(slim, bf16)] * 4
         + [((size, inner), bf16), ((size + coarse, inner), bf16), ((size + coarse, inner), bf16)]
         + [((16, CHUNK), f32)] * 2,
-        own, up, right, both, w_in, far,
+        own, up, side, both, w_in, kv,
         scratch=[pltpu.VMEM((size, inner), bf16), pltpu.VMEM((size + coarse, 128), f32)])
     b0, b1, b2, b3 = returned(a0, a1, a2, a3)
 
     d0, d1, d2, d3, grad, coarse_part = call(
         attend_back,
         [((n, d), bf16)] * 4 + [((size, 3 * inner), bf16), ((coarse, 4 * inner), bf16)],
-        own, up, right, both, w_in, q, k, v, top, inv,
+        own, up, side, both, w_in, q, k, v, top, inv,
         scratch=[pltpu.VMEM((size, inner), bf16)] + [pltpu.VMEM((size + coarse, inner), f32)] * 2
         + [pltpu.VMEM((size + coarse, 128), f32)])
     e0, e1, e2, e3 = returned(d0, d1, d2, d3)
     parts = lax.all_to_all(coarse_part, GZ, 0, 0, tiled=True)
 
-    grad, e2 = lax.optimization_barrier((grad, e2))
+    grad, parts, e0 = lax.optimization_barrier((grad, parts, e0))
     keep, send = call(
         weight_grads, [((d // 2, 4 * inner), bf16)] * 2,
-        own, up, right, both, src, grad, cot_turned, b0, b1, b2, b3,
+        own, up, side, both, src, grad, cot_turned, b0, b1, b2, b3,
         scratch=[pltpu.VMEM((d, size), bf16), pltpu.VMEM((size, inner), bf16)])
     other = lax.ppermute(send, "core", [(0, 1), (1, 0)])
-    pair, grad_pooled = call(
-        coarse_total, [((1, 4 * inner), bf16), ((8, d), f32)], parts, w_coarse, core.reshape(1, 1), scalars=(2,))
+    pair, here, there = call(
+        coarse_total, [((2, 4 * inner), f32), ((1, d), f32), ((1, d), f32)], parts, place, scalars=(1,))
+    later = passed(there, lambda a, c: (a - 1, c))
 
     (packet,) = call(
         assemble, [((plane, per * deep + 8, 4 * inner), bf16)], keep, other, pair, picked)
@@ -414,8 +448,9 @@
     (slab,) = call(plane_sums, [((deep, per * 6 * inner), bf16)], packet)
     slab = lax.all_to_all(slab, ("zh", "zl"), 0, 0, tiled=True)
 
-    (block_out,) = call(block_result, [(tokens.shape, bf16)], tokens, b0, b1, b2, b3, w_out)
-    (token_grad,) = call(token_result, [(tokens.shape, bf16)], tokens, cotangent, e0, e1, e2, e3, grad_pooled)
+    (block_out,) = call(block_result, [(tokens.shape, bf16)], tokens, b0, b1, b2, b3, w_out, place, scalars=(6,))
+    (token_grad,) = call(token_result, [(tokens.shape, bf16)], tokens, cotangent, e0, e1, e2, e3,
+        here, later, w_coarse, place, scalars=(9,))
 
     summed = jnp.sum(slab.astype(f32), axis=0).reshape(per, 6 * inner)
     input_grad = summed[:, : 3 * inner]

time: 171 us -> 175 us (1.023)
  waiting for transfers between devices: 57.2 us -> 10.6 us
  starting transfers between devices: 33.4 us -> 62.2 us
  local copies, waits for them, and re-layouts: 11.5 us -> 26.1 us
  blocking collectives: 25.6 us -> 30.1 us
  Pallas kernels: 36.2 us -> 39.3 us
    ppermute x9 -> x11, starting transfers between devices: 16.7 us -> 42.6 us  [passed(): return lax.ppermute(block, ALL, route)]
    ppermute x9 -> x11, waiting for transfers between devices: 23.4 us -> 1.9 us  [passed(): return lax.ppermute(block, ALL, route)]
    all_to_all x1, waiting for transfers between devices: 23.5 us -> 8.71 us  [body(): lax.all_to_all(jnp.concatenate([shared, kv], axis=1), GZ, 0, 0, tiled=True)]
    unnamed x64, local copies, waits for them, and re-layouts: 7.55 us -> 16.7 us
    all_to_all x1, waiting for transfers between devices: 6.3 us -> 0.01 us  [body(): parts = lax.all_to_all(coarse_part, GZ, 0, 0, tiled=True)]
    all_to_all x1, blocking collectives: 25.6 us -> 30.1 us  [body(): packet = lax.all_to_all(packet, ('x', 'y'), 0, 0, tiled=True)]
    all_to_all x1, waiting for transfers between devices: 3.99 us -> 0.01 us  [body(): slab = lax.all_to_all(slab, ('zh', 'zl'), 0, 0, tiled=True)]
    dynamic_slice x2, local copies, waits for them, and re-layouts: 0.64 us -> 4.41 us  [body(): mine = lax.dynamic_index_in_dim(mine, core, axis=6, keepdims=False)]
  transfers between devices with their start and end apart: 13 -> 15, of which waited for: 7 -> 2; matrix products, arithmetic and copies ran while one was open for 5% -> 10% of each run, Pallas kernels for 4% -> 4%
where the time goes in v2:
time: 175 us; the launch traced here: 174 us
  starting transfers between devices  62.2 us (36%)
  Pallas kernels  39.3 us (22%)
  blocking collectives  30.1 us (17%)
  local copies, waits for them, and re-layouts  26.1 us (15%)
  waiting for transfers between devices  10.6 us (6%)
  other arithmetic  4.16 us (2%)
    ppermute x11, starting transfers between devices, passed(): return lax.ppermute(block, ALL, route)  42.6 us
    pallas_call x10, Pallas kernels, call(): pl.pallas_call(kernel, out_shape=[jax.ShapeDtypeStruct(s, d) for s, d in...  39.3 us
    all_to_all x1, blocking collectives, body(): packet = lax.all_to_all(packet, ('x', 'y'), 0, 0, tiled=True)  30.1 us
    unnamed x64, local copies, waits for them, and re-layouts  16.7 us
    all_to_all x1, waiting for transfers between devices, body(): lax.all_to_all(jnp.concatenate([shared, kv], axis=1), GZ, 0, 0, tiled=True)  8.71 us
    all_to_all x1, starting transfers between devices, body(): parts = lax.all_to_all(coarse_part, GZ, 0, 0, tiled=True)  8.15 us
    all_to_all x1, starting transfers between devices, body(): slab = lax.all_to_all(slab, ('zh', 'zl'), 0, 0, tiled=True)  6.93 us
    all_to_all x1, starting transfers between devices, body(): lax.all_to_all(jnp.concatenate([shared, kv], axis=1), GZ, 0, 0, tiled=True)  4.53 us
  transfers between devices with their start and end apart: 15, of which 2 were waited for; matrix products, arithmetic and copies ran while one was open for 10% of the time, Pallas kernels for 4%

profile of v2, /device:TPU:1, one launch (start us, length us, event | category | flops | bytes accessed | tf_op | source)
XLA Modules:
  0.0 173.5 jit_solution(10815504005230389565)
XLA Ops:
  0.6 4.6 %shard_map.101 = (bf16[128,1280]{1,0:T(8,128)(2,1)}, bf16[128,1280]{1,0:T(8,128)(2,1)}, bf16[128,1280]{1,0:T(8,128)(2,1)}, bf16[128,1280]{1,0:T(8,128)(2,1)}, bf16[1,1536]{1,0:T(2,128)(2,1)}) custom-call(bf16[8,8,8,768]{3,2,1,0:T(8,128)(2,1)} %tok_ref.3, bf16[8,8,8,768]{3,2,1,0:T(8,128)(2,1)} %cot_ref.3, bf16[384,768]{1,0:T(8,128)(2,1)} %wo_ref.1, ...), custom_call_target="tpu_custom_call" | custom-call | flops 1 | bytes 1 | tf_op jit(solution)/shard_map/pallas_call | solution.py:31
  5.2 2.1 %collective-permute-start.3 = (bf16[1,1536]{1,0:T(2,128)(2,1)}, bf16[1,1536]{1,0:T(2,128)(2,1)S(1)}, u32[]{:S(2)}, u32[]{:S(2)}) collective-permute-start(bf16[1,1536]{1,0:T(2,128)(2,1)} %get-tuple-element.43), channel_id=1, source_target_pairs={{0,32},{1,33},{2,34},{3,35},{4,36},{5,37},{6,38},{7,39},{8,40},{9,... | collective-permute-start | bytes 9224 | tf_op jit(solution)/shard_map/ppermute | solution.py:352
  9.5 11.8 %collective-permute-start.2 = (bf16[128,1280]{1,0:T(8,128)(2,1)}, bf16[128,1280]{1,0:T(8,128)(2,1)}, u32[]{:S(2)}, u32[]{:S(2)}) collective-permute-start(bf16[128,1280]{1,0:T(8,128)(2,1)} %get-tuple-element.42), channel_id=1, source_target_pairs={{0,63},{1,224},{2,33},{3,226},{4,35},{5,228},{6,37},{7,230},{8,39}... | collective-permute-start | bytes 983048 | tf_op jit(solution)/shard_map/ppermute | solution.py:352
  24.2 4.5 %all-to-all-start = ((bf16[32,2,1152]{2,1,0:T(2,128)(2,1)}), bf16[32,2,1152]{2,1,0:T(2,128)(2,1)}, u32[]{:S(2)}, u32[]{:S(2)}) async-start(bf16[32,2,1152]{2,1,0:T(2,128)(2,1)} %reshape.415), calls=%async_computation | async-start | bytes 294912 | tf_op jit(solution)/shard_map/all_to_all | solution.py:396
  28.7 1.8 %fusion.11.src_ref = s32[768,1]{1,0:T(8,128)S(1)} fusion(s32[]{:T(128)} %axis_index.36), kind=kLoop, calls=%fused_computation.37 | loop fusion | flops 84480 | bytes 3076 | tf_op jit(solution)/shard_map/add | solution.py:411
  32.8 8.7 %all-to-all-done = bf16[32,2,1152]{2,1,0:T(2,128)(2,1)} async-done(((bf16[32,2,1152]{2,1,0:T(2,128)(2,1)}), bf16[32,2,1152]{2,1,0:T(2,128)(2,1)}, u32[]{:S(2)}, u32[]{:S(2)}) %all-to-all-start) | async-done | bytes 147488 | tf_op jit(solution)/shard_map/all_to_all | solution.py:396
  41.5 2.0 %reshape.416 = bf16[32,1,2304]{2,1,0:T(2,128)(2,1)} reshape(bf16[32,2,1152]{2,1,0:T(2,128)(2,1)} %all-to-all-done) | data formatting | bytes 294912
  44.6 10.1 %shard_map.103 = (bf16[128,384]{1,0:T(8,128)(2,1)S(1)}, bf16[128,384]{1,0:T(8,128)(2,1)S(1)}, bf16[128,384]{1,0:T(8,128)(2,1)S(1)}, bf16[128,384]{1,0:T(8,128)(2...) custom-call(bf16[128,1280]{1,0:T(8,128)(2,1)S(1)} %copy-done.6, ...), custom_call_target="tpu_custom_call" | custom-call | flops 1 | bytes 1 | tf_op jit(solution)/shard_map/pallas_call | solution.py:31
  56.6 12.2 %shard_map.105 = (bf16[128,768]{1,0:T(8,128)(2,1)S(1)}, bf16[128,768]{1,0:T(8,128)(2,1)}, bf16[128,768]{1,0:T(8,128)(2,1)S(1)}, bf16[128,768]{1,0:T(8,128)(2,1)S...) custom-call(bf16[128,1280]{1,0:T(8,128)(2,1)S(1)} %copy-done.6, ...), custom_call_target="tpu_custom_call" | custom-call | flops 1 | bytes 1 | tf_op jit(solution)/shard_map/pallas_call | solution.py:31
  72.0 2.4 %collective-permute-start.7 = (bf16[128,768]{1,0:T(8,128)(2,1)}, bf16[128,768]{1,0:T(8,128)(2,1)S(1)}, u32[]{:S(2)}, u32[]{:S(2)}) collective-permute-start(bf16[128,768]{1,0:T(8,128)(2,1)} %get-tuple-element.56), channel_id=1, source_target_pairs={{31,0},{0,1},{1,2},{2,3},{3,4},{4,5},{5,6},{6,7},{7,8},{8,9},{9,10... | collective-permute-start | bytes 589832 | tf_op jit(solution)/shard_map/ppermute | solution.py:352
  75.7 8.2 %all-to-all-start.1 = ((bf16[32,2,768]{2,1,0:T(2,128)(2,1)}), bf16[32,2,768]{2,1,0:T(2,128)(2,1)S(1)}, u32[]{:S(2)}, u32[]{:S(2)}) async-start(bf16[32,2,768]{2,1,0:T(2,128)(2,1)} %reshape.417), calls=%async_computation.1 | async-start | bytes 196608 | tf_op jit(solution)/shard_map/all_to_all | solution.py:432
  83.9 1.7 collective-permute-start.4
  85.6 7.6 %collective-permute-start.6 = (bf16[128,384]{1,0:T(8,128)(2,1)}, bf16[128,384]{1,0:T(8,128)(2,1)S(1)}, u32[]{:S(2)}, u32[]{:S(2)}) collective-permute-start(bf16[128,384]{1,0:T(8,128)(2,1)} %copy-done.23), channel_id=1, source_target_pairs={{63,0},{224,1},{33,2},{226,3},{35,4},{228,5},{37,6},{230,7},{39,8}... | collective-permute-start | bytes 294920 | tf_op jit(solution)/shard_map/ppermute | solution.py:352
  94.0 1.9 %collective-permute-done.6.b2_ref = bf16[128,384]{1,0:T(8,128)(2,1)S(1)} collective-permute-done((bf16[128,384]{1,0:T(8,128)(2,1)}, bf16[128,384]{1,0:T(8,128)(2,1)S(1)}, u32[]{:S(2)}, u32[]{:S(2)}) %collective-permute-start.6) | collective-permute-done | bytes 98336 | tf_op jit(solution)/shard_map/ppermute | solution.py:352
  97.2 5.0 %shard_map.106 = (bf16[384,1536]{1,0:T(8,128)(2,1)S(1)}, bf16[384,1536]{1,0:T(8,128)(2,1)}) custom-call(bf16[128,1280]{1,0:T(8,128)(2,1)S(1)} %copy-done.6, bf16[128,1280]{1,0:T(8,128)(2,1)} %collective-permute-done.up_ref, bf16[128,1280]{1,0:T(8,128)(2,1)} %collective-permute-done.1.side_ref, bf16[128,1280]{1,0:T(8,128)(2,1)} %collective-permute-done.2.both_ref, ...), custom_call_target="tpu_custom_call" | custom-call | flops 1 | bytes 1 | tf_op jit(solution)/shard_map/pallas_call | solution.py:31
  103.2 8.6 %collective-permute-start.10 = (bf16[128,768]{1,0:T(8,128)(2,1)}, bf16[128,768]{1,0:T(8,128)(2,1)}, u32[]{:S(2)}, u32[]{:S(2)}) collective-permute-start(bf16[128,768]{1,0:T(8,128)(2,1)} %copy-done.22), channel_id=1, source_target_pairs={{63,0},{224,1},{33,2},{226,3},{35,4},{228,5},{37,6},{230,7},{39,8}... | collective-permute-start | bytes 589832 | tf_op jit(solution)/shard_map/ppermute | solution.py:352
  113.8 1.9 %constant_dynamic-slice_fusion = bf16[2,2,2,4,4,4,1,3]{7,6,5,4,3,2,1,0:T(2,128)(2,1)} fusion(bf16[2,2,2,4,4,4,2,3]{7,6,5,4,3,2,1,0:T(2,128)(2,1)} %reshape.406, s32[]{:T(128)S(6)} %select_n.164), kind=kLoop, calls=%fused_computation.77 | loop fusion | bytes 6148 | tf_op jit(solution)/shard_map/jit(dynamic_index_in_dim)/dynamic_slice | solution.py:403
  115.7 2.5 %copy.23 = bf16[2,2,2,4,4,4,1,3]{5,4,7,6,3,2,1,0:T(4,128)(2,1)} copy(bf16[2,2,2,4,4,4,1,3]{7,6,5,4,3,2,1,0:T(2,128)(2,1)} %constant_dynamic-slice_fusion) | data formatting | bytes 6144 | tf_op jit(solution)/shard_map/jit(dynamic_index_in_dim)/dynamic_slice | solution.py:403
  118.2 1.6 copy.31
  120.4 30.1 %all_to_all.38.in_ref = bf16[16,32,1536]{2,1,0:T(8,128)(2,1)S(1)} all-to-all(bf16[16,32,1536]{2,1,0:T(8,128)(2,1)S(1)} %shard_map.108), channel_id=1, replica_groups=mesh['zh'=2,'x'=4,'zl'=4,'y'=4,'core'=2] {'x','y'}, dimensions={0} | all-to-all | bytes 3145728 | tf_op jit(solution)/shard_map/all_to_all | solution.py:447
  152.7 6.9 %all-to-all-start.3 = ((bf16[8,2,3456]{2,1,0:T(2,128)(2,1)}), bf16[8,2,3456]{2,1,0:T(2,128)(2,1)}, u32[]{:S(2)}, u32[]{:S(2)}) async-start(bf16[8,2,3456]{2,1,0:T(2,128)(2,1)} %reshape.419), calls=%async_computation.3 | async-start | bytes 221184 | tf_op jit(solution)/shard_map/all_to_all | solution.py:449
  159.6 6.1 %collective-permute-start.11 = (f32[1,768]{1,0:T(1,128)S(1)}, f32[1,768]{1,0:T(1,128)S(1)}, u32[]{:S(2)}, u32[]{:S(2)}) collective-permute-start(f32[1,768]{1,0:T(1,128)S(1)} %get-tuple-element.71), channel_id=1, source_target_pairs={{0,224},{1,225},{2,226},{3,227},{4,228},{5,229},{6,230},{7,231},{8... | collective-permute-start | bytes 9224 | tf_op jit(solution)/shard_map/ppermute | solution.py:352
  165.8 1.6 shard_map.104
  167.4 3.1 %shard_map.109 = bf16[8,8,8,768]{3,2,1,0:T(8,128)(2,1)} custom-call(bf16[8,8,8,768]{3,2,1,0:T(8,128)(2,1)S(1)} %copy-done.2, bf16[8,8,8,768]{3,2,1,0:T(8,128)(2,1)S(1)} %copy-done, bf16[128,768]{1,0:T(8,128)(2,1)S(1)} %copy-done.20, bf16[128,768]{1,0:T(8,128)(2,1)} %collective-permute-done.9.b1_ref, bf16[128,768]{1,0:T(8,128)(2,1)} %collective-permute-done.10.b2_ref, ...), custom_call_target="tpu_custom_call" | custom-call | flops 1 | bytes 1 | tf_op jit(solution)/shard_map/pallas_call | solution.py:31
  (105 shorter events, 25.4 us)
Async XLA Ops:
  5.2 25.3 %copy-start = (bf16[8,8,8,768]{3,2,1,0:T(8,128)(2,1)S(1)}, bf16[8,8,8,768]{3,2,1,0:T(8,128)(2,1)}, u32[]{:S(2)}) copy-start(bf16[8,8,8,768]{3,2,1,0:T(8,128)(2,1)} %cot_ref.3) | copy-start | bytes 2359300
  5.2 16.9 %collective-permute-start.3 = (bf16[1,1536]{1,0:T(2,128)(2,1)}, bf16[1,1536]{1,0:T(2,128)(2,1)S(1)}, u32[]{:S(2)}, u32[]{:S(2)}) collective-permute-start(bf16[1,1536]{1,0:T(2,128)(2,1)} %get-tuple-element.43), channel_id=1, source_target_pairs={{0,32},{1,33},{2,34},{3,35},{4,36},{5,37},{6,38},{7,39},{8,40},{9,... | collective-permute-start | bytes 9224 | tf_op jit(solution)/shard_map/ppermute | solution.py:352
  7.3 37.2 %collective-permute-start = (bf16[128,1280]{1,0:T(8,128)(2,1)}, bf16[128,1280]{1,0:T(8,128)(2,1)}, u32[]{:S(2)}, u32[]{:S(2)}) collective-permute-start(bf16[128,1280]{1,0:T(8,128)(2,1)} %get-tuple-element.40), channel_id=1, source_target_pairs={{0,31},{1,0},{2,1},{3,2},{4,3},{5,4},{6,5},{7,6},{8,7},{9,8},{10,9... | collective-permute-start | bytes 983048 | tf_op jit(solution)/shard_map/ppermute | solution.py:352
  8.6 36.0 %collective-permute-start.1 = (bf16[128,1280]{1,0:T(8,128)(2,1)}, bf16[128,1280]{1,0:T(8,128)(2,1)}, u32[]{:S(2)}, u32[]{:S(2)}) collective-permute-start(bf16[128,1280]{1,0:T(8,128)(2,1)} %get-tuple-element.41), channel_id=1, source_target_pairs={{0,224},{1,33},{2,226},{3,35},{4,228},{5,37},{6,230},{7,39},{8,232... | collective-permute-start | bytes 983048 | tf_op jit(solution)/shard_map/ppermute | solution.py:352
  9.5 35.1 %collective-permute-start.2 = (bf16[128,1280]{1,0:T(8,128)(2,1)}, bf16[128,1280]{1,0:T(8,128)(2,1)}, u32[]{:S(2)}, u32[]{:S(2)}) collective-permute-start(bf16[128,1280]{1,0:T(8,128)(2,1)} %get-tuple-element.42), channel_id=1, source_target_pairs={{0,63},{1,224},{2,33},{3,226},{4,35},{5,228},{6,37},{7,230},{8,39}... | collective-permute-start | bytes 983048 | tf_op jit(solution)/shard_map/ppermute | solution.py:352
  24.2 17.4 %all-to-all-start = ((bf16[32,2,1152]{2,1,0:T(2,128)(2,1)}), bf16[32,2,1152]{2,1,0:T(2,128)(2,1)}, u32[]{:S(2)}, u32[]{:S(2)}) async-start(bf16[32,2,1152]{2,1,0:T(2,128)(2,1)} %reshape.415), calls=%async_computation | async-start | bytes 294912 | tf_op jit(solution)/shard_map/all_to_all | solution.py:396
  30.5 14.1 %copy-start.1 = (bf16[768,1152]{1,0:T(8,128)(2,1)S(1)}, bf16[768,1152]{1,0:T(8,128)(2,1)}, u32[]{:S(2)}) copy-start(bf16[768,1152]{1,0:T(8,128)(2,1)} %wi_ref.3) | copy-start | bytes 5308420
  72.0 23.9 %copy-start.5 = (bf16[768,512]{1,0:T(8,128)(2,1)S(1)}, bf16[768,512]{1,0:T(8,128)(2,1)}, u32[]{:S(2)}) copy-start(bf16[768,512]{1,0:T(8,128)(2,1)} %copy-done.4) | copy-start | bytes 2359300
  72.0 22.0 %collective-permute-start.7 = (bf16[128,768]{1,0:T(8,128)(2,1)}, bf16[128,768]{1,0:T(8,128)(2,1)S(1)}, u32[]{:S(2)}, u32[]{:S(2)}) collective-permute-start(bf16[128,768]{1,0:T(8,128)(2,1)} %get-tuple-element.56), channel_id=1, source_target_pairs={{31,0},{0,1},{1,2},{2,3},{3,4},{4,5},{5,6},{6,7},{7,8},{8,9},{9,10... | collective-permute-start | bytes 589832 | tf_op jit(solution)/shard_map/ppermute | solution.py:352
  75.7 17.5 %all-to-all-start.1 = ((bf16[32,2,768]{2,1,0:T(2,128)(2,1)}), bf16[32,2,768]{2,1,0:T(2,128)(2,1)S(1)}, u32[]{:S(2)}, u32[]{:S(2)}) async-start(bf16[32,2,768]{2,1,0:T(2,128)(2,1)} %reshape.417), calls=%async_computation.1 | async-start | bytes 196608 | tf_op jit(solution)/shard_map/all_to_all | solution.py:432
  83.9 10.1 %collective-permute-start.4 = (bf16[128,384]{1,0:T(8,128)(2,1)}, bf16[128,384]{1,0:T(8,128)(2,1)S(1)}, u32[]{:S(2)}, u32[]{:S(2)}) collective-permute-start(bf16[128,384]{1,0:T(8,128)(2,1)} %copy-done.25), channel_id=1, source_target_pairs={{31,0},{0,1},{1,2},{2,3},{3,4},{4,5},{5,6},{6,7},{7,8},{8,9},{9,10... | collective-permute-start | bytes 294920 | tf_op jit(solution)/shard_map/ppermute | solution.py:352
  85.6 8.4 %collective-permute-start.5 = (bf16[128,384]{1,0:T(8,128)(2,1)}, bf16[128,384]{1,0:T(8,128)(2,1)S(1)}, u32[]{:S(2)}, u32[]{:S(2)}) collective-permute-start(bf16[128,384]{1,0:T(8,128)(2,1)} %copy-done.24), channel_id=1, source_target_pairs={{224,0},{33,1},{226,2},{35,3},{228,4},{37,5},{230,6},{39,7},{232,8... | collective-permute-start | bytes 294920 | tf_op jit(solution)/shard_map/ppermute | solution.py:352
  85.6 10.3 %collective-permute-start.6 = (bf16[128,384]{1,0:T(8,128)(2,1)}, bf16[128,384]{1,0:T(8,128)(2,1)S(1)}, u32[]{:S(2)}, u32[]{:S(2)}) collective-permute-start(bf16[128,384]{1,0:T(8,128)(2,1)} %copy-done.23), channel_id=1, source_target_pairs={{63,0},{224,1},{33,2},{226,3},{35,4},{228,5},{37,6},{230,7},{39,8}... | collective-permute-start | bytes 294920 | tf_op jit(solution)/shard_map/ppermute | solution.py:352
  103.2 16.7 %copy-start.16 = (bf16[32,1,1536]{2,0,1:T(8,128)(2,1)S(1)}, bf16[32,1,1536]{2,0,1:T(8,128)(2,1)}, u32[]{:S(2)}) copy-start(bf16[32,1,1536]{2,0,1:T(8,128)(2,1)} %copy.39) | copy-start | bytes 294916
  103.2 16.8 %copy-start.9 = (bf16[384,1536]{1,0:T(8,128)(2,1)S(1)}, bf16[384,1536]{1,0:T(8,128)(2,1)}, u32[]{:S(2)}) copy-start(bf16[384,1536]{1,0:T(8,128)(2,1)} %copy-done.8) | copy-start | bytes 3538948
  103.2 16.8 %collective-permute-start.8 = (bf16[384,1536]{1,0:T(8,128)(2,1)}, bf16[384,1536]{1,0:T(8,128)(2,1)S(1)}, u32[]{:S(2)}, u32[]{:S(2)}) collective-permute-start(bf16[384,1536]{1,0:T(8,128)(2,1)} %get-tuple-element.60), channel_id=1, source_target_pairs={{0,1},{1,0},{2,3},{3,2},{4,5},{5,4},{6,7},{7,6},{8,9},{9,8},{10,11... | collective-permute-start | bytes 3538952 | tf_op jit(solution)/shard_map/ppermute | solution.py:439
  103.2 17.1 %collective-permute-start.10 = (bf16[128,768]{1,0:T(8,128)(2,1)}, bf16[128,768]{1,0:T(8,128)(2,1)}, u32[]{:S(2)}, u32[]{:S(2)}) collective-permute-start(bf16[128,768]{1,0:T(8,128)(2,1)} %copy-done.22), channel_id=1, source_target_pairs={{63,0},{224,1},{33,2},{226,3},{35,4},{228,5},{37,6},{230,7},{39,8}... | collective-permute-start | bytes 589832 | tf_op jit(solution)/shard_map/ppermute | solution.py:352
  111.9 8.5 %collective-permute-start.9 = (bf16[128,768]{1,0:T(8,128)(2,1)}, bf16[128,768]{1,0:T(8,128)(2,1)}, u32[]{:S(2)}, u32[]{:S(2)}) collective-permute-start(bf16[128,768]{1,0:T(8,128)(2,1)} %copy-done.21), channel_id=1, source_target_pairs={{224,0},{33,1},{226,2},{35,3},{228,4},{37,5},{230,6},{39,7},{232,8... | collective-permute-start | bytes 589832 | tf_op jit(solution)/shard_map/ppermute | solution.py:352
  150.4 15.3 %copy-start.2 = (bf16[8,8,8,768]{3,2,1,0:T(8,128)(2,1)S(1)}, bf16[8,8,8,768]{3,2,1,0:T(8,128)(2,1)}, u32[]{:S(2)}) copy-start(bf16[8,8,8,768]{3,2,1,0:T(8,128)(2,1)} %tok_ref.3) | copy-start | bytes 2359300
  150.4 15.3 %copy-start.7 = (bf16[384,768]{1,0:T(8,128)(2,1)S(1)}, bf16[384,768]{1,0:T(8,128)(2,1)}, u32[]{:S(2)}) copy-start(bf16[384,768]{1,0:T(8,128)(2,1)} %wo_ref.1) | copy-start | bytes 1769476
  150.5 15.3 %copy-start.13 = (bf16[128,384]{1,0:T(8,128)(2,1)S(1)}, bf16[128,384]{1,0:T(8,128)(2,1)}, u32[]{:S(2)}) copy-start(bf16[128,384]{1,0:T(8,128)(2,1)} %copy-done.12) | copy-start | bytes 294916
  150.5 15.3 %copy-start.15 = (bf16[128,384]{1,0:T(8,128)(2,1)S(1)}, bf16[128,384]{1,0:T(8,128)(2,1)}, u32[]{:S(2)}) copy-start(bf16[128,384]{1,0:T(8,128)(2,1)} %copy-done.14) | copy-start | bytes 294916
  152.7 17.8 %all-to-all-start.3 = ((bf16[8,2,3456]{2,1,0:T(2,128)(2,1)}), bf16[8,2,3456]{2,1,0:T(2,128)(2,1)}, u32[]{:S(2)}, u32[]{:S(2)}) async-start(bf16[8,2,3456]{2,1,0:T(2,128)(2,1)} %reshape.419), calls=%async_computation.3 | async-start | bytes 221184 | tf_op jit(solution)/shard_map/all_to_all | solution.py:449
  159.6 7.7 %collective-permute-start.11 = (f32[1,768]{1,0:T(1,128)S(1)}, f32[1,768]{1,0:T(1,128)S(1)}, u32[]{:S(2)}, u32[]{:S(2)}) collective-permute-start(f32[1,768]{1,0:T(1,128)S(1)} %get-tuple-element.71), channel_id=1, source_target_pairs={{0,224},{1,225},{2,226},{3,227},{4,228},{5,229},{6,230},{7,231},{8... | collective-permute-start | bytes 9224 | tf_op jit(solution)/shard_map/ppermute | solution.py:352
  (17 other events, 68.4 us)

commit v3 on v2

--- a/solution.py
+++ b/solution.py
@@ -124,7 +124,7 @@
     coarse_ref[:, d:] = dot(jnp.broadcast_to(pooled, (8, d)), wc_ref[...])[:1].astype(bf16)
 
 
-def turn_cot(cot_ref, src_ref, core_ref, out_ref):
+def turn_cot(cot_ref, src_ref, here_ref, other_ref, core_ref, out_ref, picked_ref):
     d = cot_ref.shape[3]
     parts = []
     for start in halves(core_ref, cot_ref.shape[0]):
@@ -133,6 +133,14 @@
     n = parts[0].shape[0]
     for i, part in enumerate(parts):
         out_ref[:, i * n : (i + 1) * n] = dot_nt(perm, part).astype(bf16)
+    first = core_ref[0, 0] == 0
+    pair = (here_ref[...].astype(f32), other_ref[...].astype(f32))
+    pair = (jnp.where(first, pair[0], pair[1]), jnp.where(first, pair[1], pair[0]))
+    line = lax.broadcasted_iota(jnp.int32, (8, d), 0)
+    rows = jnp.zeros((8, d), f32)
+    for i in range(4):
+        rows = jnp.where(line == 2 + i, pair[i % 2][:, i // 2 * d : (i // 2 + 1) * d], rows)
+    picked_ref[...] = dot_nt(rows.astype(bf16), perm[: d // 2])
 
 
 def picks(src_ref, d):
@@ -153,65 +161,27 @@
     mask_ref[4 * n :] = jnp.zeros((mask_ref.shape[0] - 4 * n, mask_ref.shape[1]), f32)
 
 
-def attend(own_ref, up_ref, side_ref, both_ref, wi_ref, kv_ref,
-           a0_ref, a1_ref, a2_ref, a3_ref, q_ref, k_ref, v_ref, m_ref, l_ref, out_ref, mask_ref):
+def attend(own_ref, up_ref, side_ref, both_ref, wi_ref, kv_ref, r0_ref, r1_ref, r2_ref, r3_ref, grad_ref, coarse_ref,
+           q_ref, k_ref, v_ref, g_ref, att_ref, dk_ref, dv_ref, mask_ref):
     d, width = wi_ref.shape
     inner = width // 3
     n = own_ref.shape[0]
     tokens = 4 * n
-    for i, ref in enumerate((own_ref, up_ref, side_ref, both_ref)):
+    blocks = (own_ref, up_ref, side_ref, both_ref)
+    for i, ref in enumerate(blocks):
         packed = dot(ref[:, :d], wi_ref[...])
         rows = slice(i * n, (i + 1) * n)
         q_ref[rows] = packed[:, :inner].astype(bf16) * bf16(0.125)
         k_ref[rows] = packed[:, inner : 2 * inner].astype(bf16)
         v_ref[rows] = packed[:, 2 * inner :].astype(bf16)
-    hide(mask_ref, (own_ref, up_ref, side_ref, both_ref), d + inner)
+        g_ref[rows] = ref[:, d : d + inner]
+    hide(mask_ref, blocks, d + inner)
     k_ref[tokens:] = kv_ref[:, :inner]
     v_ref[tokens:] = kv_ref[:, inner:]
     eye = jnp.where(
         lax.broadcasted_iota(jnp.int32, (PAIR, PAIR), 0)
         == lax.broadcasted_iota(jnp.int32, (PAIR, PAIR), 1), 1.0, 0.0).astype(bf16)
     chunks = tokens // CHUNK
-    m_ref[...] = jnp.zeros_like(m_ref)
-    l_ref[...] = jnp.zeros_like(l_ref)
-
-    def step(i, _):
-        lanes = pl.ds(pl.multiple_of(i // chunks * PAIR, PAIR), PAIR)
-        rows = pl.ds(pl.multiple_of(i % chunks * CHUNK, CHUNK), CHUNK)
-        keys = k_ref[:, lanes]
-        vals_t = dot_nt(eye, v_ref[:, lanes]).astype(bf16)
-        query = q_ref[rows, lanes]
-        found = []
-        for half in range(2):
-            s = dot_nt(keys, head_of(query, half)) + jnp.concatenate([mask_ref[...]] * 2, axis=1)
-            top = jnp.max(s, axis=0, keepdims=True)
-            e = jnp.exp(s - top)
-            inv = 1.0 / jnp.sum(e, axis=0, keepdims=True)
-            weight = (e * inv).astype(bf16)
-            found.append(dot(vals_t[half * HEAD : (half + 1) * HEAD], weight))
-            m_ref[pl.ds(2 * i + half, 1)] = top
-            l_ref[pl.ds(2 * i + half, 1)] = inv
-        out_ref[rows, lanes] = jnp.concatenate(found, axis=0).T.astype(bf16)
-        return 0
-
-    lax.fori_loop(0, inner // PAIR * chunks, step, 0)
-    for i, ref in enumerate((a0_ref, a1_ref, a2_ref, a3_ref)):
-        ref[...] = out_ref[i * n : (i + 1) * n]
-
-
-def attend_back(own_ref, up_ref, side_ref, both_ref, wi_ref, q_ref, k_ref, v_ref, m_ref, l_ref,
-                d0_ref, d1_ref, d2_ref, d3_ref, grad_ref, coarse_ref, g_ref, dk_ref, dv_ref, mask_ref):
-    d, width = wi_ref.shape
-    inner = width // 3
-    n = own_ref.shape[0]
-    tokens = 4 * n
-    for i, ref in enumerate((own_ref, up_ref, side_ref, both_ref)):
-        g_ref[i * n : (i + 1) * n] = ref[:, d : d + inner]
-    hide(mask_ref, (own_ref, up_ref, side_ref, both_ref), d + inner)
-    eye = jnp.where(
-        lax.broadcasted_iota(jnp.int32, (PAIR, PAIR), 0)
-        == lax.broadcasted_iota(jnp.int32, (PAIR, PAIR), 1), 1.0, 0.0).astype(bf16)
-    chunks = tokens // CHUNK
     dk_ref[...] = jnp.zeros_like(dk_ref)
     dv_ref[...] = jnp.zeros_like(dv_ref)
 
@@ -221,23 +191,30 @@
         keys = k_ref[:, lanes]
         vals = v_ref[:, lanes]
         keys_t = dot_nt(eye, keys).astype(bf16)
+        vals_t = dot_nt(eye, vals).astype(bf16)
+        queries = [head_of(q_ref[rows, lanes], half) for half in range(2)]
+        gs = [head_of(g_ref[rows, lanes], half) for half in range(2)]
         found = []
+        grads = []
         dv = dv_ref[:, lanes]
         dk = dk_ref[:, lanes]
         for half in range(2):
-            query = head_of(q_ref[rows, lanes], half)
-            g = head_of(g_ref[rows, lanes], half)
-            s = dot_nt(keys, query) + jnp.concatenate([mask_ref[...]] * 2, axis=1)
-            prob = jnp.exp(s - m_ref[pl.ds(2 * i + half, 1)]) * l_ref[pl.ds(2 * i + half, 1)]
-            dv += dot(prob.astype(bf16), g)
-            spread = prob * dot_nt(vals, g)
+            part = slice(half * HEAD, (half + 1) * HEAD)
+            s = dot_nt(keys, queries[half]) + jnp.concatenate([mask_ref[...]] * 2, axis=1)
+            e = jnp.exp(s - jnp.max(s, axis=0, keepdims=True))
+            prob = e * (1.0 / jnp.sum(e, axis=0, keepdims=True))
+            weight = prob.astype(bf16)
+            found.append(dot(vals_t[part], weight))
+            dv += dot(weight, gs[half])
+            spread = prob * dot_nt(vals, gs[half])
             centre = jnp.sum(spread, axis=0, keepdims=True)
             score = (spread - prob * centre).astype(bf16)
-            dk += dot(score, query)
-            found.append(dot(keys_t[half * HEAD : (half + 1) * HEAD], score))
+            dk += dot(score, queries[half])
+            grads.append(dot(keys_t[part], score))
         dv_ref[:, lanes] = dv
         dk_ref[:, lanes] = dk
-        grad_ref[rows, lanes] = (jnp.concatenate(found, axis=0).T * 0.125).astype(bf16)
+        att_ref[rows, lanes] = jnp.concatenate(found, axis=0).T.astype(bf16)
+        grad_ref[rows, lanes] = (jnp.concatenate(grads, axis=0).T * 0.125).astype(bf16)
         return 0
 
     lax.fori_loop(0, inner // PAIR * chunks, step, 0)
@@ -250,8 +227,10 @@
     for i in range(2):
         pick = jnp.where(token == chip + i, 1.0, 0.0).astype(bf16)
         coarse_ref[:, i * 2 * inner : (i + 1) * 2 * inner] = dot(pick, part).astype(bf16)
-    for i, ref in enumerate((d0_ref, d1_ref, d2_ref, d3_ref)):
-        ref[...] = dot_nt(grad_ref[i * n : (i + 1) * n], wi_ref[...]).astype(bf16)
+    for i, ref in enumerate((r0_ref, r1_ref, r2_ref, r3_ref)):
+        rows = slice(i * n, (i + 1) * n)
+        ref[:, :d] = dot_nt(grad_ref[rows], wi_ref[...]).astype(bf16)
+        ref[:, d:] = att_ref[rows]
 
 
 def weight_grads(own_ref, up_ref, side_ref, both_ref, src_ref, grad_ref, cot_ref,
@@ -263,16 +242,16 @@
     for i, ref in enumerate((own_ref, up_ref, side_ref, both_ref)):
         turned_ref[:, i * n : (i + 1) * n] = dot_nt(perm, ref[:, :d]).astype(bf16)
     for i, ref in enumerate((b0_ref, b1_ref, b2_ref, b3_ref)):
-        att_ref[i * n : (i + 1) * n] = ref[...]
+        att_ref[i * n : (i + 1) * n] = ref[:, d:]
     for ref, rows in ((keep_ref, slice(0, d // 2)), (send_ref, slice(d // 2, d))):
         ref[:, :width] = dot(turned_ref[rows], grad_ref[...]).astype(bf16)
         ref[:, width:] = dot(cot_ref[rows], att_ref[...]).astype(bf16)
 
 
 def block_result(tok_ref, b0_ref, b1_ref, b2_ref, b3_ref, wo_ref, core_ref, out_ref):
-    x = tok_ref.shape[0]
+    x, _, _, d = tok_ref.shape
     for start, refs in zip(halves(core_ref, x), ((b0_ref, b1_ref), (b2_ref, b3_ref))):
-        branch = [dot(ref[...], wo_ref[...]).astype(bf16).astype(f32) for ref in refs]
+        branch = [dot(ref[:, d:], wo_ref[...]).astype(bf16).astype(f32) for ref in refs]
         total = x_half(tok_ref, start) + join_z(*branch)
         out_ref[pl.ds(start, x // 2)] = total.astype(bf16).reshape(
             (x // 2,) + out_ref.shape[1:])
@@ -293,13 +272,14 @@
     rows -= 8
     line = lax.broadcasted_iota(jnp.int32, (8, width), 0)
     lanes = picked_ref.shape[1]
+    picked = picked_ref[...]
     for i in range(plane):
         part = slice(i * rows, (i + 1) * rows)
         out_ref[i, :rows] = (keep_ref[part].astype(f32) + other_ref[part].astype(f32)).astype(bf16)
         extra = jnp.where(line == 0, pair_ref[0:1], jnp.where(line == 1, pair_ref[1:2], 0.0))
         out_ref[i, rows:] = extra.astype(bf16)
-        seen = jnp.where(line[:, :lanes] == 2, picked_ref[i : i + 1].astype(f32), extra[:, :lanes])
-        out_ref[i, rows:, :lanes] = seen.astype(bf16)
+        mine = pltpu.roll(picked, (lanes - i * rows) % lanes, 1)[:, :128]
+        out_ref[i, rows:, :128] = jnp.where(line[:, :128] < 2, extra[:, :128], mine).astype(bf16)
 
 
 def plane_sums(in_ref, out_ref):
@@ -310,13 +290,13 @@
     total = jnp.sum(in_ref[:, :rows].astype(f32), axis=0)
     extra = in_ref[:, rows:].astype(f32)
     line = lax.broadcasted_iota(jnp.int32, extra.shape, 1)
-    picked = jnp.sum(jnp.where(line == 2, extra, 0.0), axis=1)[:, :512].astype(bf16)
     coarse = jnp.zeros((128, half), f32)
     for i in range(4):
         if i % 2 == 0:
             grads = jnp.sum(jnp.where(line == i // 2, extra, 0.0), axis=1).astype(bf16)
+        picked = jnp.sum(jnp.where(line[:, :, :128] == 2 + i, extra[:, :, :128], 0.0), axis=1).astype(bf16)
         coarse += lax.dot_general(
-            picked[:, i * 128 : (i + 1) * 128], grads[:, i % 2 * half : (i % 2 + 1) * half],
+            picked, grads[:, i % 2 * half : (i % 2 + 1) * half],
             (((0,), (0,)), ((), ())), preferred_element_type=f32)
     step = out_ref.shape[1] // (rows // deep)
     for j in range(rows // deep):
@@ -332,7 +312,7 @@
     pooled = (pooled / float(x * y * z))[None]
     for start, refs in zip(halves(core_ref, x), ((b0_ref, b1_ref), (b2_ref, b3_ref))):
         normed, inv_std = normalize(x_half(tok_ref, start))
-        grad = join_z(*[ref[...].astype(f32) for ref in refs]) + pooled
+        grad = join_z(*[ref[:, :d].astype(f32) for ref in refs]) + pooled
         first = jnp.mean(grad, axis=-1, keepdims=True)
         second = jnp.mean(grad * normed, axis=-1, keepdims=True)
         total = x_half(cot_ref, start) + inv_std * (grad - first - normed * second)
@@ -391,50 +371,38 @@
     up, side, both = passed(up, to_up), passed(side, to_side), passed(both, to_both)
 
     odd = lax.broadcasted_iota(jnp.int32, (coarse, 1), 0) % 2 == 1
-    shared = jnp.broadcast_to(jnp.concatenate([row[:, :d], before[:, :d]], axis=1), (coarse, 2 * d))
     kv = jnp.where(odd, before[:, d:], row[:, d:])
-    far = lax.all_to_all(jnp.concatenate([shared, kv], axis=1), GZ, 0, 0, tiled=True)
-    kv = far[:, 2 * d :]
-
+    shared = jnp.concatenate([row[:, :d], before[:, :d]], axis=1)
+    shared, kv = lax.optimization_barrier((shared, kv))
+    other = lax.ppermute(shared, "core", [(0, 1), (1, 0)])
+    kv = lax.all_to_all(kv, GZ, 0, 0, tiled=True)
     zh, nx, zl, ny, cores = (lax.axis_size(a) for a in ALL)
     plane, deep = nx * ny, zh * zl
-    mine = lax.dynamic_slice_in_dim(far, lax.axis_index(GZ) // cores * cores, cores, axis=0)[:, : 2 * d]
-    mine = mine.reshape(cores, 2, zh, nx, zl, ny, cores, per)
-    mine = lax.dynamic_index_in_dim(mine, core, axis=6, keepdims=False)
-    mine = jnp.transpose(mine, (3, 5, 1, 0, 6, 2, 4)).reshape(plane, 2 * cores, per * deep)
-    picked = jnp.pad(mine, ((0, 0), (0, 0), (0, 128 - per * deep))).reshape(plane, 2 * cores * 128)
 
     row = jnp.arange(d, dtype=jnp.int32)
     half, rest = row // (d // 2), row % (d // 2)
     chip, j, depth = rest // (per * deep), rest % (per * deep) // deep, rest % deep
     device = ((depth // zl * nx + chip // ny) * zl + depth % zl) * ny + chip % ny
     src = ((device * cores + (half + core) % cores) * per + j).reshape(d, 1)
-    (cot_turned,) = call(turn_cot, [((d, size), bf16)], cotangent, src, place, scalars=(2,))
+    cot_turned, picked = call(
+        turn_cot, [((d, size), bf16), ((8, d // 2), f32)], cotangent, src, shared, other, place, scalars=(4,))
     kv, cot_turned = lax.optimization_barrier((kv, cot_turned))
 
-    slim = (n, inner)
-    a0, a1, a2, a3, q, k, v, top, inv = call(
+    tall = (size + coarse, inner)
+    r0, r1, r2, r3, grad, coarse_part = call(
         attend,
-        [(slim, bf16)] * 4
-        + [((size, inner), bf16), ((size + coarse, inner), bf16), ((size + coarse, inner), bf16)]
-        + [((16, CHUNK), f32)] * 2,
+        [((n, d + inner), bf16)] * 4 + [((size, 3 * inner), bf16), ((coarse, 4 * inner), bf16)],
         own, up, side, both, w_in, kv,
-        scratch=[pltpu.VMEM((size, inner), bf16), pltpu.VMEM((size + coarse, 128), f32)])
-    b0, b1, b2, b3 = returned(a0, a1, a2, a3)
-
-    d0, d1, d2, d3, grad, coarse_part = call(
-        attend_back,
-        [((n, d), bf16)] * 4 + [((size, 3 * inner), bf16), ((coarse, 4 * inner), bf16)],
-        own, up, side, both, w_in, q, k, v, top, inv,
-        scratch=[pltpu.VMEM((size, inner), bf16)] + [pltpu.VMEM((size + coarse, inner), f32)] * 2
-        + [pltpu.VMEM((size + coarse, 128), f32)])
-    e0, e1, e2, e3 = returned(d0, d1, d2, d3)
+        grant=24,
+        scratch=[pltpu.VMEM(s, bf16) for s in ((size, inner), tall, tall, (size, inner), (size, inner))]
+        + [pltpu.VMEM(tall, f32)] * 2 + [pltpu.VMEM((size + coarse, 128), f32)])
+    e0, e1, e2, e3 = returned(r0, r1, r2, r3)
     parts = lax.all_to_all(coarse_part, GZ, 0, 0, tiled=True)
 
-    grad, parts, e0 = lax.optimization_barrier((grad, parts, e0))
+    grad, parts, e0, e1, e2 = lax.optimization_barrier((grad, parts, e0, e1, e2))
     keep, send = call(
         weight_grads, [((d // 2, 4 * inner), bf16)] * 2,
-        own, up, side, both, src, grad, cot_turned, b0, b1, b2, b3,
+        own, up, side, both, src, grad, cot_turned, e0, e1, e2, e3,
         scratch=[pltpu.VMEM((d, size), bf16), pltpu.VMEM((size, inner), bf16)])
     other = lax.ppermute(send, "core", [(0, 1), (1, 0)])
     pair, here, there = call(
@@ -443,12 +411,12 @@
 
     (packet,) = call(
         assemble, [((plane, per * deep + 8, 4 * inner), bf16)], keep, other, pair, picked)
-    packet, e0, e1, e2 = lax.optimization_barrier((packet, e0, e1, e2))
+    packet, later = lax.optimization_barrier((packet, later))
     packet = lax.all_to_all(packet, ("x", "y"), 0, 0, tiled=True)
     (slab,) = call(plane_sums, [((deep, per * 6 * inner), bf16)], packet)
     slab = lax.all_to_all(slab, ("zh", "zl"), 0, 0, tiled=True)
 
-    (block_out,) = call(block_result, [(tokens.shape, bf16)], tokens, b0, b1, b2, b3, w_out, place, scalars=(6,))
+    (block_out,) = call(block_result, [(tokens.shape, bf16)], tokens, e0, e1, e2, e3, w_out, place, scalars=(6,))
     (token_grad,) = call(token_result, [(tokens.shape, bf16)], tokens, cotangent, e0, e1, e2, e3,
         here, later, w_coarse, place, scalars=(9,))
 

time: 175 us -> 148 us (0.85)
  starting transfers between devices: 62.2 us -> 39 us
  blocking collectives: 30.1 us -> 45.4 us
  local copies, waits for them, and re-layouts: 26.1 us -> 13.3 us
  Pallas kernels: 39.3 us -> 29.2 us
  waiting for transfers between devices: 10.6 us -> 12.6 us
    all_to_all x0 -> x1, blocking collectives: none -> 18.5 us  [body(): parts = lax.all_to_all(coarse_part, GZ, 0, 0, tiled=True)]
    ppermute x11 -> x8, starting transfers between devices: 42.6 us -> 30.5 us  [passed(): return lax.ppermute(block, ALL, route)]
    pallas_call x10 -> x9, Pallas kernels: 39.3 us -> 29.2 us  [call(): pl.pallas_call(kernel, out_shape=[jax.ShapeDtypeStruct(s, d) for s, d in...]
    all_to_all x2 -> x1, starting transfers between devices: 12.7 us -> 3.62 us  [body(): kv = lax.all_to_all(kv, GZ, 0, 0, tiled=True)]
    unnamed x64 -> x32, local copies, waits for them, and re-layouts: 16.7 us -> 10.3 us
    dynamic_slice x3 -> x0, local copies, waits for them, and re-layouts: 5.15 us -> none  [the longest x2 4.41 us: body(): mine = lax.dynamic_index_in_dim(mine, core, axis=6, keepdims=False)]
    all_to_all x1, waiting for transfers between devices: 0.01 us -> 3.98 us  [body(): slab = lax.all_to_all(slab, ('zh', 'zl'), 0, 0, tiled=True)]
    all_to_all x1, blocking collectives: 30.1 us -> 26.9 us  [body(): packet = lax.all_to_all(packet, ('x', 'y'), 0, 0, tiled=True)]
  transfers between devices with their start and end apart: 15 -> 12, of which waited for: 2 -> 3; matrix products, arithmetic and copies ran while one was open for 10% -> 4% of each run, Pallas kernels for 4% -> 4%
where the time goes in v3:
time: 148 us; the launch traced here: 145 us
  blocking collectives  45.4 us (31%)
  starting transfers between devices  39 us (26%)
  Pallas kernels  29.2 us (20%)
  local copies, waits for them, and re-layouts  13.3 us (9%)
  waiting for transfers between devices  12.6 us (9%)
  other arithmetic  4.73 us (3%)
    ppermute x8, starting transfers between devices, passed(): return lax.ppermute(block, ALL, route)  30.5 us
    pallas_call x9, Pallas kernels, call(): pl.pallas_call(kernel, out_shape=[jax.ShapeDtypeStruct(s, d) for s, d in...  29.2 us
    all_to_all x1, blocking collectives, body(): packet = lax.all_to_all(packet, ('x', 'y'), 0, 0, tiled=True)  26.9 us
    all_to_all x1, blocking collectives, body(): parts = lax.all_to_all(coarse_part, GZ, 0, 0, tiled=True)  18.5 us
    unnamed x32, local copies, waits for them, and re-layouts  10.3 us
    all_to_all x1, waiting for transfers between devices, body(): kv = lax.all_to_all(kv, GZ, 0, 0, tiled=True)  8.23 us
    all_to_all x1, starting transfers between devices, body(): slab = lax.all_to_all(slab, ('zh', 'zl'), 0, 0, tiled=True)  4.17 us
    all_to_all x1, waiting for transfers between devices, body(): slab = lax.all_to_all(slab, ('zh', 'zl'), 0, 0, tiled=True)  3.98 us
  transfers between devices with their start and end apart: 12, of which 3 were waited for; matrix products, arithmetic and copies ran while one was open for 4% of the time, Pallas kernels for 4%

profile of v3, /device:TPU:1, one launch (start us, length us, event | category | flops | bytes accessed | tf_op | source)
XLA Modules:
  0.0 145.2 jit_solution(10821999257046094673)
XLA Ops:
  0.6 4.6 %shard_map.101 = (bf16[128,1280]{1,0:T(8,128)(2,1)}, bf16[128,1280]{1,0:T(8,128)(2,1)}, bf16[128,1280]{1,0:T(8,128)(2,1)}, bf16[128,1280]{1,0:T(8,128)(2,1)}, bf16[1,1536]{1,0:T(2,128)(2,1)}) custom-call(bf16[8,8,8,768]{3,2,1,0:T(8,128)(2,1)} %tok_ref.3, bf16[8,8,8,768]{3,2,1,0:T(8,128)(2,1)} %cot_ref.3, bf16[384,768]{1,0:T(8,128)(2,1)} %wo_ref.1, ...), custom_call_target="tpu_custom_call" | custom-call | flops 1 | bytes 1 | tf_op jit(solution)/shard_map/pallas_call | solution.py:31
  5.2 2.1 %collective-permute-start.3 = (bf16[1,1536]{1,0:T(2,128)(2,1)}, bf16[1,1536]{1,0:T(2,128)(2,1)S(1)}, u32[]{:S(2)}, u32[]{:S(2)}) collective-permute-start(bf16[1,1536]{1,0:T(2,128)(2,1)} %get-tuple-element.38), channel_id=1, source_target_pairs={{0,32},{1,33},{2,34},{3,35},{4,36},{5,37},{6,38},{7,39},{8,40},{9,... | collective-permute-start | bytes 9224 | tf_op jit(solution)/shard_map/ppermute | solution.py:332
  7.3 1.3 collective-permute-start
  9.5 11.8 %collective-permute-start.2 = (bf16[128,1280]{1,0:T(8,128)(2,1)}, bf16[128,1280]{1,0:T(8,128)(2,1)S(1)}, u32[]{:S(2)}, u32[]{:S(2)}) collective-permute-start(bf16[128,1280]{1,0:T(8,128)(2,1)} %get-tuple-element.37), channel_id=1, source_target_pairs={{0,63},{1,224},{2,33},{3,226},{4,35},{5,228},{6,37},{7,230},{8,39}... | collective-permute-start | bytes 983048 | tf_op jit(solution)/shard_map/ppermute | solution.py:332
  24.0 3.6 %all-to-all-start = ((bf16[32,2,384]{2,1,0:T(2,128)(2,1)}), bf16[32,2,384]{2,1,0:T(2,128)(2,1)S(1)}, u32[]{:S(2)}, u32[]{:S(2)}) async-start(bf16[32,2,384]{2,1,0:T(2,128)(2,1)} %reshape.399), calls=%async_computation | async-start | bytes 98304 | tf_op jit(solution)/shard_map/all_to_all | solution.py:378
  27.9 1.8 %fusion.11.src_ref = s32[768,1]{1,0:T(8,128)S(1)} fusion(s32[]{:T(128)} %axis_index.12), kind=kLoop, calls=%fused_computation.37 | loop fusion | flops 84480 | bytes 3076 | tf_op jit(solution)/shard_map/add | solution.py:386
  29.7 1.5 %shard_map.102 = (bf16[768,512]{1,0:T(8,128)(2,1)S(1)}, f32[8,384]{1,0:T(8,128)S(1)}) custom-call(bf16[8,8,8,768]{3,2,1,0:T(8,128)(2,1)S(1)} %copy-done.1, s32[768,1]{1,0:T(8,128)S(1)} %fusion.11.src_ref, bf16[1,1536]{1,0:T(2,128)(2,1)S(1)} %pad_maximum_fusion.here_ref, bf16[1,1536]{1,0:T(2,128)(2,1)S(1)} %collective-permute-done.4.other_ref, ...), custom_call_target="tpu_custom_call" | custom-call | flops 1 | bytes 1 | tf_op jit(solution)/shard_map/pallas_call | solution.py:31
  32.2 8.2 %all-to-all-done = bf16[32,2,384]{2,1,0:T(2,128)(2,1)S(1)} async-done(((bf16[32,2,384]{2,1,0:T(2,128)(2,1)}), bf16[32,2,384]{2,1,0:T(2,128)(2,1)S(1)}, u32[]{:S(2)}, u32[]{:S(2)}) %all-to-all-start) | async-done | bytes 49184 | tf_op jit(solution)/shard_map/all_to_all | solution.py:378
  40.5 1.6 %copy-done.4 = bf16[768,1152]{1,0:T(8,128)(2,1)S(1)} copy-done((bf16[768,1152]{1,0:T(8,128)(2,1)S(1)}, bf16[768,1152]{1,0:T(8,128)(2,1)}, u32[]{:S(2)}) %copy-start.4) | copy-done | bytes 1769496
  42.1 15.2 %shard_map.103 = (bf16[128,1152]{1,0:T(8,128)(2,1)S(1)}, bf16[128,1152]{1,0:T(8,128)(2,1)}, bf16[128,1152]{1,0:T(8,128)(2,1)}, bf16[128,1152]{1,0:T(8,128)(2,1)}...) custom-call(bf16[128,1280]{1,0:T(8,128)(2,1)S(1)} %copy-done.5, ...), custom_call_target="tpu_custom_call" | custom-call | flops 1 | bytes 1 | tf_op jit(solution)/shard_map/pallas_call | solution.py:31
  58.3 1.9 %collective-permute-start.5 = (bf16[128,1152]{1,0:T(8,128)(2,1)}, bf16[128,1152]{1,0:T(8,128)(2,1)S(1)}, u32[]{:S(2)}, u32[]{:S(2)}) collective-permute-start(bf16[128,1152]{1,0:T(8,128)(2,1)} %get-tuple-element.45), channel_id=1, source_target_pairs={{31,0},{0,1},{1,2},{2,3},{3,4},{4,5},{5,6},{6,7},{7,8},{8,9},{9,10... | collective-permute-start | bytes 884744 | tf_op jit(solution)/shard_map/ppermute | solution.py:332
  60.3 7.5 %collective-permute-start.7 = (bf16[128,1152]{1,0:T(8,128)(2,1)}, bf16[128,1152]{1,0:T(8,128)(2,1)S(1)}, u32[]{:S(2)}, u32[]{:S(2)}) collective-permute-start(bf16[128,1152]{1,0:T(8,128)(2,1)} %get-tuple-element.47), channel_id=1, source_target_pairs={{63,0},{224,1},{33,2},{226,3},{35,4},{228,5},{37,6},{230,7},{39,8}... | collective-permute-start | bytes 884744 | tf_op jit(solution)/shard_map/ppermute | solution.py:332
  68.4 18.5 %all_to_all.38 = bf16[32,2,768]{2,1,0:T(2,128)(2,1)} all-to-all(bf16[32,2,768]{2,1,0:T(2,128)(2,1)S(1)} %reshape.401), channel_id=1, replica_groups=mesh['zh'=2,'x'=4,'zl'=4,'y'=4,'core'=2] {'zl','y','core'}, dimensions={0} | all-to-all | bytes 196608 | tf_op jit(solution)/shard_map/all_to_all | solution.py:400
  88.9 1.3 copy-done.9
  90.2 1.1 copy-done.11
  91.3 2.9 %shard_map.106 = (bf16[384,1536]{1,0:T(8,128)(2,1)S(1)}, bf16[384,1536]{1,0:T(8,128)(2,1)S(1)}) custom-call(bf16[128,1280]{1,0:T(8,128)(2,1)S(1)} %copy-done.5, bf16[128,1280]{1,0:T(8,128)(2,1)S(1)} %collective-permute-done.up_ref, bf16[128,1280]{1,0:T(8,128)(2,1)S(1)} %collective-permute-done.1.side_ref, bf16[128,1280]{1,0:T(8,128)(2,1)S(1)} %copy-done.7, ...), custom_call_target="tpu_custom_call" | custom-call | flops 1 | bytes 1 | tf_op jit(solution)/shard_map/pallas_call | solution.py:31
  94.8 5.0 %collective-permute-start.9 = (f32[1,768]{1,0:T(1,128)S(1)}, f32[1,768]{1,0:T(1,128)S(1)}, u32[]{:S(2)}, u32[]{:S(2)}) collective-permute-start(f32[1,768]{1,0:T(1,128)S(1)} %get-tuple-element.60), channel_id=1, source_target_pairs={{0,224},{1,225},{2,226},{3,227},{4,228},{5,229},{6,230},{7,231},{8... | collective-permute-start | bytes 9224 | tf_op jit(solution)/shard_map/ppermute | solution.py:332
  100.5 26.9 %all_to_all.39.in_ref = bf16[16,32,1536]{2,1,0:T(8,128)(2,1)S(1)} all-to-all(bf16[16,32,1536]{2,1,0:T(8,128)(2,1)S(1)} %shard_map.107), channel_id=1, replica_groups=mesh['zh'=2,'x'=4,'zl'=4,'y'=4,'core'=2] {'x','y'}, dimensions={0} | all-to-all | bytes 3145728 | tf_op jit(solution)/shard_map/all_to_all | solution.py:415
  128.3 1.3 reduce.7
  129.6 1.6 %reshape.403 = bf16[8,2,3456]{2,1,0:T(2,128)(2,1)} reshape(bf16[8,6912]{1,0:T(8,128)(2,1)} %reduce.7) | data formatting | bytes 221184
  131.2 4.2 %all-to-all-start.3 = ((bf16[8,2,3456]{2,1,0:T(2,128)(2,1)}), bf16[8,2,3456]{2,1,0:T(2,128)(2,1)S(1)}, u32[]{:S(2)}, u32[]{:S(2)}) async-start(bf16[8,2,3456]{2,1,0:T(2,128)(2,1)} %reshape.403), calls=%async_computation.3 | async-start | bytes 221184 | tf_op jit(solution)/shard_map/all_to_all | solution.py:417
  135.4 1.6 %shard_map.104 = bf16[8,8,8,768]{3,2,1,0:T(8,128)(2,1)} custom-call(bf16[8,8,8,768]{3,2,1,0:T(8,128)(2,1)S(1)} %copy-done, bf16[128,1152]{1,0:T(8,128)(2,1)S(1)} %collective-permute-done.5.b0_ref, bf16[128,1152]{1,0:T(8,128)(2,1)S(1)} %collective-permute-done.6.b1_ref, bf16[128,1152]{1,0:T(8,128)(2,1)S(1)} %collective-permute-done.7.b2_ref, ...), custom_call_target="tpu_custom_call" | custom-call | flops 1 | bytes 1 | tf_op jit(solution)/shard_map/pallas_call | solution.py:31
  137.0 2.1 %shard_map.108 = bf16[8,8,8,768]{3,2,1,0:T(8,128)(2,1)} custom-call(bf16[8,8,8,768]{3,2,1,0:T(8,128)(2,1)S(1)} %copy-done, bf16[8,8,8,768]{3,2,1,0:T(8,128)(2,1)S(1)} %copy-done.1, bf16[128,1152]{1,0:T(8,128)(2,1)S(1)} %collective-permute-done.5.b0_ref, bf16[128,1152]{1,0:T(8,128)(2,1)S(1)} %collective-permute-done.6.b1_ref, ...), custom_call_target="tpu_custom_call" | custom-call | flops 1 | bytes 1 | tf_op jit(solution)/shard_map/pallas_call | solution.py:31
  139.1 4.0 %all-to-all-done.3 = bf16[8,2,3456]{2,1,0:T(2,128)(2,1)S(1)} async-done(((bf16[8,2,3456]{2,1,0:T(2,128)(2,1)}), bf16[8,2,3456]{2,1,0:T(2,128)(2,1)S(1)}, u32[]{:S(2)}, u32[]{:S(2)}) %all-to-all-start.3) | async-done | bytes 110624 | tf_op jit(solution)/shard_map/all_to_all | solution.py:417
  (58 shorter events, 12.8 us)
Async XLA Ops:
  5.2 24.5 %copy-start.1 = (bf16[8,8,8,768]{3,2,1,0:T(8,128)(2,1)S(1)}, bf16[8,8,8,768]{3,2,1,0:T(8,128)(2,1)}, u32[]{:S(2)}) copy-start(bf16[8,8,8,768]{3,2,1,0:T(8,128)(2,1)} %cot_ref.3) | copy-start | bytes 2359300
  5.2 35.3 %copy-start.5 = (bf16[128,1280]{1,0:T(8,128)(2,1)S(1)}, bf16[128,1280]{1,0:T(8,128)(2,1)}, u32[]{:S(2)}) copy-start(bf16[128,1280]{1,0:T(8,128)(2,1)} %get-tuple-element.34.own_ref) | copy-start | bytes 983044
  5.2 16.9 %collective-permute-start.3 = (bf16[1,1536]{1,0:T(2,128)(2,1)}, bf16[1,1536]{1,0:T(2,128)(2,1)S(1)}, u32[]{:S(2)}, u32[]{:S(2)}) collective-permute-start(bf16[1,1536]{1,0:T(2,128)(2,1)} %get-tuple-element.38), channel_id=1, source_target_pairs={{0,32},{1,33},{2,34},{3,35},{4,36},{5,37},{6,38},{7,39},{8,40},{9,... | collective-permute-start | bytes 9224 | tf_op jit(solution)/shard_map/ppermute | solution.py:332
  7.3 33.1 %collective-permute-start = (bf16[128,1280]{1,0:T(8,128)(2,1)}, bf16[128,1280]{1,0:T(8,128)(2,1)S(1)}, u32[]{:S(2)}, u32[]{:S(2)}) collective-permute-start(bf16[128,1280]{1,0:T(8,128)(2,1)} %get-tuple-element.35), channel_id=1, source_target_pairs={{0,31},{1,0},{2,1},{3,2},{4,3},{5,4},{6,5},{7,6},{8,7},{9,8},{10,9... | collective-permute-start | bytes 983048 | tf_op jit(solution)/shard_map/ppermute | solution.py:332
  8.6 31.8 %collective-permute-start.1 = (bf16[128,1280]{1,0:T(8,128)(2,1)}, bf16[128,1280]{1,0:T(8,128)(2,1)S(1)}, u32[]{:S(2)}, u32[]{:S(2)}) collective-permute-start(bf16[128,1280]{1,0:T(8,128)(2,1)} %get-tuple-element.36), channel_id=1, source_target_pairs={{0,224},{1,33},{2,226},{3,35},{4,228},{5,37},{6,230},{7,39},{8,232... | collective-permute-start | bytes 983048 | tf_op jit(solution)/shard_map/ppermute | solution.py:332
  9.5 31.0 %collective-permute-start.2 = (bf16[128,1280]{1,0:T(8,128)(2,1)}, bf16[128,1280]{1,0:T(8,128)(2,1)S(1)}, u32[]{:S(2)}, u32[]{:S(2)}) collective-permute-start(bf16[128,1280]{1,0:T(8,128)(2,1)} %get-tuple-element.37), channel_id=1, source_target_pairs={{0,63},{1,224},{2,33},{3,226},{4,35},{5,228},{6,37},{7,230},{8,39}... | collective-permute-start | bytes 983048 | tf_op jit(solution)/shard_map/ppermute | solution.py:332
  24.0 16.4 %all-to-all-start = ((bf16[32,2,384]{2,1,0:T(2,128)(2,1)}), bf16[32,2,384]{2,1,0:T(2,128)(2,1)S(1)}, u32[]{:S(2)}, u32[]{:S(2)}) async-start(bf16[32,2,384]{2,1,0:T(2,128)(2,1)} %reshape.399), calls=%async_computation | async-start | bytes 98304 | tf_op jit(solution)/shard_map/all_to_all | solution.py:378
  27.7 2.1 %collective-permute-start.4 = (bf16[1,1536]{1,0:T(2,128)(2,1)S(1)}, bf16[1,1536]{1,0:T(2,128)(2,1)S(1)}, u32[]{:S(2)}, u32[]{:S(2)}) collective-permute-start(bf16[1,1536]{1,0:T(2,128)(2,1)S(1)} %pad_maximum_fusion.here_ref), channel_id=1, source_target_pairs={{0,1},{1,0},{2,3},{3,2},{4,5},{5,4},{6,7},{7,6},{8,9},{9,8},{10,11... | collective-permute-start | bytes 9224 | tf_op jit(solution)/shard_map/ppermute | solution.py:377
  31.3 0.9 copy-start.10
  40.5 16.8 %copy-start.6 = (bf16[128,1280]{1,0:T(8,128)(2,1)}, bf16[128,1280]{1,0:T(8,128)(2,1)S(1)}, u32[]{:S(2)}) copy-start(bf16[128,1280]{1,0:T(8,128)(2,1)S(1)} %collective-permute-done.2.both_ref) | copy-start | bytes 983044
  40.5 1.6 %copy-start.4 = (bf16[768,1152]{1,0:T(8,128)(2,1)S(1)}, bf16[768,1152]{1,0:T(8,128)(2,1)}, u32[]{:S(2)}) copy-start(bf16[768,1152]{1,0:T(8,128)(2,1)} %wi_ref.1) | copy-start | bytes 5308420
  57.3 1.0 copy-start.8
  58.3 29.6 %collective-permute-start.5 = (bf16[128,1152]{1,0:T(8,128)(2,1)}, bf16[128,1152]{1,0:T(8,128)(2,1)S(1)}, u32[]{:S(2)}, u32[]{:S(2)}) collective-permute-start(bf16[128,1152]{1,0:T(8,128)(2,1)} %get-tuple-element.45), channel_id=1, source_target_pairs={{31,0},{0,1},{1,2},{2,3},{3,4},{4,5},{5,6},{6,7},{7,8},{8,9},{9,10... | collective-permute-start | bytes 884744 | tf_op jit(solution)/shard_map/ppermute | solution.py:332
  60.3 27.7 %collective-permute-start.6 = (bf16[128,1152]{1,0:T(8,128)(2,1)}, bf16[128,1152]{1,0:T(8,128)(2,1)S(1)}, u32[]{:S(2)}, u32[]{:S(2)}) collective-permute-start(bf16[128,1152]{1,0:T(8,128)(2,1)} %get-tuple-element.46), channel_id=1, source_target_pairs={{224,0},{33,1},{226,2},{35,3},{228,4},{37,5},{230,6},{39,7},{232,8... | collective-permute-start | bytes 884744 | tf_op jit(solution)/shard_map/ppermute | solution.py:332
  60.3 27.7 %collective-permute-start.7 = (bf16[128,1152]{1,0:T(8,128)(2,1)}, bf16[128,1152]{1,0:T(8,128)(2,1)S(1)}, u32[]{:S(2)}, u32[]{:S(2)}) collective-permute-start(bf16[128,1152]{1,0:T(8,128)(2,1)} %get-tuple-element.47), channel_id=1, source_target_pairs={{63,0},{224,1},{33,2},{226,3},{35,4},{228,5},{37,6},{230,7},{39,8}... | collective-permute-start | bytes 884744 | tf_op jit(solution)/shard_map/ppermute | solution.py:332
  88.0 1.0 copy-start.7
  88.9 1.3 copy-start.9
  90.2 1.1 copy-start.11
  94.2 5.5 %collective-permute-start.8 = (bf16[384,1536]{1,0:T(8,128)(2,1)S(1)}, bf16[384,1536]{1,0:T(8,128)(2,1)S(1)}, u32[]{:S(2)}, u32[]{:S(2)}) collective-permute-start(bf16[384,1536]{1,0:T(8,128)(2,1)S(1)} %get-tuple-element.57), channel_id=1, source_target_pairs={{0,1},{1,0},{2,3},{3,2},{4,5},{5,4},{6,7},{7,6},{8,9},{9,8},{10,11... | collective-permute-start | bytes 3538952 | tf_op jit(solution)/shard_map/ppermute | solution.py:407
  94.8 5.7 %collective-permute-start.9 = (f32[1,768]{1,0:T(1,128)S(1)}, f32[1,768]{1,0:T(1,128)S(1)}, u32[]{:S(2)}, u32[]{:S(2)}) collective-permute-start(f32[1,768]{1,0:T(1,128)S(1)} %get-tuple-element.60), channel_id=1, source_target_pairs={{0,224},{1,225},{2,226},{3,227},{4,228},{5,229},{6,230},{7,231},{8... | collective-permute-start | bytes 9224 | tf_op jit(solution)/shard_map/ppermute | solution.py:332
  127.4 8.0 %copy-start = (bf16[8,8,8,768]{3,2,1,0:T(8,128)(2,1)S(1)}, bf16[8,8,8,768]{3,2,1,0:T(8,128)(2,1)}, u32[]{:S(2)}) copy-start(bf16[8,8,8,768]{3,2,1,0:T(8,128)(2,1)} %tok_ref.3) | copy-start | bytes 2359300
  127.4 8.0 %copy-start.3 = (bf16[384,768]{1,0:T(8,128)(2,1)S(1)}, bf16[384,768]{1,0:T(8,128)(2,1)}, u32[]{:S(2)}) copy-start(bf16[384,768]{1,0:T(8,128)(2,1)} %wo_ref.1) | copy-start | bytes 1769476
  131.2 11.9 %all-to-all-start.3 = ((bf16[8,2,3456]{2,1,0:T(2,128)(2,1)}), bf16[8,2,3456]{2,1,0:T(2,128)(2,1)S(1)}, u32[]{:S(2)}, u32[]{:S(2)}) async-start(bf16[8,2,3456]{2,1,0:T(2,128)(2,1)} %reshape.403), calls=%async_computation.3 | async-start | bytes 221184 | tf_op jit(solution)/shard_map/all_to_all | solution.py:417
  135.3 1.6 %copy-start.2 = (bf16[768,768]{1,0:T(8,128)(2,1)S(1)}, bf16[768,768]{1,0:T(8,128)(2,1)}, u32[]{:S(2)}) copy-start(bf16[768,768]{1,0:T(8,128)(2,1)} %wc_ref.1) | copy-start | bytes 3538948

commit v4 on v3

--- a/solution.py
+++ b/solution.py
@@ -10,7 +10,7 @@
 
 HEAD = 64
 PAIR = 2 * HEAD
-CHUNK = 256
+CHUNK = 512
 HIDDEN = -1e30
 GX = ("zh", "x")
 GZ = ("zl", "y", "core")
@@ -161,13 +161,12 @@
     mask_ref[4 * n :] = jnp.zeros((mask_ref.shape[0] - 4 * n, mask_ref.shape[1]), f32)
 
 
-def attend(own_ref, up_ref, side_ref, both_ref, wi_ref, kv_ref, r0_ref, r1_ref, r2_ref, r3_ref, grad_ref, coarse_ref,
-           q_ref, k_ref, v_ref, g_ref, att_ref, dk_ref, dv_ref, mask_ref):
+def project(own_ref, up_ref, side_ref, both_ref, wi_ref, src_ref, q_ref, k_ref, v_ref, g_ref, mask_ref, turned_ref):
     d, width = wi_ref.shape
     inner = width // 3
     n = own_ref.shape[0]
-    tokens = 4 * n
     blocks = (own_ref, up_ref, side_ref, both_ref)
+    perm = picks(src_ref, d)
     for i, ref in enumerate(blocks):
         packed = dot(ref[:, :d], wi_ref[...])
         rows = slice(i * n, (i + 1) * n)
@@ -175,7 +174,18 @@
         k_ref[rows] = packed[:, inner : 2 * inner].astype(bf16)
         v_ref[rows] = packed[:, 2 * inner :].astype(bf16)
         g_ref[rows] = ref[:, d : d + inner]
+        turned_ref[:, rows] = dot_nt(perm, ref[:, :d]).astype(bf16)
     hide(mask_ref, blocks, d + inner)
+
+
+def attend(q_ref, kw_ref, vw_ref, g_ref, mask_ref, wi_ref, kv_ref, r0_ref, r1_ref, r2_ref, r3_ref, grad_ref, coarse_ref,
+           k_ref, v_ref, att_ref, dk_ref, dv_ref):
+    d, width = wi_ref.shape
+    inner = width // 3
+    tokens = q_ref.shape[0]
+    n = tokens // 4
+    k_ref[:tokens] = kw_ref[...]
+    v_ref[:tokens] = vw_ref[...]
     k_ref[tokens:] = kv_ref[:, :inner]
     v_ref[tokens:] = kv_ref[:, inner:]
     eye = jnp.where(
@@ -200,7 +210,7 @@
         dk = dk_ref[:, lanes]
         for half in range(2):
             part = slice(half * HEAD, (half + 1) * HEAD)
-            s = dot_nt(keys, queries[half]) + jnp.concatenate([mask_ref[...]] * 2, axis=1)
+            s = dot_nt(keys, queries[half]) + jnp.concatenate([mask_ref[...]] * (CHUNK // 128), axis=1)
             e = jnp.exp(s - jnp.max(s, axis=0, keepdims=True))
             prob = e * (1.0 / jnp.sum(e, axis=0, keepdims=True))
             weight = prob.astype(bf16)
@@ -233,14 +243,10 @@
         ref[:, d:] = att_ref[rows]
 
 
-def weight_grads(own_ref, up_ref, side_ref, both_ref, src_ref, grad_ref, cot_ref,
-                 b0_ref, b1_ref, b2_ref, b3_ref, keep_ref, send_ref, turned_ref, att_ref):
-    d = src_ref.shape[0]
-    n = own_ref.shape[0]
+def weight_grads(turned_ref, grad_ref, cot_ref, b0_ref, b1_ref, b2_ref, b3_ref, keep_ref, send_ref, att_ref):
+    d = turned_ref.shape[0]
+    n = b0_ref.shape[0]
     width = grad_ref.shape[1]
-    perm = picks(src_ref, d)
-    for i, ref in enumerate((own_ref, up_ref, side_ref, both_ref)):
-        turned_ref[:, i * n : (i + 1) * n] = dot_nt(perm, ref[:, :d]).astype(bf16)
     for i, ref in enumerate((b0_ref, b1_ref, b2_ref, b3_ref)):
         att_ref[i * n : (i + 1) * n] = ref[:, d:]
     for ref, rows in ((keep_ref, slice(0, d // 2)), (send_ref, slice(d // 2, d))):
@@ -267,42 +273,71 @@
         ref[...] = jnp.where(core_ref[0, 0] == 0, total[:, :d], total[:, d:])
 
 
-def assemble(keep_ref, other_ref, pair_ref, picked_ref, out_ref):
+def assemble(keep_ref, other_ref, pair_ref, picked_ref, out_ref, pair_rows):
     plane, rows, width = out_ref.shape
-    rows -= 8
-    line = lax.broadcasted_iota(jnp.int32, (8, width), 0)
+    width -= 256
     lanes = picked_ref.shape[1]
+    per_row = width // 128
+    for i in range(rows):
+        at = i % per_row * 128
+        pair_rows[i : i + 1] = pair_ref[i // per_row : i // per_row + 1, at : at + 128]
+    pairs = pair_rows[...]
     picked = picked_ref[...]
+    empty = jnp.zeros((rows - 8, 128), f32)
     for i in range(plane):
         part = slice(i * rows, (i + 1) * rows)
-        out_ref[i, :rows] = (keep_ref[part].astype(f32) + other_ref[part].astype(f32)).astype(bf16)
-        extra = jnp.where(line == 0, pair_ref[0:1], jnp.where(line == 1, pair_ref[1:2], 0.0))
-        out_ref[i, rows:] = extra.astype(bf16)
+        out_ref[i, :, :width] = (keep_ref[part].astype(f32) + other_ref[part].astype(f32)).astype(bf16)
         mine = pltpu.roll(picked, (lanes - i * rows) % lanes, 1)[:, :128]
-        out_ref[i, rows:, :128] = jnp.where(line[:, :128] < 2, extra[:, :128], mine).astype(bf16)
-
-
-def plane_sums(in_ref, out_ref):
+        beside = jnp.concatenate([pairs, jnp.concatenate([mine, empty], axis=0)], axis=1)
+        out_ref[i, :, width:] = beside.astype(bf16)
+
+
+def place_of(tile, tiles):
+    return tile // tiles, tile % tiles * 128
+
+
+def plane_sums(in_ref, out_ref, flat_ref):
     plane, rows, width = in_ref.shape
-    rows -= 8
-    deep = out_ref.shape[0]
+    width -= 256
+    deep, lines, lanes = out_ref.shape
     half = width // 2
-    total = jnp.sum(in_ref[:, :rows].astype(f32), axis=0)
-    extra = in_ref[:, rows:].astype(f32)
-    line = lax.broadcasted_iota(jnp.int32, extra.shape, 1)
+    total = jnp.sum(in_ref[:, :, :width].astype(f32), axis=0)
+    pairs = in_ref[:, :, width : width + 128].astype(f32)
+    picked = in_ref[:, :8, width + 128 :].astype(f32)
+    line = lax.broadcasted_iota(jnp.int32, picked.shape, 1)
+
+    def row(block, i):
+        return jnp.sum(jnp.where(line == i, block, 0.0), axis=1).astype(bf16)
+
     coarse = jnp.zeros((128, half), f32)
+    tiles = half // 128
     for i in range(4):
-        if i % 2 == 0:
-            grads = jnp.sum(jnp.where(line == i // 2, extra, 0.0), axis=1).astype(bf16)
-        picked = jnp.sum(jnp.where(line[:, :, :128] == 2 + i, extra[:, :, :128], 0.0), axis=1).astype(bf16)
+        grads = [row(pairs[:, q // 8 * 8 : q // 8 * 8 + 8], q % 8) for q in range(i * tiles, (i + 1) * tiles)]
         coarse += lax.dot_general(
-            picked, grads[:, i % 2 * half : (i % 2 + 1) * half],
+            row(picked, 2 + i), jnp.concatenate(grads, axis=1),
             (((0,), (0,)), ((), ())), preferred_element_type=f32)
-    step = out_ref.shape[1] // (rows // deep)
+    flat_ref[...] = jnp.zeros_like(flat_ref)
+    tile = 0
     for j in range(rows // deep):
         part = slice(j * deep, (j + 1) * deep)
-        out_ref[:, j * step : j * step + width] = total[part].astype(bf16)
-        out_ref[:, j * step + width : (j + 1) * step] = coarse[part].astype(bf16)
+        for block in (total[part], coarse[part]):
+            for at in range(0, block.shape[1], 128):
+                r, lane = place_of(tile, lanes // 128)
+                flat_ref[lane // 128, pl.ds(r, deep, stride=lines), :] = block[:, at : at + 128]
+                tile += 1
+    for i in range(lanes // 128):
+        out_ref[:, :, i * 128 : (i + 1) * 128] = flat_ref[i].reshape(deep, lines, 128).astype(bf16)
+
+
+def depth_sums(in_ref, *outs):
+    total = jnp.sum(in_ref[...].astype(f32), axis=0)
+    tile = 0
+    for j in range(outs[0].shape[0]):
+        for ref in outs:
+            for at in range(0, ref.shape[1], 128):
+                r, lane = place_of(tile, total.shape[1] // 128)
+                ref[j : j + 1, at : at + 128] = total[r : r + 1, lane : lane + 128]
+                tile += 1
 
 
 def token_result(tok_ref, cot_ref, b0_ref, b1_ref, b2_ref, b3_ref, here_ref, next_ref, wc_ref, core_ref, out_ref):
@@ -388,42 +423,44 @@
         turn_cot, [((d, size), bf16), ((8, d // 2), f32)], cotangent, src, shared, other, place, scalars=(4,))
     kv, cot_turned = lax.optimization_barrier((kv, cot_turned))
 
-    tall = (size + coarse, inner)
+    flat, tall = (size, inner), (size + coarse, inner)
+    q, k, v, g, mask, win_turned = call(
+        project, [(flat, bf16)] * 4 + [((size + coarse, 128), f32), ((d, size), bf16)],
+        own, up, side, both, w_in, src)
     r0, r1, r2, r3, grad, coarse_part = call(
         attend,
         [((n, d + inner), bf16)] * 4 + [((size, 3 * inner), bf16), ((coarse, 4 * inner), bf16)],
-        own, up, side, both, w_in, kv,
+        q, k, v, g, mask, w_in, kv,
         grant=24,
-        scratch=[pltpu.VMEM(s, bf16) for s in ((size, inner), tall, tall, (size, inner), (size, inner))]
-        + [pltpu.VMEM(tall, f32)] * 2 + [pltpu.VMEM((size + coarse, 128), f32)])
+        scratch=[pltpu.VMEM(s, bf16) for s in (tall, tall, flat)] + [pltpu.VMEM(tall, f32)] * 2)
     e0, e1, e2, e3 = returned(r0, r1, r2, r3)
     parts = lax.all_to_all(coarse_part, GZ, 0, 0, tiled=True)
 
     grad, parts, e0, e1, e2 = lax.optimization_barrier((grad, parts, e0, e1, e2))
     keep, send = call(
         weight_grads, [((d // 2, 4 * inner), bf16)] * 2,
-        own, up, side, both, src, grad, cot_turned, e0, e1, e2, e3,
-        scratch=[pltpu.VMEM((d, size), bf16), pltpu.VMEM((size, inner), bf16)])
+        win_turned, grad, cot_turned, e0, e1, e2, e3, scratch=[pltpu.VMEM((size, inner), bf16)])
     other = lax.ppermute(send, "core", [(0, 1), (1, 0)])
     pair, here, there = call(
         coarse_total, [((2, 4 * inner), f32), ((1, d), f32), ((1, d), f32)], parts, place, scalars=(1,))
     later = passed(there, lambda a, c: (a - 1, c))
 
     (packet,) = call(
-        assemble, [((plane, per * deep + 8, 4 * inner), bf16)], keep, other, pair, picked)
-    packet, later = lax.optimization_barrier((packet, later))
+        assemble, [((plane, per * deep, 4 * inner + 256), bf16)], keep, other, pair, picked,
+        scratch=[pltpu.VMEM((per * deep, 128), f32)])
     packet = lax.all_to_all(packet, ("x", "y"), 0, 0, tiled=True)
-    (slab,) = call(plane_sums, [((deep, per * 6 * inner), bf16)], packet)
+    tiles = -(-per * 6 * inner // 1024)
+    (slab,) = call(
+        plane_sums, [((deep, 8, tiles * 128), bf16)], packet, scratch=[pltpu.VMEM((tiles, deep * 8, 128), f32)])
     slab = lax.all_to_all(slab, ("zh", "zl"), 0, 0, tiled=True)
 
     (block_out,) = call(block_result, [(tokens.shape, bf16)], tokens, e0, e1, e2, e3, w_out, place, scalars=(6,))
     (token_grad,) = call(token_result, [(tokens.shape, bf16)], tokens, cotangent, e0, e1, e2, e3,
         here, later, w_coarse, place, scalars=(9,))
 
-    summed = jnp.sum(slab.astype(f32), axis=0).reshape(per, 6 * inner)
-    input_grad = summed[:, : 3 * inner]
-    output_grad = summed[:, 3 * inner : 4 * inner].T
-    coarse_grad = summed[:, 4 * inner :]
+    input_grad, output_grad, coarse_grad = call(
+        depth_sums, [((per, 3 * inner), f32), ((per, inner), f32), ((per, 2 * inner), f32)], slab)
+    output_grad = output_grad.T
     return (block_out, token_grad, input_grad, output_grad, coarse_grad)
 
 

time: 148 us -> 136 us (0.919)
  local copies, waits for them, and re-layouts: 13.3 us -> 7.32 us
  blocking collectives: 45.4 us -> 41.7 us
  waiting for transfers between devices: 12.6 us -> 10.5 us
  starting transfers between devices: 39 us -> 40.6 us
  other arithmetic: 4.73 us -> 3.18 us
    unnamed x32 -> x38, local copies, waits for them, and re-layouts: 10.3 us -> 6.06 us
    all_to_all x1, waiting for transfers between devices: 3.98 us -> 0.01 us  [body(): slab = lax.all_to_all(slab, ('zh', 'zl'), 0, 0, tiled=True)]
    all_to_all x1, blocking collectives: 26.9 us -> 23.5 us  [body(): packet = lax.all_to_all(packet, ('x', 'y'), 0, 0, tiled=True)]
    ppermute x1, waiting for transfers between devices: 0.01 us -> 2.37 us  [body(): other = lax.ppermute(send, 'core', [(0, 1), (1, 0)])]
    pallas_call x9 -> x11, Pallas kernels: 29.2 us -> 29.4 us  [call(): pl.pallas_call(kernel, out_shape=[jax.ShapeDtypeStruct(s, d) for s, d in...]
  transfers between devices with their start and end apart: 12 -> 12, of which waited for: 3 -> 2; matrix products, arithmetic and copies ran while one was open for 4% -> 4% of each run, Pallas kernels for 4% -> 4%
where the time goes in v4:
time: 136 us; the launch traced here: 134 us
  blocking collectives  41.7 us (31%)
  starting transfers between devices  40.6 us (30%)
  Pallas kernels  29.4 us (22%)
  waiting for transfers between devices  10.5 us (8%)
  local copies, waits for them, and re-layouts  7.32 us (5%)
  other arithmetic  3.18 us (2%)
    ppermute x8, starting transfers between devices, passed(): return lax.ppermute(block, ALL, route)  31.9 us
    pallas_call x11, Pallas kernels, call(): pl.pallas_call(kernel, out_shape=[jax.ShapeDtypeStruct(s, d) for s, d in...  29.4 us
    all_to_all x1, blocking collectives, body(): packet = lax.all_to_all(packet, ('x', 'y'), 0, 0, tiled=True)  23.5 us
    all_to_all x1, blocking collectives, body(): parts = lax.all_to_all(coarse_part, GZ, 0, 0, tiled=True)  18.2 us
    all_to_all x1, waiting for transfers between devices, body(): kv = lax.all_to_all(kv, GZ, 0, 0, tiled=True)  8.09 us
    unnamed x38, local copies, waits for them, and re-layouts  6.06 us
    all_to_all x1, starting transfers between devices, body(): slab = lax.all_to_all(slab, ('zh', 'zl'), 0, 0, tiled=True)  4.22 us
    all_to_all x1, starting transfers between devices, body(): kv = lax.all_to_all(kv, GZ, 0, 0, tiled=True)  4 us
  transfers between devices with their start and end apart: 12, of which 2 were waited for; matrix products, arithmetic and copies ran while one was open for 4% of the time, Pallas kernels for 4%

profile of v4, /device:TPU:1, one launch (start us, length us, event | category | flops | bytes accessed | tf_op | source)
XLA Modules:
  0.0 133.7 jit_solution(2946087546916605600)
XLA Ops:
  0.6 4.6 %shard_map.101 = (bf16[128,1280]{1,0:T(8,128)(2,1)}, bf16[128,1280]{1,0:T(8,128)(2,1)}, bf16[128,1280]{1,0:T(8,128)(2,1)}, bf16[128,1280]{1,0:T(8,128)(2,1)}, bf16[1,1536]{1,0:T(2,128)(2,1)}) custom-call(bf16[8,8,8,768]{3,2,1,0:T(8,128)(2,1)} %tok_ref.3, bf16[8,8,8,768]{3,2,1,0:T(8,128)(2,1)} %cot_ref.3, bf16[384,768]{1,0:T(8,128)(2,1)} %wo_ref.1, ...), custom_call_target="tpu_custom_call" | custom-call | flops 1 | bytes 1 | tf_op jit(solution)/shard_map/pallas_call | solution.py:31
  5.3 2.1 %collective-permute-start.3 = (bf16[1,1536]{1,0:T(2,128)(2,1)}, bf16[1,1536]{1,0:T(2,128)(2,1)S(1)}, u32[]{:S(2)}, u32[]{:S(2)}) collective-permute-start(bf16[1,1536]{1,0:T(2,128)(2,1)} %get-tuple-element.50), channel_id=1, source_target_pairs={{0,32},{1,33},{2,34},{3,35},{4,36},{5,37},{6,38},{7,39},{8,40},{9,... | collective-permute-start | bytes 9224 | tf_op jit(solution)/shard_map/ppermute | solution.py:367
  7.4 1.3 collective-permute-start
  9.6 11.8 %collective-permute-start.2 = (bf16[128,1280]{1,0:T(8,128)(2,1)}, bf16[128,1280]{1,0:T(8,128)(2,1)}, u32[]{:S(2)}, u32[]{:S(2)}) collective-permute-start(bf16[128,1280]{1,0:T(8,128)(2,1)} %get-tuple-element.44), channel_id=1, source_target_pairs={{0,63},{1,224},{2,33},{3,226},{4,35},{5,228},{6,37},{7,230},{8,39}... | collective-permute-start | bytes 983048 | tf_op jit(solution)/shard_map/ppermute | solution.py:367
  24.2 4.0 %all-to-all-start = ((bf16[32,2,384]{2,1,0:T(2,128)(2,1)}), bf16[32,2,384]{2,1,0:T(2,128)(2,1)S(1)}, u32[]{:S(2)}, u32[]{:S(2)}) async-start(bf16[32,2,384]{2,1,0:T(2,128)(2,1)} %reshape.392), calls=%async_computation | async-start | bytes 98304 | tf_op jit(solution)/shard_map/all_to_all | solution.py:413
  28.2 1.8 %fusion.11.src_ref = s32[768,1]{1,0:T(8,128)S(1)} fusion(s32[]{:T(128)} %axis_index.12), kind=kLoop, calls=%fused_computation.37 | loop fusion | flops 84480 | bytes 3076 | tf_op jit(solution)/shard_map/add | solution.py:421
  30.0 1.5 %shard_map.103 = (bf16[768,512]{1,0:T(8,128)(2,1)S(1)}, f32[8,384]{1,0:T(8,128)S(1)}) custom-call(bf16[8,8,8,768]{3,2,1,0:T(8,128)(2,1)S(1)} %copy-done.2, s32[768,1]{1,0:T(8,128)S(1)} %fusion.11.src_ref, bf16[1,1536]{1,0:T(2,128)(2,1)S(1)} %pad_maximum_fusion.here_ref, bf16[1,1536]{1,0:T(2,128)(2,1)S(1)} %collective-permute-done.4.other_ref, ...), custom_call_target="tpu_custom_call" | custom-call | flops 1 | bytes 1 | tf_op jit(solution)/shard_map/pallas_call | solution.py:31
  32.4 8.1 %all-to-all-done = bf16[32,2,384]{2,1,0:T(2,128)(2,1)S(1)} async-done(((bf16[32,2,384]{2,1,0:T(2,128)(2,1)}), bf16[32,2,384]{2,1,0:T(2,128)(2,1)S(1)}, u32[]{:S(2)}, u32[]{:S(2)}) %all-to-all-start) | async-done | bytes 49184 | tf_op jit(solution)/shard_map/all_to_all | solution.py:413
  40.6 3.6 %shard_map.102 = (bf16[512,384]{1,0:T(8,128)(2,1)S(1)}, bf16[512,384]{1,0:T(8,128)(2,1)S(1)}, bf16[512,384]{1,0:T(8,128)(2,1)S(1)}, bf16[512,384]{1,0:T(8,128)(2...) custom-call(bf16[128,1280]{1,0:T(8,128)(2,1)S(1)} %copy-done.11, ...), custom_call_target="tpu_custom_call" | custom-call | flops 1 | bytes 1 | tf_op jit(solution)/shard_map/pallas_call | solution.py:31
  45.2 11.8 %shard_map.104 = (bf16[128,1152]{1,0:T(8,128)(2,1)S(1)}, bf16[128,1152]{1,0:T(8,128)(2,1)}, bf16[128,1152]{1,0:T(8,128)(2,1)}, bf16[128,1152]{1,0:T(8,128)(2,1)S...) custom-call(bf16[512,384]{1,0:T(8,128)(2,1)S(1)} %get-tuple-element.45.q_ref, ...), custom_call_target="tpu_custom_call" | custom-call | flops 1 | bytes 1 | tf_op jit(solution)/shard_map/pallas_call | solution.py:31
  56.9 1.0 copy-done.5
  58.0 1.9 %collective-permute-start.5 = (bf16[128,1152]{1,0:T(8,128)(2,1)}, bf16[128,1152]{1,0:T(8,128)(2,1)S(1)}, u32[]{:S(2)}, u32[]{:S(2)}) collective-permute-start(bf16[128,1152]{1,0:T(8,128)(2,1)} %get-tuple-element.57), channel_id=1, source_target_pairs={{31,0},{0,1},{1,2},{2,3},{3,4},{4,5},{5,6},{6,7},{7,8},{8,9},{9,10... | collective-permute-start | bytes 884744 | tf_op jit(solution)/shard_map/ppermute | solution.py:367
  59.9 7.5 %collective-permute-start.7 = (bf16[128,1152]{1,0:T(8,128)(2,1)S(1)}, bf16[128,1152]{1,0:T(8,128)(2,1)S(1)}, u32[]{:S(2)}, u32[]{:S(2)}) collective-permute-start(bf16[128,1152]{1,0:T(8,128)(2,1)S(1)} %get-tuple-element.59), channel_id=1, source_target_pairs={{63,0},{224,1},{33,2},{226,3},{35,4},{228,5},{37,6},{230,7},{39,8}... | collective-permute-start | bytes 884744 | tf_op jit(solution)/shard_map/ppermute | solution.py:367
  68.1 18.2 %all_to_all.34 = bf16[32,2,768]{2,1,0:T(2,128)(2,1)S(1)} all-to-all(bf16[32,2,768]{2,1,0:T(2,128)(2,1)S(1)} %reshape.394), channel_id=1, replica_groups=mesh['zh'=2,'x'=4,'zl'=4,'y'=4,'core'=2] {'zl','y','core'}, dimensions={0} | all-to-all | bytes 196608 | tf_op jit(solution)/shard_map/all_to_all | solution.py:437
  86.4 1.3 copy-done.6
  87.7 1.1 copy-done.10
  88.8 1.6 %shard_map.108 = (bf16[384,1536]{1,0:T(8,128)(2,1)S(1)}, bf16[384,1536]{1,0:T(8,128)(2,1)S(1)}) custom-call(bf16[768,512]{1,0:T(8,128)(2,1)S(1)} %copy-done.10, bf16[512,1152]{1,0:T(8,128)(2,1)S(1)} %copy-done.6, bf16[768,512]{1,0:T(8,128)(2,1)S(1)} %copy-done.8, bf16[128,1152]{1,0:T(8,128)(2,1)S(1)} %collective-permute-done.5.b0_ref, ...), custom_call_target="tpu_custom_call" | custom-call | flops 1 | bytes 1 | tf_op jit(solution)/shard_map/pallas_call | solution.py:31
  91.0 2.4 %collective-permute-done.9.other_ref = bf16[384,1536]{1,0:T(8,128)(2,1)S(1)} collective-permute-done((bf16[384,1536]{1,0:T(8,128)(2,1)S(1)}, bf16[384,1536]{1,0:T(8,128)(2,1)S(1)}, u32[]{:S(2)}, u32[]{:S(2)}) %collective-permute-start.9) | collective-permute-done | bytes 1179680 | tf_op jit(solution)/shard_map/ppermute | solution.py:443
  93.7 23.5 %all_to_all.35.in_ref = bf16[16,24,1792]{2,1,0:T(8,128)(2,1)S(1)} all-to-all(bf16[16,24,1792]{2,1,0:T(8,128)(2,1)S(1)} %shard_map.109), channel_id=1, replica_groups=mesh['zh'=2,'x'=4,'zl'=4,'y'=4,'core'=2] {'x','y'}, dimensions={0} | all-to-all | bytes 2752512 | tf_op jit(solution)/shard_map/all_to_all | solution.py:451
  117.2 1.5 %shard_map.110 = bf16[8,8,896]{2,1,0:T(8,128)(2,1)} custom-call(bf16[16,24,1792]{2,1,0:T(8,128)(2,1)S(1)} %all_to_all.35.in_ref), custom_call_target="tpu_custom_call" | custom-call | flops 1 | bytes 1 | tf_op jit(solution)/shard_map/pallas_call | solution.py:31
  118.7 4.2 %all-to-all-start.3 = ((bf16[8,8,896]{2,1,0:T(8,128)(2,1)}), bf16[8,8,896]{2,1,0:T(8,128)(2,1)S(1)}, u32[]{:S(2)}, u32[]{:S(2)}) async-start(bf16[8,8,896]{2,1,0:T(8,128)(2,1)} %shard_map.110), calls=%async_computation.3 | async-start | bytes 229376 | tf_op jit(solution)/shard_map/all_to_all | solution.py:455
  123.0 6.4 %collective-permute-start.8 = (f32[1,768]{1,0:T(1,128)S(1)}, f32[1,768]{1,0:T(1,128)S(1)}, u32[]{:S(2)}, u32[]{:S(2)}) collective-permute-start(f32[1,768]{1,0:T(1,128)S(1)} %copy-done.15), channel_id=1, source_target_pairs={{0,224},{1,225},{2,226},{3,227},{4,228},{5,229},{6,230},{7,231},{8... | collective-permute-start | bytes 9224 | tf_op jit(solution)/shard_map/ppermute | solution.py:367
  129.4 1.6 %shard_map.105 = bf16[8,8,8,768]{3,2,1,0:T(8,128)(2,1)} custom-call(bf16[8,8,8,768]{3,2,1,0:T(8,128)(2,1)S(1)} %copy-done.1, bf16[128,1152]{1,0:T(8,128)(2,1)S(1)} %collective-permute-done.5.b0_ref, bf16[128,1152]{1,0:T(8,128)(2,1)S(1)} %collective-permute-done.6.b1_ref, bf16[128,1152]{1,0:T(8,128)(2,1)S(1)} %collective-permute-done.7.b2_ref, ...), custom_call_target="tpu_custom_call" | custom-call | flops 1 | bytes 1 | tf_op jit(solution)/shard_map/pallas_call | solution.py:31
  130.9 2.1 %shard_map.107 = bf16[8,8,8,768]{3,2,1,0:T(8,128)(2,1)} custom-call(bf16[8,8,8,768]{3,2,1,0:T(8,128)(2,1)S(1)} %copy-done.1, bf16[8,8,8,768]{3,2,1,0:T(8,128)(2,1)S(1)} %copy-done.2, bf16[128,1152]{1,0:T(8,128)(2,1)S(1)} %collective-permute-done.5.b0_ref, bf16[128,1152]{1,0:T(8,128)(2,1)S(1)} %collective-permute-done.6.b1_ref, ...), custom_call_target="tpu_custom_call" | custom-call | flops 1 | bytes 1 | tf_op jit(solution)/shard_map/pallas_call | solution.py:31
  (60 shorter events, 7.8 us)
Async XLA Ops:
  0.6 29.3 %copy-start.2 = (bf16[8,8,8,768]{3,2,1,0:T(8,128)(2,1)S(1)}, bf16[8,8,8,768]{3,2,1,0:T(8,128)(2,1)}, u32[]{:S(2)}) copy-start(bf16[8,8,8,768]{3,2,1,0:T(8,128)(2,1)} %cot_ref.3) | copy-start | bytes 2359300
  5.3 35.3 %copy-start = (bf16[768,1152]{1,0:T(8,128)(2,1)S(1)}, bf16[768,1152]{1,0:T(8,128)(2,1)}, u32[]{:S(2)}) copy-start(bf16[768,1152]{1,0:T(8,128)(2,1)} %wi_ref.3) | copy-start | bytes 5308420
  5.3 35.3 %copy-start.11 = (bf16[128,1280]{1,0:T(8,128)(2,1)S(1)}, bf16[128,1280]{1,0:T(8,128)(2,1)}, u32[]{:S(2)}) copy-start(bf16[128,1280]{1,0:T(8,128)(2,1)} %get-tuple-element.41.own_ref) | copy-start | bytes 983044
  5.3 16.9 %collective-permute-start.3 = (bf16[1,1536]{1,0:T(2,128)(2,1)}, bf16[1,1536]{1,0:T(2,128)(2,1)S(1)}, u32[]{:S(2)}, u32[]{:S(2)}) collective-permute-start(bf16[1,1536]{1,0:T(2,128)(2,1)} %get-tuple-element.50), channel_id=1, source_target_pairs={{0,32},{1,33},{2,34},{3,35},{4,36},{5,37},{6,38},{7,39},{8,40},{9,... | collective-permute-start | bytes 9224 | tf_op jit(solution)/shard_map/ppermute | solution.py:367
  7.4 33.1 %collective-permute-start = (bf16[128,1280]{1,0:T(8,128)(2,1)}, bf16[128,1280]{1,0:T(8,128)(2,1)}, u32[]{:S(2)}, u32[]{:S(2)}) collective-permute-start(bf16[128,1280]{1,0:T(8,128)(2,1)} %get-tuple-element.42), channel_id=1, source_target_pairs={{0,31},{1,0},{2,1},{3,2},{4,3},{5,4},{6,5},{7,6},{8,7},{9,8},{10,9... | collective-permute-start | bytes 983048 | tf_op jit(solution)/shard_map/ppermute | solution.py:367
  8.7 31.9 %collective-permute-start.1 = (bf16[128,1280]{1,0:T(8,128)(2,1)}, bf16[128,1280]{1,0:T(8,128)(2,1)}, u32[]{:S(2)}, u32[]{:S(2)}) collective-permute-start(bf16[128,1280]{1,0:T(8,128)(2,1)} %get-tuple-element.43), channel_id=1, source_target_pairs={{0,224},{1,33},{2,226},{3,35},{4,228},{5,37},{6,230},{7,39},{8,232... | collective-permute-start | bytes 983048 | tf_op jit(solution)/shard_map/ppermute | solution.py:367
  9.6 31.0 %collective-permute-start.2 = (bf16[128,1280]{1,0:T(8,128)(2,1)}, bf16[128,1280]{1,0:T(8,128)(2,1)}, u32[]{:S(2)}, u32[]{:S(2)}) collective-permute-start(bf16[128,1280]{1,0:T(8,128)(2,1)} %get-tuple-element.44), channel_id=1, source_target_pairs={{0,63},{1,224},{2,33},{3,226},{4,35},{5,228},{6,37},{7,230},{8,39}... | collective-permute-start | bytes 983048 | tf_op jit(solution)/shard_map/ppermute | solution.py:367
  22.3 7.6 %collective-permute-start.4 = (bf16[1,1536]{1,0:T(2,128)(2,1)S(1)}, bf16[1,1536]{1,0:T(2,128)(2,1)S(1)}, u32[]{:S(2)}, u32[]{:S(2)}) collective-permute-start(bf16[1,1536]{1,0:T(2,128)(2,1)S(1)} %pad_maximum_fusion.here_ref), channel_id=1, source_target_pairs={{0,1},{1,0},{2,3},{3,2},{4,5},{5,4},{6,7},{7,6},{8,9},{9,8},{10,11... | collective-permute-start | bytes 9224 | tf_op jit(solution)/shard_map/ppermute | solution.py:412
  24.2 16.3 %all-to-all-start = ((bf16[32,2,384]{2,1,0:T(2,128)(2,1)}), bf16[32,2,384]{2,1,0:T(2,128)(2,1)S(1)}, u32[]{:S(2)}, u32[]{:S(2)}) async-start(bf16[32,2,384]{2,1,0:T(2,128)(2,1)} %reshape.392), calls=%async_computation | async-start | bytes 98304 | tf_op jit(solution)/shard_map/all_to_all | solution.py:413
  58.0 28.4 %copy-start.8 = (bf16[768,512]{1,0:T(8,128)(2,1)S(1)}, bf16[768,512]{1,0:T(8,128)(2,1)}, u32[]{:S(2)}) copy-start(bf16[768,512]{1,0:T(8,128)(2,1)} %copy-done.7) | copy-start | bytes 2359300
  58.0 28.4 %collective-permute-start.5 = (bf16[128,1152]{1,0:T(8,128)(2,1)}, bf16[128,1152]{1,0:T(8,128)(2,1)S(1)}, u32[]{:S(2)}, u32[]{:S(2)}) collective-permute-start(bf16[128,1152]{1,0:T(8,128)(2,1)} %get-tuple-element.57), channel_id=1, source_target_pairs={{31,0},{0,1},{1,2},{2,3},{3,4},{4,5},{5,6},{6,7},{7,8},{8,9},{9,10... | collective-permute-start | bytes 884744 | tf_op jit(solution)/shard_map/ppermute | solution.py:367
  59.9 26.5 %collective-permute-start.6 = (bf16[128,1152]{1,0:T(8,128)(2,1)}, bf16[128,1152]{1,0:T(8,128)(2,1)S(1)}, u32[]{:S(2)}, u32[]{:S(2)}) collective-permute-start(bf16[128,1152]{1,0:T(8,128)(2,1)} %get-tuple-element.58), channel_id=1, source_target_pairs={{224,0},{33,1},{226,2},{35,3},{228,4},{37,5},{230,6},{39,7},{232,8... | collective-permute-start | bytes 884744 | tf_op jit(solution)/shard_map/ppermute | solution.py:367
  59.9 26.5 %collective-permute-start.7 = (bf16[128,1152]{1,0:T(8,128)(2,1)S(1)}, bf16[128,1152]{1,0:T(8,128)(2,1)S(1)}, u32[]{:S(2)}, u32[]{:S(2)}) collective-permute-start(bf16[128,1152]{1,0:T(8,128)(2,1)S(1)} %get-tuple-element.59), channel_id=1, source_target_pairs={{63,0},{224,1},{33,2},{226,3},{35,4},{228,5},{37,6},{230,7},{39,8}... | collective-permute-start | bytes 884744 | tf_op jit(solution)/shard_map/ppermute | solution.py:367
  86.4 1.3 copy-start.6
  90.4 3.0 %collective-permute-start.9 = (bf16[384,1536]{1,0:T(8,128)(2,1)S(1)}, bf16[384,1536]{1,0:T(8,128)(2,1)S(1)}, u32[]{:S(2)}, u32[]{:S(2)}) collective-permute-start(bf16[384,1536]{1,0:T(8,128)(2,1)S(1)} %get-tuple-element.71), channel_id=1, source_target_pairs={{0,1},{1,0},{2,3},{3,2},{4,5},{5,4},{6,7},{7,6},{8,9},{9,8},{10,11... | collective-permute-start | bytes 3538952 | tf_op jit(solution)/shard_map/ppermute | solution.py:443
  91.0 2.4 %copy-start.12 = (f32[1,768]{1,0:T(1,128)}, f32[1,768]{1,0:T(1,128)S(1)}, u32[]{:S(2)}) copy-start(f32[1,768]{1,0:T(1,128)S(1)} %get-tuple-element.65.here_ref) | copy-start | bytes 9220
  91.0 2.7 %copy-start.14 = (f32[1,768]{1,0:T(1,128)}, f32[1,768]{1,0:T(1,128)S(1)}, u32[]{:S(2)}) copy-start(f32[1,768]{1,0:T(1,128)S(1)} %get-tuple-element.66) | copy-start | bytes 9220
  117.2 5.8 %copy-start.15 = (f32[1,768]{1,0:T(1,128)S(1)}, f32[1,768]{1,0:T(1,128)}, u32[]{:S(2)}) copy-start(f32[1,768]{1,0:T(1,128)} %copy-done.14) | copy-start | bytes 9220
  117.2 12.2 %copy-start.1 = (bf16[8,8,8,768]{3,2,1,0:T(8,128)(2,1)S(1)}, bf16[8,8,8,768]{3,2,1,0:T(8,128)(2,1)}, u32[]{:S(2)}) copy-start(bf16[8,8,8,768]{3,2,1,0:T(8,128)(2,1)} %tok_ref.3) | copy-start | bytes 2359300
  117.2 12.2 %copy-start.4 = (bf16[384,768]{1,0:T(8,128)(2,1)S(1)}, bf16[384,768]{1,0:T(8,128)(2,1)}, u32[]{:S(2)}) copy-start(bf16[384,768]{1,0:T(8,128)(2,1)} %wo_ref.1) | copy-start | bytes 1769476
  118.7 14.3 %all-to-all-start.3 = ((bf16[8,8,896]{2,1,0:T(8,128)(2,1)}), bf16[8,8,896]{2,1,0:T(8,128)(2,1)S(1)}, u32[]{:S(2)}, u32[]{:S(2)}) async-start(bf16[8,8,896]{2,1,0:T(8,128)(2,1)} %shard_map.110), calls=%async_computation.3 | async-start | bytes 229376 | tf_op jit(solution)/shard_map/all_to_all | solution.py:455
  123.0 8.0 %copy-start.3 = (bf16[768,768]{1,0:T(8,128)(2,1)S(1)}, bf16[768,768]{1,0:T(8,128)(2,1)}, u32[]{:S(2)}) copy-start(bf16[768,768]{1,0:T(8,128)(2,1)} %wc_ref.1) | copy-start | bytes 3538948
  123.0 8.0 %copy-start.13 = (f32[1,768]{1,0:T(1,128)S(1)}, f32[1,768]{1,0:T(1,128)}, u32[]{:S(2)}) copy-start(f32[1,768]{1,0:T(1,128)} %copy-done.12) | copy-start | bytes 9220
  123.0 8.0 %collective-permute-start.8 = (f32[1,768]{1,0:T(1,128)S(1)}, f32[1,768]{1,0:T(1,128)S(1)}, u32[]{:S(2)}, u32[]{:S(2)}) collective-permute-start(f32[1,768]{1,0:T(1,128)S(1)} %copy-done.15), channel_id=1, source_target_pairs={{0,224},{1,225},{2,226},{3,227},{4,228},{5,229},{6,230},{7,231},{8... | collective-permute-start | bytes 9224 | tf_op jit(solution)/shard_map/ppermute | solution.py:367
  (4 other events, 3.9 us)

commit v5 on v4

--- a/solution.py
+++ b/solution.py
@@ -178,8 +178,9 @@
     hide(mask_ref, blocks, d + inner)
 
 
-def attend(q_ref, kw_ref, vw_ref, g_ref, mask_ref, wi_ref, kv_ref, r0_ref, r1_ref, r2_ref, r3_ref, grad_ref, coarse_ref,
-           k_ref, v_ref, att_ref, dk_ref, dv_ref):
+def attend(q_ref, kw_ref, vw_ref, g_ref, mask_ref, wi_ref, kv_ref, turned_ref,
+           r0_ref, r1_ref, r2_ref, r3_ref, keep_ref, send_ref, coarse_ref,
+           k_ref, v_ref, att_ref, grad_ref, dk_ref, dv_ref):
     d, width = wi_ref.shape
     inner = width // 3
     tokens = q_ref.shape[0]
@@ -241,17 +242,17 @@
         rows = slice(i * n, (i + 1) * n)
         ref[:, :d] = dot_nt(grad_ref[rows], wi_ref[...]).astype(bf16)
         ref[:, d:] = att_ref[rows]
-
-
-def weight_grads(turned_ref, grad_ref, cot_ref, b0_ref, b1_ref, b2_ref, b3_ref, keep_ref, send_ref, att_ref):
-    d = turned_ref.shape[0]
+    for ref, rows in ((keep_ref, slice(0, d // 2)), (send_ref, slice(d // 2, d))):
+        ref[...] = dot(turned_ref[rows], grad_ref[...]).astype(bf16)
+
+
+def output_grads(cot_ref, b0_ref, b1_ref, b2_ref, b3_ref, keep_ref, send_ref, att_ref):
+    d = cot_ref.shape[0]
     n = b0_ref.shape[0]
-    width = grad_ref.shape[1]
     for i, ref in enumerate((b0_ref, b1_ref, b2_ref, b3_ref)):
         att_ref[i * n : (i + 1) * n] = ref[:, d:]
     for ref, rows in ((keep_ref, slice(0, d // 2)), (send_ref, slice(d // 2, d))):
-        ref[:, :width] = dot(turned_ref[rows], grad_ref[...]).astype(bf16)
-        ref[:, width:] = dot(cot_ref[rows], att_ref[...]).astype(bf16)
+        ref[...] = dot(cot_ref[rows], att_ref[...]).astype(bf16)
 
 
 def block_result(tok_ref, b0_ref, b1_ref, b2_ref, b3_ref, wo_ref, core_ref, out_ref):
@@ -273,7 +274,7 @@
         ref[...] = jnp.where(core_ref[0, 0] == 0, total[:, :d], total[:, d:])
 
 
-def assemble(keep_ref, other_ref, pair_ref, picked_ref, out_ref, pair_rows):
+def assemble(keep_ref, other_ref, out_keep_ref, out_other_ref, pair_ref, picked_ref, out_ref, pair_rows):
     plane, rows, width = out_ref.shape
     width -= 256
     lanes = picked_ref.shape[1]
@@ -286,7 +287,9 @@
     empty = jnp.zeros((rows - 8, 128), f32)
     for i in range(plane):
         part = slice(i * rows, (i + 1) * rows)
-        out_ref[i, :, :width] = (keep_ref[part].astype(f32) + other_ref[part].astype(f32)).astype(bf16)
+        split = keep_ref.shape[1]
+        out_ref[i, :, :split] = (keep_ref[part].astype(f32) + other_ref[part].astype(f32)).astype(bf16)
+        out_ref[i, :, split:width] = (out_keep_ref[part].astype(f32) + out_other_ref[part].astype(f32)).astype(bf16)
         mine = pltpu.roll(picked, (lanes - i * rows) % lanes, 1)[:, :128]
         beside = jnp.concatenate([pairs, jnp.concatenate([mine, empty], axis=0)], axis=1)
         out_ref[i, :, width:] = beside.astype(bf16)
@@ -427,36 +430,38 @@
     q, k, v, g, mask, win_turned = call(
         project, [(flat, bf16)] * 4 + [((size + coarse, 128), f32), ((d, size), bf16)],
         own, up, side, both, w_in, src)
-    r0, r1, r2, r3, grad, coarse_part = call(
+    r0, r1, r2, r3, keep, send, coarse_part = call(
         attend,
-        [((n, d + inner), bf16)] * 4 + [((size, 3 * inner), bf16), ((coarse, 4 * inner), bf16)],
-        q, k, v, g, mask, w_in, kv,
-        grant=24,
-        scratch=[pltpu.VMEM(s, bf16) for s in (tall, tall, flat)] + [pltpu.VMEM(tall, f32)] * 2)
+        [((n, d + inner), bf16)] * 4 + [((d // 2, 3 * inner), bf16)] * 2 + [((coarse, 4 * inner), bf16)],
+        q, k, v, g, mask, w_in, kv, win_turned,
+        grant=16,
+        scratch=[pltpu.VMEM(s, bf16) for s in (tall, tall, flat, (size, 3 * inner))] + [pltpu.VMEM(tall, f32)] * 2)
     e0, e1, e2, e3 = returned(r0, r1, r2, r3)
     parts = lax.all_to_all(coarse_part, GZ, 0, 0, tiled=True)
 
-    grad, parts, e0, e1, e2 = lax.optimization_barrier((grad, parts, e0, e1, e2))
-    keep, send = call(
-        weight_grads, [((d // 2, 4 * inner), bf16)] * 2,
-        win_turned, grad, cot_turned, e0, e1, e2, e3, scratch=[pltpu.VMEM((size, inner), bf16)])
-    other = lax.ppermute(send, "core", [(0, 1), (1, 0)])
+    swap = [(0, 1), (1, 0)]
+    other = lax.ppermute(send, "core", swap)
+    cot_turned, parts, other, e0, e1, e2 = lax.optimization_barrier((cot_turned, parts, other, e0, e1, e2))
+    out_keep, out_send = call(
+        output_grads, [((d // 2, inner), bf16)] * 2,
+        cot_turned, e0, e1, e2, e3, scratch=[pltpu.VMEM((size, inner), bf16)])
+    out_other = lax.ppermute(out_send, "core", swap)
     pair, here, there = call(
         coarse_total, [((2, 4 * inner), f32), ((1, d), f32), ((1, d), f32)], parts, place, scalars=(1,))
     later = passed(there, lambda a, c: (a - 1, c))
 
     (packet,) = call(
-        assemble, [((plane, per * deep, 4 * inner + 256), bf16)], keep, other, pair, picked,
+        assemble, [((plane, per * deep, 4 * inner + 256), bf16)], keep, other, out_keep, out_other, pair, picked,
         scratch=[pltpu.VMEM((per * deep, 128), f32)])
     packet = lax.all_to_all(packet, ("x", "y"), 0, 0, tiled=True)
+    (block_out,) = call(block_result, [(tokens.shape, bf16)], tokens, e0, e1, e2, e3, w_out, place, scalars=(6,))
+    (token_grad,) = call(token_result, [(tokens.shape, bf16)], tokens, cotangent, e0, e1, e2, e3,
+        here, later, w_coarse, place, scalars=(9,))
+    packet, block_out, token_grad = lax.optimization_barrier((packet, block_out, token_grad))
     tiles = -(-per * 6 * inner // 1024)
     (slab,) = call(
         plane_sums, [((deep, 8, tiles * 128), bf16)], packet, scratch=[pltpu.VMEM((tiles, deep * 8, 128), f32)])
     slab = lax.all_to_all(slab, ("zh", "zl"), 0, 0, tiled=True)
-
-    (block_out,) = call(block_result, [(tokens.shape, bf16)], tokens, e0, e1, e2, e3, w_out, place, scalars=(6,))
-    (token_grad,) = call(token_result, [(tokens.shape, bf16)], tokens, cotangent, e0, e1, e2, e3,
-        here, later, w_coarse, place, scalars=(9,))
 
     input_grad, output_grad, coarse_grad = call(
         depth_sums, [((per, 3 * inner), f32), ((per, inner), f32), ((per, 2 * inner), f32)], slab)

time: 136 us -> 133 us (0.978)
  blocking collectives: 41.7 us -> 31 us
  waiting for transfers between devices: 10.5 us -> 15.9 us
  Pallas kernels: 29.4 us -> 31.4 us
  local copies, waits for them, and re-layouts: 7.32 us -> 8.91 us
    all_to_all x1, blocking collectives: 23.5 us -> 13.1 us  [body(): slab = lax.all_to_all(slab, ('zh', 'zl'), 0, 0, tiled=True)]
    ppermute x8, waiting for transfers between devices: 0.02 us -> 6.67 us  [passed(): return lax.ppermute(block, ALL, route)]
    pallas_call x11, Pallas kernels: 29.4 us -> 31.4 us  [call(): pl.pallas_call(kernel, out_shape=[jax.ShapeDtypeStruct(s, d) for s, d in...]
    ppermute x1 -> x2, waiting for transfers between devices: 2.37 us -> 0.55 us  [the longest x1 0.55 us: body(): out_other = lax.ppermute(out_send, 'core', swap)]
    unnamed x38 -> x42, local copies, waits for them, and re-layouts: 6.06 us -> 7.65 us
    ppermute x8, starting transfers between devices: 31.9 us -> 30.4 us  [passed(): return lax.ppermute(block, ALL, route)]
  transfers between devices with their start and end apart: 12 -> 13, of which waited for: 2 -> 4; matrix products, arithmetic and copies ran while one was open for 4% -> 4% of each run, Pallas kernels for 4% -> 4%
where the time goes in v5:
time: 133 us; the launch traced here: 131 us
  starting transfers between devices  40 us (30%)
  Pallas kernels  31.4 us (24%)
  blocking collectives  31 us (23%)
  waiting for transfers between devices  15.9 us (12%)
  local copies, waits for them, and re-layouts  8.91 us (7%)
  other arithmetic  3.18 us (2%)
    pallas_call x11, Pallas kernels, call(): pl.pallas_call(kernel, out_shape=[jax.ShapeDtypeStruct(s, d) for s, d in...  31.4 us
    ppermute x8, starting transfers between devices, passed(): return lax.ppermute(block, ALL, route)  30.4 us
    all_to_all x1, blocking collectives, body(): parts = lax.all_to_all(coarse_part, GZ, 0, 0, tiled=True)  17.9 us
    all_to_all x1, blocking collectives, body(): slab = lax.all_to_all(slab, ('zh', 'zl'), 0, 0, tiled=True)  13.1 us
    all_to_all x1, waiting for transfers between devices, body(): kv = lax.all_to_all(kv, GZ, 0, 0, tiled=True)  8.27 us
    unnamed x42, local copies, waits for them, and re-layouts  7.65 us
    ppermute x8, waiting for transfers between devices, passed(): return lax.ppermute(block, ALL, route)  6.67 us
    all_to_all x1, starting transfers between devices, body(): packet = lax.all_to_all(packet, ('x', 'y'), 0, 0, tiled=True)  4.28 us
  transfers between devices with their start and end apart: 13, of which 4 were waited for; matrix products, arithmetic and copies ran while one was open for 4% of the time, Pallas kernels for 4%

profile of v5, /device:TPU:1, one launch (start us, length us, event | category | flops | bytes accessed | tf_op | source)
XLA Modules:
  0.0 131.3 jit_solution(14824814491956662105)
XLA Ops:
  0.6 4.6 %shard_map.101 = (bf16[128,1280]{1,0:T(8,128)(2,1)}, bf16[128,1280]{1,0:T(8,128)(2,1)}, bf16[128,1280]{1,0:T(8,128)(2,1)}, bf16[128,1280]{1,0:T(8,128)(2,1)}, bf16[1,1536]{1,0:T(2,128)(2,1)}) custom-call(bf16[8,8,8,768]{3,2,1,0:T(8,128)(2,1)} %tok_ref.3, bf16[8,8,8,768]{3,2,1,0:T(8,128)(2,1)} %cot_ref.3, bf16[384,768]{1,0:T(8,128)(2,1)} %wo_ref.1, ...), custom_call_target="tpu_custom_call" | custom-call | flops 1 | bytes 1 | tf_op jit(solution)/shard_map/pallas_call | solution.py:31
  5.3 2.1 %collective-permute-start.3 = (bf16[1,1536]{1,0:T(2,128)(2,1)}, bf16[1,1536]{1,0:T(2,128)(2,1)S(1)}, u32[]{:S(2)}, u32[]{:S(2)}) collective-permute-start(bf16[1,1536]{1,0:T(2,128)(2,1)} %get-tuple-element.55), channel_id=1, source_target_pairs={{0,32},{1,33},{2,34},{3,35},{4,36},{5,37},{6,38},{7,39},{8,40},{9,... | collective-permute-start | bytes 9224 | tf_op jit(solution)/shard_map/ppermute | solution.py:370
  7.4 1.3 collective-permute-start
  9.6 11.9 %collective-permute-start.2 = (bf16[128,1280]{1,0:T(8,128)(2,1)}, bf16[128,1280]{1,0:T(8,128)(2,1)}, u32[]{:S(2)}, u32[]{:S(2)}) collective-permute-start(bf16[128,1280]{1,0:T(8,128)(2,1)} %get-tuple-element.49), channel_id=1, source_target_pairs={{0,63},{1,224},{2,33},{3,226},{4,35},{5,228},{6,37},{7,230},{8,39}... | collective-permute-start | bytes 983048 | tf_op jit(solution)/shard_map/ppermute | solution.py:370
  24.1 3.6 %all-to-all-start = ((bf16[32,2,384]{2,1,0:T(2,128)(2,1)}), bf16[32,2,384]{2,1,0:T(2,128)(2,1)S(1)}, u32[]{:S(2)}, u32[]{:S(2)}) async-start(bf16[32,2,384]{2,1,0:T(2,128)(2,1)} %reshape.392), calls=%async_computation | async-start | bytes 98304 | tf_op jit(solution)/shard_map/all_to_all | solution.py:416
  28.0 1.8 %fusion.11.src_ref = s32[768,1]{1,0:T(8,128)S(1)} fusion(s32[]{:T(128)} %axis_index.12), kind=kLoop, calls=%fused_computation.37 | loop fusion | flops 84480 | bytes 3076 | tf_op jit(solution)/shard_map/add | solution.py:424
  29.8 1.5 %shard_map.103 = (bf16[768,512]{1,0:T(8,128)(2,1)S(1)}, f32[8,384]{1,0:T(8,128)S(1)}) custom-call(bf16[8,8,8,768]{3,2,1,0:T(8,128)(2,1)S(1)} %copy-done.2, s32[768,1]{1,0:T(8,128)S(1)} %fusion.11.src_ref, bf16[1,1536]{1,0:T(2,128)(2,1)S(1)} %pad_maximum_fusion.here_ref, bf16[1,1536]{1,0:T(2,128)(2,1)S(1)} %collective-permute-done.4.other_ref, ...), custom_call_target="tpu_custom_call" | custom-call | flops 1 | bytes 1 | tf_op jit(solution)/shard_map/pallas_call | solution.py:31
  32.2 8.3 %all-to-all-done = bf16[32,2,384]{2,1,0:T(2,128)(2,1)S(1)} async-done(((bf16[32,2,384]{2,1,0:T(2,128)(2,1)}), bf16[32,2,384]{2,1,0:T(2,128)(2,1)S(1)}, u32[]{:S(2)}, u32[]{:S(2)}) %all-to-all-start) | async-done | bytes 49184 | tf_op jit(solution)/shard_map/all_to_all | solution.py:416
  40.6 3.6 %shard_map.102 = (bf16[512,384]{1,0:T(8,128)(2,1)S(1)}, bf16[512,384]{1,0:T(8,128)(2,1)S(1)}, bf16[512,384]{1,0:T(8,128)(2,1)S(1)}, bf16[512,384]{1,0:T(8,128)(2...) custom-call(bf16[128,1280]{1,0:T(8,128)(2,1)S(1)} %copy-done.15, ...), custom_call_target="tpu_custom_call" | custom-call | flops 1 | bytes 1 | tf_op jit(solution)/shard_map/pallas_call | solution.py:31
  44.3 13.2 %shard_map.104 = (bf16[128,1152]{1,0:T(8,128)(2,1)S(1)}, bf16[128,1152]{1,0:T(8,128)(2,1)}, bf16[128,1152]{1,0:T(8,128)(2,1)}, bf16[128,1152]{1,0:T(8,128)(2,1)S...) custom-call(bf16[512,384]{1,0:T(8,128)(2,1)S(1)} %get-tuple-element.50.q_ref, ...), custom_call_target="tpu_custom_call" | custom-call | flops 1 | bytes 1 | tf_op jit(solution)/shard_map/pallas_call | solution.py:31
  59.4 1.0 collective-permute-start.6
  60.3 2.5 %collective-permute-start.7 = (bf16[128,1152]{1,0:T(8,128)(2,1)}, bf16[128,1152]{1,0:T(8,128)(2,1)S(1)}, u32[]{:S(2)}, u32[]{:S(2)}) collective-permute-start(bf16[128,1152]{1,0:T(8,128)(2,1)} %get-tuple-element.66), channel_id=1, source_target_pairs={{224,0},{33,1},{226,2},{35,3},{228,4},{37,5},{230,6},{39,7},{232,8... | collective-permute-start | bytes 884744 | tf_op jit(solution)/shard_map/ppermute | solution.py:370
  62.9 5.4 %collective-permute-start.8 = (bf16[128,1152]{1,0:T(8,128)(2,1)S(1)}, bf16[128,1152]{1,0:T(8,128)(2,1)S(1)}, u32[]{:S(2)}, u32[]{:S(2)}) collective-permute-start(bf16[128,1152]{1,0:T(8,128)(2,1)S(1)} %get-tuple-element.67), channel_id=1, source_target_pairs={{63,0},{224,1},{33,2},{226,3},{35,4},{228,5},{37,6},{230,7},{39,8}... | collective-permute-start | bytes 884744 | tf_op jit(solution)/shard_map/ppermute | solution.py:370
  69.0 17.9 %all_to_all.34 = bf16[32,2,768]{2,1,0:T(2,128)(2,1)S(1)} all-to-all(bf16[32,2,768]{2,1,0:T(2,128)(2,1)S(1)} %reshape.394), channel_id=1, replica_groups=mesh['zh'=2,'x'=4,'zl'=4,'y'=4,'core'=2] {'zl','y','core'}, dimensions={0} | all-to-all | bytes 196608 | tf_op jit(solution)/shard_map/all_to_all | solution.py:440
  87.1 1.4 %copy-done.14 = bf16[768,512]{1,0:T(8,128)(2,1)S(1)} copy-done((bf16[768,512]{1,0:T(8,128)(2,1)S(1)}, bf16[768,512]{1,0:T(8,128)(2,1)}, u32[]{:S(2)}) %copy-start.14) | copy-done | bytes 786456
  90.8 2.6 %shard_map.107 = bf16[16,24,1792]{2,1,0:T(8,128)(2,1)} custom-call(bf16[384,1152]{1,0:T(8,128)(2,1)S(1)} %copy-done.12, bf16[384,1152]{1,0:T(8,128)(2,1)} %collective-permute-done.5.other_ref, bf16[384,384]{1,0:T(8,128)(2,1)S(1)} %get-tuple-element.74.out_keep_ref, bf16[384,384]{1,0:T(8,128)(2,1)S(1)} %collective-permute-done.9.out_other_ref, ...), custom_call_target="tpu_custom_call" | custom-call | flops 1 | bytes 1 | tf_op jit(solution)/shard_map/pallas_call | solution.py:31
  93.3 4.3 %all-to-all-start.2 = ((bf16[16,24,1792]{2,1,0:T(8,128)(2,1)}), bf16[16,24,1792]{2,1,0:T(8,128)(2,1)S(1)}, u32[]{:S(2)}, u32[]{:S(2)}) async-start(bf16[16,24,1792]{2,1,0:T(8,128)(2,1)} %shard_map.107), calls=%async_computation.2 | async-start | bytes 2752512 | tf_op jit(solution)/shard_map/all_to_all | solution.py:456
  97.6 5.3 %collective-permute-start.10 = (f32[1,768]{1,0:T(1,128)S(1)}, f32[1,768]{1,0:T(1,128)S(1)}, u32[]{:S(2)}, u32[]{:S(2)}) collective-permute-start(f32[1,768]{1,0:T(1,128)S(1)} %copy-done.17), channel_id=1, source_target_pairs={{0,224},{1,225},{2,226},{3,227},{4,228},{5,229},{6,230},{7,231},{8... | collective-permute-start | bytes 9224 | tf_op jit(solution)/shard_map/ppermute | solution.py:370
  103.0 1.0 copy-done.5
  104.9 1.1 copy-done.10
  106.0 1.6 %shard_map.108 = bf16[8,8,8,768]{3,2,1,0:T(8,128)(2,1)} custom-call(bf16[8,8,8,768]{3,2,1,0:T(8,128)(2,1)S(1)} %copy-done.1, bf16[128,1152]{1,0:T(8,128)(2,1)S(1)} %collective-permute-done.6.b0_ref, bf16[128,1152]{1,0:T(8,128)(2,1)S(1)} %copy-done.5, bf16[128,1152]{1,0:T(8,128)(2,1)S(1)} %copy-done.8, bf16[128,1152]{1,0:T(8,128)(2,1)S(1)} %get-tuple-element.73.b3_ref, ...), custom_call_target="tpu_custom_call" | custom-call | flops 1 | bytes 1 | tf_op jit(solution)/shard_map/pallas_call | solution.py:31
  107.5 6.7 %collective-permute-done.10.next_ref = f32[1,768]{1,0:T(1,128)S(1)} collective-permute-done((f32[1,768]{1,0:T(1,128)S(1)}, f32[1,768]{1,0:T(1,128)S(1)}, u32[]{:S(2)}, u32[]{:S(2)}) %collective-permute-start.10) | collective-permute-done | bytes 3104 | tf_op jit(solution)/shard_map/ppermute | solution.py:370
  114.2 2.1 %shard_map.109 = bf16[8,8,8,768]{3,2,1,0:T(8,128)(2,1)} custom-call(bf16[8,8,8,768]{3,2,1,0:T(8,128)(2,1)S(1)} %copy-done.1, bf16[8,8,8,768]{3,2,1,0:T(8,128)(2,1)S(1)} %copy-done.2, bf16[128,1152]{1,0:T(8,128)(2,1)S(1)} %collective-permute-done.6.b0_ref, bf16[128,1152]{1,0:T(8,128)(2,1)S(1)} %copy-done.6, bf16[128,1152]{1,0:T(8,128)(2,1)S(1)} %copy-done.9, ...), custom_call_target="tpu_custom_call" | custom-call | flops 1 | bytes 1 | tf_op jit(solution)/shard_map/pallas_call | solution.py:31
  117.6 13.1 %all_to_all.35.in_ref = bf16[8,8,896]{2,1,0:T(8,128)(2,1)S(1)} all-to-all(bf16[8,8,896]{2,1,0:T(8,128)(2,1)S(1)} %shard_map.110), channel_id=1, replica_groups=mesh['zh'=2,'x'=4,'zl'=4,'y'=4,'core'=2] {'zh','zl'}, dimensions={0} | all-to-all | bytes 229376 | tf_op jit(solution)/shard_map/all_to_all | solution.py:464
  (66 shorter events, 12.6 us)
Async XLA Ops:
  0.6 29.2 %copy-start.2 = (bf16[8,8,8,768]{3,2,1,0:T(8,128)(2,1)S(1)}, bf16[8,8,8,768]{3,2,1,0:T(8,128)(2,1)}, u32[]{:S(2)}) copy-start(bf16[8,8,8,768]{3,2,1,0:T(8,128)(2,1)} %cot_ref.3) | copy-start | bytes 2359300
  5.3 35.3 %copy-start = (bf16[768,1152]{1,0:T(8,128)(2,1)S(1)}, bf16[768,1152]{1,0:T(8,128)(2,1)}, u32[]{:S(2)}) copy-start(bf16[768,1152]{1,0:T(8,128)(2,1)} %wi_ref.3) | copy-start | bytes 5308420
  5.3 35.3 %copy-start.15 = (bf16[128,1280]{1,0:T(8,128)(2,1)S(1)}, bf16[128,1280]{1,0:T(8,128)(2,1)}, u32[]{:S(2)}) copy-start(bf16[128,1280]{1,0:T(8,128)(2,1)} %get-tuple-element.46.own_ref) | copy-start | bytes 983044
  5.3 16.9 %collective-permute-start.3 = (bf16[1,1536]{1,0:T(2,128)(2,1)}, bf16[1,1536]{1,0:T(2,128)(2,1)S(1)}, u32[]{:S(2)}, u32[]{:S(2)}) collective-permute-start(bf16[1,1536]{1,0:T(2,128)(2,1)} %get-tuple-element.55), channel_id=1, source_target_pairs={{0,32},{1,33},{2,34},{3,35},{4,36},{5,37},{6,38},{7,39},{8,40},{9,... | collective-permute-start | bytes 9224 | tf_op jit(solution)/shard_map/ppermute | solution.py:370
  7.4 33.1 %collective-permute-start = (bf16[128,1280]{1,0:T(8,128)(2,1)}, bf16[128,1280]{1,0:T(8,128)(2,1)}, u32[]{:S(2)}, u32[]{:S(2)}) collective-permute-start(bf16[128,1280]{1,0:T(8,128)(2,1)} %get-tuple-element.47), channel_id=1, source_target_pairs={{0,31},{1,0},{2,1},{3,2},{4,3},{5,4},{6,5},{7,6},{8,7},{9,8},{10,9... | collective-permute-start | bytes 983048 | tf_op jit(solution)/shard_map/ppermute | solution.py:370
  8.7 31.9 %collective-permute-start.1 = (bf16[128,1280]{1,0:T(8,128)(2,1)}, bf16[128,1280]{1,0:T(8,128)(2,1)}, u32[]{:S(2)}, u32[]{:S(2)}) collective-permute-start(bf16[128,1280]{1,0:T(8,128)(2,1)} %get-tuple-element.48), channel_id=1, source_target_pairs={{0,224},{1,33},{2,226},{3,35},{4,228},{5,37},{6,230},{7,39},{8,232... | collective-permute-start | bytes 983048 | tf_op jit(solution)/shard_map/ppermute | solution.py:370
  9.6 31.0 %collective-permute-start.2 = (bf16[128,1280]{1,0:T(8,128)(2,1)}, bf16[128,1280]{1,0:T(8,128)(2,1)}, u32[]{:S(2)}, u32[]{:S(2)}) collective-permute-start(bf16[128,1280]{1,0:T(8,128)(2,1)} %get-tuple-element.49), channel_id=1, source_target_pairs={{0,63},{1,224},{2,33},{3,226},{4,35},{5,228},{6,37},{7,230},{8,39}... | collective-permute-start | bytes 983048 | tf_op jit(solution)/shard_map/ppermute | solution.py:370
  24.1 16.4 %all-to-all-start = ((bf16[32,2,384]{2,1,0:T(2,128)(2,1)}), bf16[32,2,384]{2,1,0:T(2,128)(2,1)S(1)}, u32[]{:S(2)}, u32[]{:S(2)}) async-start(bf16[32,2,384]{2,1,0:T(2,128)(2,1)} %reshape.392), calls=%async_computation | async-start | bytes 98304 | tf_op jit(solution)/shard_map/all_to_all | solution.py:416
  27.7 2.1 %collective-permute-start.4 = (bf16[1,1536]{1,0:T(2,128)(2,1)S(1)}, bf16[1,1536]{1,0:T(2,128)(2,1)S(1)}, u32[]{:S(2)}, u32[]{:S(2)}) collective-permute-start(bf16[1,1536]{1,0:T(2,128)(2,1)S(1)} %pad_maximum_fusion.here_ref), channel_id=1, source_target_pairs={{0,1},{1,0},{2,3},{3,2},{4,5},{5,4},{6,7},{7,6},{8,9},{9,8},{10,11... | collective-permute-start | bytes 9224 | tf_op jit(solution)/shard_map/ppermute | solution.py:415
  58.4 28.6 %collective-permute-start.5 = (bf16[384,1152]{1,0:T(8,128)(2,1)}, bf16[384,1152]{1,0:T(8,128)(2,1)}, u32[]{:S(2)}, u32[]{:S(2)}) collective-permute-start(bf16[384,1152]{1,0:T(8,128)(2,1)} %get-tuple-element.64), channel_id=1, source_target_pairs={{0,1},{1,0},{2,3},{3,2},{4,5},{5,4},{6,7},{7,6},{8,9},{9,8},{10,11... | collective-permute-start | bytes 2654216 | tf_op jit(solution)/shard_map/ppermute | solution.py:443
  59.4 27.6 %collective-permute-start.6 = (bf16[128,1152]{1,0:T(8,128)(2,1)}, bf16[128,1152]{1,0:T(8,128)(2,1)S(1)}, u32[]{:S(2)}, u32[]{:S(2)}) collective-permute-start(bf16[128,1152]{1,0:T(8,128)(2,1)} %get-tuple-element.65), channel_id=1, source_target_pairs={{31,0},{0,1},{1,2},{2,3},{3,4},{4,5},{5,6},{6,7},{7,8},{8,9},{9,10... | collective-permute-start | bytes 884744 | tf_op jit(solution)/shard_map/ppermute | solution.py:370
  60.3 26.7 %collective-permute-start.7 = (bf16[128,1152]{1,0:T(8,128)(2,1)}, bf16[128,1152]{1,0:T(8,128)(2,1)S(1)}, u32[]{:S(2)}, u32[]{:S(2)}) collective-permute-start(bf16[128,1152]{1,0:T(8,128)(2,1)} %get-tuple-element.66), channel_id=1, source_target_pairs={{224,0},{33,1},{226,2},{35,3},{228,4},{37,5},{230,6},{39,7},{232,8... | collective-permute-start | bytes 884744 | tf_op jit(solution)/shard_map/ppermute | solution.py:370
  62.9 24.2 %collective-permute-start.8 = (bf16[128,1152]{1,0:T(8,128)(2,1)S(1)}, bf16[128,1152]{1,0:T(8,128)(2,1)S(1)}, u32[]{:S(2)}, u32[]{:S(2)}) collective-permute-start(bf16[128,1152]{1,0:T(8,128)(2,1)S(1)} %get-tuple-element.67), channel_id=1, source_target_pairs={{63,0},{224,1},{33,2},{226,3},{35,4},{228,5},{37,6},{230,7},{39,8}... | collective-permute-start | bytes 884744 | tf_op jit(solution)/shard_map/ppermute | solution.py:370
  86.9 3.9 %copy-start.12 = (bf16[384,1152]{1,0:T(8,128)(2,1)S(1)}, bf16[384,1152]{1,0:T(8,128)(2,1)}, u32[]{:S(2)}) copy-start(bf16[384,1152]{1,0:T(8,128)(2,1)} %copy-done.11) | copy-start | bytes 2654212
  87.0 3.7 %copy-start.4 = (bf16[128,1152]{1,0:T(8,128)(2,1)}, bf16[128,1152]{1,0:T(8,128)(2,1)S(1)}, u32[]{:S(2)}) copy-start(bf16[128,1152]{1,0:T(8,128)(2,1)S(1)} %collective-permute-done.7.b1_ref) | copy-start | bytes 884740
  87.0 3.7 %copy-start.7 = (bf16[128,1152]{1,0:T(8,128)(2,1)}, bf16[128,1152]{1,0:T(8,128)(2,1)S(1)}, u32[]{:S(2)}) copy-start(bf16[128,1152]{1,0:T(8,128)(2,1)S(1)} %collective-permute-done.8.b2_ref) | copy-start | bytes 884740
  89.1 1.7 %collective-permute-start.9 = (bf16[384,384]{1,0:T(8,128)(2,1)S(1)}, bf16[384,384]{1,0:T(8,128)(2,1)S(1)}, u32[]{:S(2)}, u32[]{:S(2)}) collective-permute-start(bf16[384,384]{1,0:T(8,128)(2,1)S(1)} %get-tuple-element.75), channel_id=1, source_target_pairs={{0,1},{1,0},{2,3},{3,2},{4,5},{5,4},{6,7},{7,6},{8,9},{9,8},{10,11... | collective-permute-start | bytes 884744 | tf_op jit(solution)/shard_map/ppermute | solution.py:448
  93.3 4.3 %copy-start.17 = (f32[1,768]{1,0:T(1,128)S(1)}, f32[1,768]{1,0:T(1,128)}, u32[]{:S(2)}) copy-start(f32[1,768]{1,0:T(1,128)} %copy-done.16) | copy-start | bytes 9220
  93.3 9.7 %copy-start.1 = (bf16[8,8,8,768]{3,2,1,0:T(8,128)(2,1)S(1)}, bf16[8,8,8,768]{3,2,1,0:T(8,128)(2,1)}, u32[]{:S(2)}) copy-start(bf16[8,8,8,768]{3,2,1,0:T(8,128)(2,1)} %tok_ref.3) | copy-start | bytes 2359300
  93.3 23.4 %all-to-all-start.2 = ((bf16[16,24,1792]{2,1,0:T(8,128)(2,1)}), bf16[16,24,1792]{2,1,0:T(8,128)(2,1)S(1)}, u32[]{:S(2)}, u32[]{:S(2)}) async-start(bf16[16,24,1792]{2,1,0:T(8,128)(2,1)} %shard_map.107), calls=%async_computation.2 | async-start | bytes 2752512 | tf_op jit(solution)/shard_map/all_to_all | solution.py:456
  97.6 16.6 %copy-start.3 = (bf16[768,768]{1,0:T(8,128)(2,1)S(1)}, bf16[768,768]{1,0:T(8,128)(2,1)}, u32[]{:S(2)}) copy-start(bf16[768,768]{1,0:T(8,128)(2,1)} %wc_ref.1) | copy-start | bytes 3538948
  97.6 16.6 %collective-permute-start.10 = (f32[1,768]{1,0:T(1,128)S(1)}, f32[1,768]{1,0:T(1,128)S(1)}, u32[]{:S(2)}, u32[]{:S(2)}) collective-permute-start(f32[1,768]{1,0:T(1,128)S(1)} %copy-done.17), channel_id=1, source_target_pairs={{0,224},{1,225},{2,226},{3,227},{4,228},{5,229},{6,230},{7,231},{8... | collective-permute-start | bytes 9224 | tf_op jit(solution)/shard_map/ppermute | solution.py:370
  106.0 8.2 %copy-start.6 = (bf16[128,1152]{1,0:T(8,128)(2,1)S(1)}, bf16[128,1152]{1,0:T(8,128)(2,1)}, u32[]{:S(2)}) copy-start(bf16[128,1152]{1,0:T(8,128)(2,1)} %copy-done.4) | copy-start | bytes 884740
  106.0 8.2 %copy-start.9 = (bf16[128,1152]{1,0:T(8,128)(2,1)S(1)}, bf16[128,1152]{1,0:T(8,128)(2,1)}, u32[]{:S(2)}) copy-start(bf16[128,1152]{1,0:T(8,128)(2,1)} %copy-done.7) | copy-start | bytes 884740
  (7 other events, 6.8 us)

commit v6 on v5

--- a/solution.py
+++ b/solution.py
@@ -228,7 +228,7 @@
         grad_ref[rows, lanes] = (jnp.concatenate(grads, axis=0).T * 0.125).astype(bf16)
         return 0
 
-    lax.fori_loop(0, inner // PAIR * chunks, step, 0)
+    lax.fori_loop(0, inner // PAIR * chunks, step, 0, unroll=True)
     grad_ref[:, inner : 2 * inner] = dk_ref[:tokens].astype(bf16)
     grad_ref[:, 2 * inner :] = dv_ref[:tokens].astype(bf16)
     peers = coarse_ref.shape[0]

time: 133 us -> 132 us (level)
  no operation moved by 1% of the time
where the time goes in v6:
time: 132 us; the launch traced here: 131 us
  starting transfers between devices  40 us (30%)
  blocking collectives  30.9 us (23%)
  Pallas kernels  30.7 us (23%)
  waiting for transfers between devices  15.9 us (12%)
  local copies, waits for them, and re-layouts  8.91 us (7%)
  other arithmetic  3.18 us (2%)
    pallas_call x11, Pallas kernels, call(): pl.pallas_call(kernel, out_shape=[jax.ShapeDtypeStruct(s, d) for s, d in...  30.7 us
    ppermute x8, starting transfers between devices, passed(): return lax.ppermute(block, ALL, route)  30.4 us
    all_to_all x1, blocking collectives, body(): parts = lax.all_to_all(coarse_part, GZ, 0, 0, tiled=True)  17.9 us
    all_to_all x1, blocking collectives, body(): slab = lax.all_to_all(slab, ('zh', 'zl'), 0, 0, tiled=True)  13 us
    all_to_all x1, waiting for transfers between devices, body(): kv = lax.all_to_all(kv, GZ, 0, 0, tiled=True)  8.27 us
    unnamed x42, local copies, waits for them, and re-layouts  7.65 us
    ppermute x8, waiting for transfers between devices, passed(): return lax.ppermute(block, ALL, route)  6.68 us
    all_to_all x1, starting transfers between devices, body(): packet = lax.all_to_all(packet, ('x', 'y'), 0, 0, tiled=True)  4.27 us
  transfers between devices with their start and end apart: 13, of which 4 were waited for; matrix products, arithmetic and copies ran while one was open for 4% of the time, Pallas kernels for 4%

profile of v6, /device:TPU:1, one launch (start us, length us, event | category | flops | bytes accessed | tf_op | source)
XLA Modules:
  0.0 130.5 jit_solution(10118829940417327938)
XLA Ops:
  0.6 4.6 %shard_map.101 = (bf16[128,1280]{1,0:T(8,128)(2,1)}, bf16[128,1280]{1,0:T(8,128)(2,1)}, bf16[128,1280]{1,0:T(8,128)(2,1)}, bf16[128,1280]{1,0:T(8,128)(2,1)}, bf16[1,1536]{1,0:T(2,128)(2,1)}) custom-call(bf16[8,8,8,768]{3,2,1,0:T(8,128)(2,1)} %tok_ref.3, bf16[8,8,8,768]{3,2,1,0:T(8,128)(2,1)} %cot_ref.3, bf16[384,768]{1,0:T(8,128)(2,1)} %wo_ref.1, ...), custom_call_target="tpu_custom_call" | custom-call | flops 1 | bytes 1 | tf_op jit(solution)/shard_map/pallas_call | solution.py:31
  5.3 2.1 %collective-permute-start.3 = (bf16[1,1536]{1,0:T(2,128)(2,1)}, bf16[1,1536]{1,0:T(2,128)(2,1)S(1)}, u32[]{:S(2)}, u32[]{:S(2)}) collective-permute-start(bf16[1,1536]{1,0:T(2,128)(2,1)} %get-tuple-element.55), channel_id=1, source_target_pairs={{0,32},{1,33},{2,34},{3,35},{4,36},{5,37},{6,38},{7,39},{8,40},{9,... | collective-permute-start | bytes 9224 | tf_op jit(solution)/shard_map/ppermute | solution.py:370
  7.4 1.3 collective-permute-start
  9.6 11.9 %collective-permute-start.2 = (bf16[128,1280]{1,0:T(8,128)(2,1)}, bf16[128,1280]{1,0:T(8,128)(2,1)}, u32[]{:S(2)}, u32[]{:S(2)}) collective-permute-start(bf16[128,1280]{1,0:T(8,128)(2,1)} %get-tuple-element.49), channel_id=1, source_target_pairs={{0,63},{1,224},{2,33},{3,226},{4,35},{5,228},{6,37},{7,230},{8,39}... | collective-permute-start | bytes 983048 | tf_op jit(solution)/shard_map/ppermute | solution.py:370
  24.1 3.6 %all-to-all-start = ((bf16[32,2,384]{2,1,0:T(2,128)(2,1)}), bf16[32,2,384]{2,1,0:T(2,128)(2,1)S(1)}, u32[]{:S(2)}, u32[]{:S(2)}) async-start(bf16[32,2,384]{2,1,0:T(2,128)(2,1)} %reshape.392), calls=%async_computation | async-start | bytes 98304 | tf_op jit(solution)/shard_map/all_to_all | solution.py:416
  28.0 1.8 %fusion.11.src_ref = s32[768,1]{1,0:T(8,128)S(1)} fusion(s32[]{:T(128)} %axis_index.12), kind=kLoop, calls=%fused_computation.37 | loop fusion | flops 84480 | bytes 3076 | tf_op jit(solution)/shard_map/add | solution.py:424
  29.8 1.5 %shard_map.103 = (bf16[768,512]{1,0:T(8,128)(2,1)S(1)}, f32[8,384]{1,0:T(8,128)S(1)}) custom-call(bf16[8,8,8,768]{3,2,1,0:T(8,128)(2,1)S(1)} %copy-done.2, s32[768,1]{1,0:T(8,128)S(1)} %fusion.11.src_ref, bf16[1,1536]{1,0:T(2,128)(2,1)S(1)} %pad_maximum_fusion.here_ref, bf16[1,1536]{1,0:T(2,128)(2,1)S(1)} %collective-permute-done.4.other_ref, ...), custom_call_target="tpu_custom_call" | custom-call | flops 1 | bytes 1 | tf_op jit(solution)/shard_map/pallas_call | solution.py:31
  32.2 8.3 %all-to-all-done = bf16[32,2,384]{2,1,0:T(2,128)(2,1)S(1)} async-done(((bf16[32,2,384]{2,1,0:T(2,128)(2,1)}), bf16[32,2,384]{2,1,0:T(2,128)(2,1)S(1)}, u32[]{:S(2)}, u32[]{:S(2)}) %all-to-all-start) | async-done | bytes 49184 | tf_op jit(solution)/shard_map/all_to_all | solution.py:416
  40.6 3.6 %shard_map.102 = (bf16[512,384]{1,0:T(8,128)(2,1)S(1)}, bf16[512,384]{1,0:T(8,128)(2,1)S(1)}, bf16[512,384]{1,0:T(8,128)(2,1)S(1)}, bf16[512,384]{1,0:T(8,128)(2...) custom-call(bf16[128,1280]{1,0:T(8,128)(2,1)S(1)} %copy-done.15, ...), custom_call_target="tpu_custom_call" | custom-call | flops 1 | bytes 1 | tf_op jit(solution)/shard_map/pallas_call | solution.py:31
  44.3 12.5 %shard_map.104 = (bf16[128,1152]{1,0:T(8,128)(2,1)S(1)}, bf16[128,1152]{1,0:T(8,128)(2,1)}, bf16[128,1152]{1,0:T(8,128)(2,1)}, bf16[128,1152]{1,0:T(8,128)(2,1)S...) custom-call(bf16[512,384]{1,0:T(8,128)(2,1)S(1)} %get-tuple-element.50.q_ref, ...), custom_call_target="tpu_custom_call" | custom-call | flops 1 | bytes 1 | tf_op jit(solution)/shard_map/pallas_call | solution.py:31
  58.6 1.0 collective-permute-start.6
  59.6 2.6 %collective-permute-start.7 = (bf16[128,1152]{1,0:T(8,128)(2,1)}, bf16[128,1152]{1,0:T(8,128)(2,1)S(1)}, u32[]{:S(2)}, u32[]{:S(2)}) collective-permute-start(bf16[128,1152]{1,0:T(8,128)(2,1)} %get-tuple-element.66), channel_id=1, source_target_pairs={{224,0},{33,1},{226,2},{35,3},{228,4},{37,5},{230,6},{39,7},{232,8... | collective-permute-start | bytes 884744 | tf_op jit(solution)/shard_map/ppermute | solution.py:370
  62.1 5.4 %collective-permute-start.8 = (bf16[128,1152]{1,0:T(8,128)(2,1)S(1)}, bf16[128,1152]{1,0:T(8,128)(2,1)S(1)}, u32[]{:S(2)}, u32[]{:S(2)}) collective-permute-start(bf16[128,1152]{1,0:T(8,128)(2,1)S(1)} %get-tuple-element.67), channel_id=1, source_target_pairs={{63,0},{224,1},{33,2},{226,3},{35,4},{228,5},{37,6},{230,7},{39,8}... | collective-permute-start | bytes 884744 | tf_op jit(solution)/shard_map/ppermute | solution.py:370
  68.3 17.9 %all_to_all.34 = bf16[32,2,768]{2,1,0:T(2,128)(2,1)S(1)} all-to-all(bf16[32,2,768]{2,1,0:T(2,128)(2,1)S(1)} %reshape.394), channel_id=1, replica_groups=mesh['zh'=2,'x'=4,'zl'=4,'y'=4,'core'=2] {'zl','y','core'}, dimensions={0} | all-to-all | bytes 196608 | tf_op jit(solution)/shard_map/all_to_all | solution.py:440
  86.3 1.4 %copy-done.14 = bf16[768,512]{1,0:T(8,128)(2,1)S(1)} copy-done((bf16[768,512]{1,0:T(8,128)(2,1)S(1)}, bf16[768,512]{1,0:T(8,128)(2,1)}, u32[]{:S(2)}) %copy-start.14) | copy-done | bytes 786456
  90.0 2.6 %shard_map.107 = bf16[16,24,1792]{2,1,0:T(8,128)(2,1)} custom-call(bf16[384,1152]{1,0:T(8,128)(2,1)S(1)} %copy-done.12, bf16[384,1152]{1,0:T(8,128)(2,1)} %collective-permute-done.5.other_ref, bf16[384,384]{1,0:T(8,128)(2,1)S(1)} %get-tuple-element.74.out_keep_ref, bf16[384,384]{1,0:T(8,128)(2,1)S(1)} %collective-permute-done.9.out_other_ref, ...), custom_call_target="tpu_custom_call" | custom-call | flops 1 | bytes 1 | tf_op jit(solution)/shard_map/pallas_call | solution.py:31
  92.6 4.3 %all-to-all-start.2 = ((bf16[16,24,1792]{2,1,0:T(8,128)(2,1)}), bf16[16,24,1792]{2,1,0:T(8,128)(2,1)S(1)}, u32[]{:S(2)}, u32[]{:S(2)}) async-start(bf16[16,24,1792]{2,1,0:T(8,128)(2,1)} %shard_map.107), calls=%async_computation.2 | async-start | bytes 2752512 | tf_op jit(solution)/shard_map/all_to_all | solution.py:456
  96.9 5.3 %collective-permute-start.10 = (f32[1,768]{1,0:T(1,128)S(1)}, f32[1,768]{1,0:T(1,128)S(1)}, u32[]{:S(2)}, u32[]{:S(2)}) collective-permute-start(f32[1,768]{1,0:T(1,128)S(1)} %copy-done.17), channel_id=1, source_target_pairs={{0,224},{1,225},{2,226},{3,227},{4,228},{5,229},{6,230},{7,231},{8... | collective-permute-start | bytes 9224 | tf_op jit(solution)/shard_map/ppermute | solution.py:370
  102.2 1.0 copy-done.5
  104.2 1.1 copy-done.10
  105.2 1.6 %shard_map.108 = bf16[8,8,8,768]{3,2,1,0:T(8,128)(2,1)} custom-call(bf16[8,8,8,768]{3,2,1,0:T(8,128)(2,1)S(1)} %copy-done.1, bf16[128,1152]{1,0:T(8,128)(2,1)S(1)} %collective-permute-done.6.b0_ref, bf16[128,1152]{1,0:T(8,128)(2,1)S(1)} %copy-done.5, bf16[128,1152]{1,0:T(8,128)(2,1)S(1)} %copy-done.8, bf16[128,1152]{1,0:T(8,128)(2,1)S(1)} %get-tuple-element.73.b3_ref, ...), custom_call_target="tpu_custom_call" | custom-call | flops 1 | bytes 1 | tf_op jit(solution)/shard_map/pallas_call | solution.py:31
  106.8 6.7 %collective-permute-done.10.next_ref = f32[1,768]{1,0:T(1,128)S(1)} collective-permute-done((f32[1,768]{1,0:T(1,128)S(1)}, f32[1,768]{1,0:T(1,128)S(1)}, u32[]{:S(2)}, u32[]{:S(2)}) %collective-permute-start.10) | collective-permute-done | bytes 3104 | tf_op jit(solution)/shard_map/ppermute | solution.py:370
  113.5 2.1 %shard_map.109 = bf16[8,8,8,768]{3,2,1,0:T(8,128)(2,1)} custom-call(bf16[8,8,8,768]{3,2,1,0:T(8,128)(2,1)S(1)} %copy-done.1, bf16[8,8,8,768]{3,2,1,0:T(8,128)(2,1)S(1)} %copy-done.2, bf16[128,1152]{1,0:T(8,128)(2,1)S(1)} %collective-permute-done.6.b0_ref, bf16[128,1152]{1,0:T(8,128)(2,1)S(1)} %copy-done.6, bf16[128,1152]{1,0:T(8,128)(2,1)S(1)} %copy-done.9, ...), custom_call_target="tpu_custom_call" | custom-call | flops 1 | bytes 1 | tf_op jit(solution)/shard_map/pallas_call | solution.py:31
  116.9 13.0 %all_to_all.35.in_ref = bf16[8,8,896]{2,1,0:T(8,128)(2,1)S(1)} all-to-all(bf16[8,8,896]{2,1,0:T(8,128)(2,1)S(1)} %shard_map.110), channel_id=1, replica_groups=mesh['zh'=2,'x'=4,'zl'=4,'y'=4,'core'=2] {'zh','zl'}, dimensions={0} | all-to-all | bytes 229376 | tf_op jit(solution)/shard_map/all_to_all | solution.py:464
  (66 shorter events, 12.6 us)
Async XLA Ops:
  0.6 29.2 %copy-start.2 = (bf16[8,8,8,768]{3,2,1,0:T(8,128)(2,1)S(1)}, bf16[8,8,8,768]{3,2,1,0:T(8,128)(2,1)}, u32[]{:S(2)}) copy-start(bf16[8,8,8,768]{3,2,1,0:T(8,128)(2,1)} %cot_ref.3) | copy-start | bytes 2359300
  5.3 35.3 %copy-start = (bf16[768,1152]{1,0:T(8,128)(2,1)S(1)}, bf16[768,1152]{1,0:T(8,128)(2,1)}, u32[]{:S(2)}) copy-start(bf16[768,1152]{1,0:T(8,128)(2,1)} %wi_ref.3) | copy-start | bytes 5308420
  5.3 35.3 %copy-start.15 = (bf16[128,1280]{1,0:T(8,128)(2,1)S(1)}, bf16[128,1280]{1,0:T(8,128)(2,1)}, u32[]{:S(2)}) copy-start(bf16[128,1280]{1,0:T(8,128)(2,1)} %get-tuple-element.46.own_ref) | copy-start | bytes 983044
  5.3 16.9 %collective-permute-start.3 = (bf16[1,1536]{1,0:T(2,128)(2,1)}, bf16[1,1536]{1,0:T(2,128)(2,1)S(1)}, u32[]{:S(2)}, u32[]{:S(2)}) collective-permute-start(bf16[1,1536]{1,0:T(2,128)(2,1)} %get-tuple-element.55), channel_id=1, source_target_pairs={{0,32},{1,33},{2,34},{3,35},{4,36},{5,37},{6,38},{7,39},{8,40},{9,... | collective-permute-start | bytes 9224 | tf_op jit(solution)/shard_map/ppermute | solution.py:370
  7.4 33.1 %collective-permute-start = (bf16[128,1280]{1,0:T(8,128)(2,1)}, bf16[128,1280]{1,0:T(8,128)(2,1)}, u32[]{:S(2)}, u32[]{:S(2)}) collective-permute-start(bf16[128,1280]{1,0:T(8,128)(2,1)} %get-tuple-element.47), channel_id=1, source_target_pairs={{0,31},{1,0},{2,1},{3,2},{4,3},{5,4},{6,5},{7,6},{8,7},{9,8},{10,9... | collective-permute-start | bytes 983048 | tf_op jit(solution)/shard_map/ppermute | solution.py:370
  8.7 31.9 %collective-permute-start.1 = (bf16[128,1280]{1,0:T(8,128)(2,1)}, bf16[128,1280]{1,0:T(8,128)(2,1)}, u32[]{:S(2)}, u32[]{:S(2)}) collective-permute-start(bf16[128,1280]{1,0:T(8,128)(2,1)} %get-tuple-element.48), channel_id=1, source_target_pairs={{0,224},{1,33},{2,226},{3,35},{4,228},{5,37},{6,230},{7,39},{8,232... | collective-permute-start | bytes 983048 | tf_op jit(solution)/shard_map/ppermute | solution.py:370
  9.6 31.0 %collective-permute-start.2 = (bf16[128,1280]{1,0:T(8,128)(2,1)}, bf16[128,1280]{1,0:T(8,128)(2,1)}, u32[]{:S(2)}, u32[]{:S(2)}) collective-permute-start(bf16[128,1280]{1,0:T(8,128)(2,1)} %get-tuple-element.49), channel_id=1, source_target_pairs={{0,63},{1,224},{2,33},{3,226},{4,35},{5,228},{6,37},{7,230},{8,39}... | collective-permute-start | bytes 983048 | tf_op jit(solution)/shard_map/ppermute | solution.py:370
  24.1 16.4 %all-to-all-start = ((bf16[32,2,384]{2,1,0:T(2,128)(2,1)}), bf16[32,2,384]{2,1,0:T(2,128)(2,1)S(1)}, u32[]{:S(2)}, u32[]{:S(2)}) async-start(bf16[32,2,384]{2,1,0:T(2,128)(2,1)} %reshape.392), calls=%async_computation | async-start | bytes 98304 | tf_op jit(solution)/shard_map/all_to_all | solution.py:416
  27.7 2.1 %collective-permute-start.4 = (bf16[1,1536]{1,0:T(2,128)(2,1)S(1)}, bf16[1,1536]{1,0:T(2,128)(2,1)S(1)}, u32[]{:S(2)}, u32[]{:S(2)}) collective-permute-start(bf16[1,1536]{1,0:T(2,128)(2,1)S(1)} %pad_maximum_fusion.here_ref), channel_id=1, source_target_pairs={{0,1},{1,0},{2,3},{3,2},{4,5},{5,4},{6,7},{7,6},{8,9},{9,8},{10,11... | collective-permute-start | bytes 9224 | tf_op jit(solution)/shard_map/ppermute | solution.py:415
  57.7 28.7 %collective-permute-start.5 = (bf16[384,1152]{1,0:T(8,128)(2,1)}, bf16[384,1152]{1,0:T(8,128)(2,1)}, u32[]{:S(2)}, u32[]{:S(2)}) collective-permute-start(bf16[384,1152]{1,0:T(8,128)(2,1)} %get-tuple-element.64), channel_id=1, source_target_pairs={{0,1},{1,0},{2,3},{3,2},{4,5},{5,4},{6,7},{7,6},{8,9},{9,8},{10,11... | collective-permute-start | bytes 2654216 | tf_op jit(solution)/shard_map/ppermute | solution.py:443
  58.6 27.7 %collective-permute-start.6 = (bf16[128,1152]{1,0:T(8,128)(2,1)}, bf16[128,1152]{1,0:T(8,128)(2,1)S(1)}, u32[]{:S(2)}, u32[]{:S(2)}) collective-permute-start(bf16[128,1152]{1,0:T(8,128)(2,1)} %get-tuple-element.65), channel_id=1, source_target_pairs={{31,0},{0,1},{1,2},{2,3},{3,4},{4,5},{5,6},{6,7},{7,8},{8,9},{9,10... | collective-permute-start | bytes 884744 | tf_op jit(solution)/shard_map/ppermute | solution.py:370
  59.6 26.7 %collective-permute-start.7 = (bf16[128,1152]{1,0:T(8,128)(2,1)}, bf16[128,1152]{1,0:T(8,128)(2,1)S(1)}, u32[]{:S(2)}, u32[]{:S(2)}) collective-permute-start(bf16[128,1152]{1,0:T(8,128)(2,1)} %get-tuple-element.66), channel_id=1, source_target_pairs={{224,0},{33,1},{226,2},{35,3},{228,4},{37,5},{230,6},{39,7},{232,8... | collective-permute-start | bytes 884744 | tf_op jit(solution)/shard_map/ppermute | solution.py:370
  62.1 24.2 %collective-permute-start.8 = (bf16[128,1152]{1,0:T(8,128)(2,1)S(1)}, bf16[128,1152]{1,0:T(8,128)(2,1)S(1)}, u32[]{:S(2)}, u32[]{:S(2)}) collective-permute-start(bf16[128,1152]{1,0:T(8,128)(2,1)S(1)} %get-tuple-element.67), channel_id=1, source_target_pairs={{63,0},{224,1},{33,2},{226,3},{35,4},{228,5},{37,6},{230,7},{39,8}... | collective-permute-start | bytes 884744 | tf_op jit(solution)/shard_map/ppermute | solution.py:370
  86.2 3.9 %copy-start.12 = (bf16[384,1152]{1,0:T(8,128)(2,1)S(1)}, bf16[384,1152]{1,0:T(8,128)(2,1)}, u32[]{:S(2)}) copy-start(bf16[384,1152]{1,0:T(8,128)(2,1)} %copy-done.11) | copy-start | bytes 2654212
  86.3 3.7 %copy-start.4 = (bf16[128,1152]{1,0:T(8,128)(2,1)}, bf16[128,1152]{1,0:T(8,128)(2,1)S(1)}, u32[]{:S(2)}) copy-start(bf16[128,1152]{1,0:T(8,128)(2,1)S(1)} %collective-permute-done.7.b1_ref) | copy-start | bytes 884740
  86.3 3.7 %copy-start.7 = (bf16[128,1152]{1,0:T(8,128)(2,1)}, bf16[128,1152]{1,0:T(8,128)(2,1)S(1)}, u32[]{:S(2)}) copy-start(bf16[128,1152]{1,0:T(8,128)(2,1)S(1)} %collective-permute-done.8.b2_ref) | copy-start | bytes 884740
  88.3 1.7 %collective-permute-start.9 = (bf16[384,384]{1,0:T(8,128)(2,1)S(1)}, bf16[384,384]{1,0:T(8,128)(2,1)S(1)}, u32[]{:S(2)}, u32[]{:S(2)}) collective-permute-start(bf16[384,384]{1,0:T(8,128)(2,1)S(1)} %get-tuple-element.75), channel_id=1, source_target_pairs={{0,1},{1,0},{2,3},{3,2},{4,5},{5,4},{6,7},{7,6},{8,9},{9,8},{10,11... | collective-permute-start | bytes 884744 | tf_op jit(solution)/shard_map/ppermute | solution.py:448
  92.6 4.3 %copy-start.17 = (f32[1,768]{1,0:T(1,128)S(1)}, f32[1,768]{1,0:T(1,128)}, u32[]{:S(2)}) copy-start(f32[1,768]{1,0:T(1,128)} %copy-done.16) | copy-start | bytes 9220
  92.6 9.6 %copy-start.1 = (bf16[8,8,8,768]{3,2,1,0:T(8,128)(2,1)S(1)}, bf16[8,8,8,768]{3,2,1,0:T(8,128)(2,1)}, u32[]{:S(2)}) copy-start(bf16[8,8,8,768]{3,2,1,0:T(8,128)(2,1)} %tok_ref.3) | copy-start | bytes 2359300
  92.6 23.4 %all-to-all-start.2 = ((bf16[16,24,1792]{2,1,0:T(8,128)(2,1)}), bf16[16,24,1792]{2,1,0:T(8,128)(2,1)S(1)}, u32[]{:S(2)}, u32[]{:S(2)}) async-start(bf16[16,24,1792]{2,1,0:T(8,128)(2,1)} %shard_map.107), calls=%async_computation.2 | async-start | bytes 2752512 | tf_op jit(solution)/shard_map/all_to_all | solution.py:456
  96.9 16.6 %copy-start.3 = (bf16[768,768]{1,0:T(8,128)(2,1)S(1)}, bf16[768,768]{1,0:T(8,128)(2,1)}, u32[]{:S(2)}) copy-start(bf16[768,768]{1,0:T(8,128)(2,1)} %wc_ref.1) | copy-start | bytes 3538948
  96.9 16.6 %collective-permute-start.10 = (f32[1,768]{1,0:T(1,128)S(1)}, f32[1,768]{1,0:T(1,128)S(1)}, u32[]{:S(2)}, u32[]{:S(2)}) collective-permute-start(f32[1,768]{1,0:T(1,128)S(1)} %copy-done.17), channel_id=1, source_target_pairs={{0,224},{1,225},{2,226},{3,227},{4,228},{5,229},{6,230},{7,231},{8... | collective-permute-start | bytes 9224 | tf_op jit(solution)/shard_map/ppermute | solution.py:370
  105.2 8.2 %copy-start.6 = (bf16[128,1152]{1,0:T(8,128)(2,1)S(1)}, bf16[128,1152]{1,0:T(8,128)(2,1)}, u32[]{:S(2)}) copy-start(bf16[128,1152]{1,0:T(8,128)(2,1)} %copy-done.4) | copy-start | bytes 884740
  105.2 8.2 %copy-start.9 = (bf16[128,1152]{1,0:T(8,128)(2,1)S(1)}, bf16[128,1152]{1,0:T(8,128)(2,1)}, u32[]{:S(2)}) copy-start(bf16[128,1152]{1,0:T(8,128)(2,1)} %copy-done.7) | copy-start | bytes 884740
  (7 other events, 6.8 us)

commit v7 on v6

--- a/solution.py
+++ b/solution.py
@@ -383,7 +383,8 @@
 
 
 def returned(own, up, side, both):
-    return passed(up, to_up, True), passed(side, to_side, True), passed(both, to_both, True), own
+    side, both = passed(side, to_side, True), passed(both, to_both, True)
+    return passed(up, to_up, True), side, both, own
 
 
 def body(tokens, body_mask, cotangent, w_in, w_out, w_coarse):
@@ -406,7 +407,7 @@
         grant=60,
         scratch=[pltpu.VMEM(a.shape, bf16) for a in (tokens, cotangent, w_out, w_coarse)] + [pltpu.SemaphoreType.DMA((4,))])
     before = passed(row, lambda a, c: (a + 1, c))
-    up, side, both = passed(up, to_up), passed(side, to_side), passed(both, to_both)
+    side, both, up = passed(side, to_side), passed(both, to_both), passed(up, to_up)
 
     odd = lax.broadcasted_iota(jnp.int32, (coarse, 1), 0) % 2 == 1
     kv = jnp.where(odd, before[:, d:], row[:, d:])

time: 132 us -> 132 us (level)
  no operation moved by 1% of the time
where the time goes in v7:
time: 132 us; the launch traced here: 131 us
  starting transfers between devices  40 us (30%)
  blocking collectives  30.9 us (23%)
  Pallas kernels  30.7 us (23%)
  waiting for transfers between devices  15.9 us (12%)
  local copies, waits for them, and re-layouts  8.91 us (7%)
  other arithmetic  3.18 us (2%)
    pallas_call x11, Pallas kernels, call(): pl.pallas_call(kernel, out_shape=[jax.ShapeDtypeStruct(s, d) for s, d in...  30.7 us
    ppermute x8, starting transfers between devices, passed(): return lax.ppermute(block, ALL, route)  30.4 us
    all_to_all x1, blocking collectives, body(): parts = lax.all_to_all(coarse_part, GZ, 0, 0, tiled=True)  17.9 us
    all_to_all x1, blocking collectives, body(): slab = lax.all_to_all(slab, ('zh', 'zl'), 0, 0, tiled=True)  13 us
    all_to_all x1, waiting for transfers between devices, body(): kv = lax.all_to_all(kv, GZ, 0, 0, tiled=True)  8.27 us
    unnamed x42, local copies, waits for them, and re-layouts  7.65 us
    ppermute x8, waiting for transfers between devices, passed(): return lax.ppermute(block, ALL, route)  6.68 us
    all_to_all x1, starting transfers between devices, body(): packet = lax.all_to_all(packet, ('x', 'y'), 0, 0, tiled=True)  4.27 us
  transfers between devices with their start and end apart: 13, of which 4 were waited for; matrix products, arithmetic and copies ran while one was open for 4% of the time, Pallas kernels for 4%

profile of v7, /device:TPU:1, one launch (start us, length us, event | category | flops | bytes accessed | tf_op | source)
XLA Modules:
  0.0 130.5 jit_solution(10118829940417327938)
XLA Ops:
  0.6 4.6 %shard_map.101 = (bf16[128,1280]{1,0:T(8,128)(2,1)}, bf16[128,1280]{1,0:T(8,128)(2,1)}, bf16[128,1280]{1,0:T(8,128)(2,1)}, bf16[128,1280]{1,0:T(8,128)(2,1)}, bf16[1,1536]{1,0:T(2,128)(2,1)}) custom-call(bf16[8,8,8,768]{3,2,1,0:T(8,128)(2,1)} %tok_ref.3, bf16[8,8,8,768]{3,2,1,0:T(8,128)(2,1)} %cot_ref.3, bf16[384,768]{1,0:T(8,128)(2,1)} %wo_ref.1, ...), custom_call_target="tpu_custom_call" | custom-call | flops 1 | bytes 1 | tf_op jit(solution)/shard_map/pallas_call | solution.py:31
  5.3 2.1 %collective-permute-start.3 = (bf16[1,1536]{1,0:T(2,128)(2,1)}, bf16[1,1536]{1,0:T(2,128)(2,1)S(1)}, u32[]{:S(2)}, u32[]{:S(2)}) collective-permute-start(bf16[1,1536]{1,0:T(2,128)(2,1)} %get-tuple-element.55), channel_id=1, source_target_pairs={{0,32},{1,33},{2,34},{3,35},{4,36},{5,37},{6,38},{7,39},{8,40},{9,... | collective-permute-start | bytes 9224 | tf_op jit(solution)/shard_map/ppermute | solution.py:370
  7.4 1.3 collective-permute-start
  9.6 11.9 %collective-permute-start.2 = (bf16[128,1280]{1,0:T(8,128)(2,1)}, bf16[128,1280]{1,0:T(8,128)(2,1)}, u32[]{:S(2)}, u32[]{:S(2)}) collective-permute-start(bf16[128,1280]{1,0:T(8,128)(2,1)} %get-tuple-element.49), channel_id=1, source_target_pairs={{0,63},{1,224},{2,33},{3,226},{4,35},{5,228},{6,37},{7,230},{8,39}... | collective-permute-start | bytes 983048 | tf_op jit(solution)/shard_map/ppermute | solution.py:370
  24.1 3.6 %all-to-all-start = ((bf16[32,2,384]{2,1,0:T(2,128)(2,1)}), bf16[32,2,384]{2,1,0:T(2,128)(2,1)S(1)}, u32[]{:S(2)}, u32[]{:S(2)}) async-start(bf16[32,2,384]{2,1,0:T(2,128)(2,1)} %reshape.392), calls=%async_computation | async-start | bytes 98304 | tf_op jit(solution)/shard_map/all_to_all | solution.py:417
  28.0 1.8 %fusion.11.src_ref = s32[768,1]{1,0:T(8,128)S(1)} fusion(s32[]{:T(128)} %axis_index.12), kind=kLoop, calls=%fused_computation.37 | loop fusion | flops 84480 | bytes 3076 | tf_op jit(solution)/shard_map/add | solution.py:425
  29.8 1.5 %shard_map.103 = (bf16[768,512]{1,0:T(8,128)(2,1)S(1)}, f32[8,384]{1,0:T(8,128)S(1)}) custom-call(bf16[8,8,8,768]{3,2,1,0:T(8,128)(2,1)S(1)} %copy-done.2, s32[768,1]{1,0:T(8,128)S(1)} %fusion.11.src_ref, bf16[1,1536]{1,0:T(2,128)(2,1)S(1)} %pad_maximum_fusion.here_ref, bf16[1,1536]{1,0:T(2,128)(2,1)S(1)} %collective-permute-done.4.other_ref, ...), custom_call_target="tpu_custom_call" | custom-call | flops 1 | bytes 1 | tf_op jit(solution)/shard_map/pallas_call | solution.py:31
  32.2 8.3 %all-to-all-done = bf16[32,2,384]{2,1,0:T(2,128)(2,1)S(1)} async-done(((bf16[32,2,384]{2,1,0:T(2,128)(2,1)}), bf16[32,2,384]{2,1,0:T(2,128)(2,1)S(1)}, u32[]{:S(2)}, u32[]{:S(2)}) %all-to-all-start) | async-done | bytes 49184 | tf_op jit(solution)/shard_map/all_to_all | solution.py:417
  40.6 3.6 %shard_map.102 = (bf16[512,384]{1,0:T(8,128)(2,1)S(1)}, bf16[512,384]{1,0:T(8,128)(2,1)S(1)}, bf16[512,384]{1,0:T(8,128)(2,1)S(1)}, bf16[512,384]{1,0:T(8,128)(2...) custom-call(bf16[128,1280]{1,0:T(8,128)(2,1)S(1)} %copy-done.15, ...), custom_call_target="tpu_custom_call" | custom-call | flops 1 | bytes 1 | tf_op jit(solution)/shard_map/pallas_call | solution.py:31
  44.3 12.5 %shard_map.104 = (bf16[128,1152]{1,0:T(8,128)(2,1)S(1)}, bf16[128,1152]{1,0:T(8,128)(2,1)}, bf16[128,1152]{1,0:T(8,128)(2,1)}, bf16[128,1152]{1,0:T(8,128)(2,1)S...) custom-call(bf16[512,384]{1,0:T(8,128)(2,1)S(1)} %get-tuple-element.50.q_ref, ...), custom_call_target="tpu_custom_call" | custom-call | flops 1 | bytes 1 | tf_op jit(solution)/shard_map/pallas_call | solution.py:31
  58.6 1.0 collective-permute-start.6
  59.6 2.6 %collective-permute-start.7 = (bf16[128,1152]{1,0:T(8,128)(2,1)}, bf16[128,1152]{1,0:T(8,128)(2,1)S(1)}, u32[]{:S(2)}, u32[]{:S(2)}) collective-permute-start(bf16[128,1152]{1,0:T(8,128)(2,1)} %get-tuple-element.66), channel_id=1, source_target_pairs={{224,0},{33,1},{226,2},{35,3},{228,4},{37,5},{230,6},{39,7},{232,8... | collective-permute-start | bytes 884744 | tf_op jit(solution)/shard_map/ppermute | solution.py:370
  62.1 5.4 %collective-permute-start.8 = (bf16[128,1152]{1,0:T(8,128)(2,1)S(1)}, bf16[128,1152]{1,0:T(8,128)(2,1)S(1)}, u32[]{:S(2)}, u32[]{:S(2)}) collective-permute-start(bf16[128,1152]{1,0:T(8,128)(2,1)S(1)} %get-tuple-element.67), channel_id=1, source_target_pairs={{63,0},{224,1},{33,2},{226,3},{35,4},{228,5},{37,6},{230,7},{39,8}... | collective-permute-start | bytes 884744 | tf_op jit(solution)/shard_map/ppermute | solution.py:370
  68.3 17.9 %all_to_all.34 = bf16[32,2,768]{2,1,0:T(2,128)(2,1)S(1)} all-to-all(bf16[32,2,768]{2,1,0:T(2,128)(2,1)S(1)} %reshape.394), channel_id=1, replica_groups=mesh['zh'=2,'x'=4,'zl'=4,'y'=4,'core'=2] {'zl','y','core'}, dimensions={0} | all-to-all | bytes 196608 | tf_op jit(solution)/shard_map/all_to_all | solution.py:441
  86.3 1.4 %copy-done.14 = bf16[768,512]{1,0:T(8,128)(2,1)S(1)} copy-done((bf16[768,512]{1,0:T(8,128)(2,1)S(1)}, bf16[768,512]{1,0:T(8,128)(2,1)}, u32[]{:S(2)}) %copy-start.14) | copy-done | bytes 786456
  90.0 2.6 %shard_map.107 = bf16[16,24,1792]{2,1,0:T(8,128)(2,1)} custom-call(bf16[384,1152]{1,0:T(8,128)(2,1)S(1)} %copy-done.12, bf16[384,1152]{1,0:T(8,128)(2,1)} %collective-permute-done.5.other_ref, bf16[384,384]{1,0:T(8,128)(2,1)S(1)} %get-tuple-element.74.out_keep_ref, bf16[384,384]{1,0:T(8,128)(2,1)S(1)} %collective-permute-done.9.out_other_ref, ...), custom_call_target="tpu_custom_call" | custom-call | flops 1 | bytes 1 | tf_op jit(solution)/shard_map/pallas_call | solution.py:31
  92.6 4.3 %all-to-all-start.2 = ((bf16[16,24,1792]{2,1,0:T(8,128)(2,1)}), bf16[16,24,1792]{2,1,0:T(8,128)(2,1)S(1)}, u32[]{:S(2)}, u32[]{:S(2)}) async-start(bf16[16,24,1792]{2,1,0:T(8,128)(2,1)} %shard_map.107), calls=%async_computation.2 | async-start | bytes 2752512 | tf_op jit(solution)/shard_map/all_to_all | solution.py:457
  96.9 5.3 %collective-permute-start.10 = (f32[1,768]{1,0:T(1,128)S(1)}, f32[1,768]{1,0:T(1,128)S(1)}, u32[]{:S(2)}, u32[]{:S(2)}) collective-permute-start(f32[1,768]{1,0:T(1,128)S(1)} %copy-done.17), channel_id=1, source_target_pairs={{0,224},{1,225},{2,226},{3,227},{4,228},{5,229},{6,230},{7,231},{8... | collective-permute-start | bytes 9224 | tf_op jit(solution)/shard_map/ppermute | solution.py:370
  102.2 1.0 copy-done.5
  104.2 1.1 copy-done.10
  105.2 1.6 %shard_map.108 = bf16[8,8,8,768]{3,2,1,0:T(8,128)(2,1)} custom-call(bf16[8,8,8,768]{3,2,1,0:T(8,128)(2,1)S(1)} %copy-done.1, bf16[128,1152]{1,0:T(8,128)(2,1)S(1)} %collective-permute-done.6.b0_ref, bf16[128,1152]{1,0:T(8,128)(2,1)S(1)} %copy-done.5, bf16[128,1152]{1,0:T(8,128)(2,1)S(1)} %copy-done.8, bf16[128,1152]{1,0:T(8,128)(2,1)S(1)} %get-tuple-element.73.b3_ref, ...), custom_call_target="tpu_custom_call" | custom-call | flops 1 | bytes 1 | tf_op jit(solution)/shard_map/pallas_call | solution.py:31
  106.8 6.7 %collective-permute-done.10.next_ref = f32[1,768]{1,0:T(1,128)S(1)} collective-permute-done((f32[1,768]{1,0:T(1,128)S(1)}, f32[1,768]{1,0:T(1,128)S(1)}, u32[]{:S(2)}, u32[]{:S(2)}) %collective-permute-start.10) | collective-permute-done | bytes 3104 | tf_op jit(solution)/shard_map/ppermute | solution.py:370
  113.5 2.1 %shard_map.109 = bf16[8,8,8,768]{3,2,1,0:T(8,128)(2,1)} custom-call(bf16[8,8,8,768]{3,2,1,0:T(8,128)(2,1)S(1)} %copy-done.1, bf16[8,8,8,768]{3,2,1,0:T(8,128)(2,1)S(1)} %copy-done.2, bf16[128,1152]{1,0:T(8,128)(2,1)S(1)} %collective-permute-done.6.b0_ref, bf16[128,1152]{1,0:T(8,128)(2,1)S(1)} %copy-done.6, bf16[128,1152]{1,0:T(8,128)(2,1)S(1)} %copy-done.9, ...), custom_call_target="tpu_custom_call" | custom-call | flops 1 | bytes 1 | tf_op jit(solution)/shard_map/pallas_call | solution.py:31
  116.9 13.0 %all_to_all.35.in_ref = bf16[8,8,896]{2,1,0:T(8,128)(2,1)S(1)} all-to-all(bf16[8,8,896]{2,1,0:T(8,128)(2,1)S(1)} %shard_map.110), channel_id=1, replica_groups=mesh['zh'=2,'x'=4,'zl'=4,'y'=4,'core'=2] {'zh','zl'}, dimensions={0} | all-to-all | bytes 229376 | tf_op jit(solution)/shard_map/all_to_all | solution.py:465
  (66 shorter events, 12.6 us)
Async XLA Ops:
  0.6 29.2 %copy-start.2 = (bf16[8,8,8,768]{3,2,1,0:T(8,128)(2,1)S(1)}, bf16[8,8,8,768]{3,2,1,0:T(8,128)(2,1)}, u32[]{:S(2)}) copy-start(bf16[8,8,8,768]{3,2,1,0:T(8,128)(2,1)} %cot_ref.3) | copy-start | bytes 2359300
  5.3 35.3 %copy-start = (bf16[768,1152]{1,0:T(8,128)(2,1)S(1)}, bf16[768,1152]{1,0:T(8,128)(2,1)}, u32[]{:S(2)}) copy-start(bf16[768,1152]{1,0:T(8,128)(2,1)} %wi_ref.3) | copy-start | bytes 5308420
  5.3 35.3 %copy-start.15 = (bf16[128,1280]{1,0:T(8,128)(2,1)S(1)}, bf16[128,1280]{1,0:T(8,128)(2,1)}, u32[]{:S(2)}) copy-start(bf16[128,1280]{1,0:T(8,128)(2,1)} %get-tuple-element.46.own_ref) | copy-start | bytes 983044
  5.3 16.9 %collective-permute-start.3 = (bf16[1,1536]{1,0:T(2,128)(2,1)}, bf16[1,1536]{1,0:T(2,128)(2,1)S(1)}, u32[]{:S(2)}, u32[]{:S(2)}) collective-permute-start(bf16[1,1536]{1,0:T(2,128)(2,1)} %get-tuple-element.55), channel_id=1, source_target_pairs={{0,32},{1,33},{2,34},{3,35},{4,36},{5,37},{6,38},{7,39},{8,40},{9,... | collective-permute-start | bytes 9224 | tf_op jit(solution)/shard_map/ppermute | solution.py:370
  7.4 33.1 %collective-permute-start = (bf16[128,1280]{1,0:T(8,128)(2,1)}, bf16[128,1280]{1,0:T(8,128)(2,1)}, u32[]{:S(2)}, u32[]{:S(2)}) collective-permute-start(bf16[128,1280]{1,0:T(8,128)(2,1)} %get-tuple-element.47), channel_id=1, source_target_pairs={{0,31},{1,0},{2,1},{3,2},{4,3},{5,4},{6,5},{7,6},{8,7},{9,8},{10,9... | collective-permute-start | bytes 983048 | tf_op jit(solution)/shard_map/ppermute | solution.py:370
  8.7 31.9 %collective-permute-start.1 = (bf16[128,1280]{1,0:T(8,128)(2,1)}, bf16[128,1280]{1,0:T(8,128)(2,1)}, u32[]{:S(2)}, u32[]{:S(2)}) collective-permute-start(bf16[128,1280]{1,0:T(8,128)(2,1)} %get-tuple-element.48), channel_id=1, source_target_pairs={{0,224},{1,33},{2,226},{3,35},{4,228},{5,37},{6,230},{7,39},{8,232... | collective-permute-start | bytes 983048 | tf_op jit(solution)/shard_map/ppermute | solution.py:370
  9.6 31.0 %collective-permute-start.2 = (bf16[128,1280]{1,0:T(8,128)(2,1)}, bf16[128,1280]{1,0:T(8,128)(2,1)}, u32[]{:S(2)}, u32[]{:S(2)}) collective-permute-start(bf16[128,1280]{1,0:T(8,128)(2,1)} %get-tuple-element.49), channel_id=1, source_target_pairs={{0,63},{1,224},{2,33},{3,226},{4,35},{5,228},{6,37},{7,230},{8,39}... | collective-permute-start | bytes 983048 | tf_op jit(solution)/shard_map/ppermute | solution.py:370
  24.1 16.4 %all-to-all-start = ((bf16[32,2,384]{2,1,0:T(2,128)(2,1)}), bf16[32,2,384]{2,1,0:T(2,128)(2,1)S(1)}, u32[]{:S(2)}, u32[]{:S(2)}) async-start(bf16[32,2,384]{2,1,0:T(2,128)(2,1)} %reshape.392), calls=%async_computation | async-start | bytes 98304 | tf_op jit(solution)/shard_map/all_to_all | solution.py:417
  27.7 2.1 %collective-permute-start.4 = (bf16[1,1536]{1,0:T(2,128)(2,1)S(1)}, bf16[1,1536]{1,0:T(2,128)(2,1)S(1)}, u32[]{:S(2)}, u32[]{:S(2)}) collective-permute-start(bf16[1,1536]{1,0:T(2,128)(2,1)S(1)} %pad_maximum_fusion.here_ref), channel_id=1, source_target_pairs={{0,1},{1,0},{2,3},{3,2},{4,5},{5,4},{6,7},{7,6},{8,9},{9,8},{10,11... | collective-permute-start | bytes 9224 | tf_op jit(solution)/shard_map/ppermute | solution.py:416
  57.7 28.7 %collective-permute-start.5 = (bf16[384,1152]{1,0:T(8,128)(2,1)}, bf16[384,1152]{1,0:T(8,128)(2,1)}, u32[]{:S(2)}, u32[]{:S(2)}) collective-permute-start(bf16[384,1152]{1,0:T(8,128)(2,1)} %get-tuple-element.64), channel_id=1, source_target_pairs={{0,1},{1,0},{2,3},{3,2},{4,5},{5,4},{6,7},{7,6},{8,9},{9,8},{10,11... | collective-permute-start | bytes 2654216 | tf_op jit(solution)/shard_map/ppermute | solution.py:444
  58.6 27.7 %collective-permute-start.6 = (bf16[128,1152]{1,0:T(8,128)(2,1)}, bf16[128,1152]{1,0:T(8,128)(2,1)S(1)}, u32[]{:S(2)}, u32[]{:S(2)}) collective-permute-start(bf16[128,1152]{1,0:T(8,128)(2,1)} %get-tuple-element.65), channel_id=1, source_target_pairs={{31,0},{0,1},{1,2},{2,3},{3,4},{4,5},{5,6},{6,7},{7,8},{8,9},{9,10... | collective-permute-start | bytes 884744 | tf_op jit(solution)/shard_map/ppermute | solution.py:370
  59.6 26.7 %collective-permute-start.7 = (bf16[128,1152]{1,0:T(8,128)(2,1)}, bf16[128,1152]{1,0:T(8,128)(2,1)S(1)}, u32[]{:S(2)}, u32[]{:S(2)}) collective-permute-start(bf16[128,1152]{1,0:T(8,128)(2,1)} %get-tuple-element.66), channel_id=1, source_target_pairs={{224,0},{33,1},{226,2},{35,3},{228,4},{37,5},{230,6},{39,7},{232,8... | collective-permute-start | bytes 884744 | tf_op jit(solution)/shard_map/ppermute | solution.py:370
  62.1 24.2 %collective-permute-start.8 = (bf16[128,1152]{1,0:T(8,128)(2,1)S(1)}, bf16[128,1152]{1,0:T(8,128)(2,1)S(1)}, u32[]{:S(2)}, u32[]{:S(2)}) collective-permute-start(bf16[128,1152]{1,0:T(8,128)(2,1)S(1)} %get-tuple-element.67), channel_id=1, source_target_pairs={{63,0},{224,1},{33,2},{226,3},{35,4},{228,5},{37,6},{230,7},{39,8}... | collective-permute-start | bytes 884744 | tf_op jit(solution)/shard_map/ppermute | solution.py:370
  86.2 3.9 %copy-start.12 = (bf16[384,1152]{1,0:T(8,128)(2,1)S(1)}, bf16[384,1152]{1,0:T(8,128)(2,1)}, u32[]{:S(2)}) copy-start(bf16[384,1152]{1,0:T(8,128)(2,1)} %copy-done.11) | copy-start | bytes 2654212
  86.3 3.7 %copy-start.4 = (bf16[128,1152]{1,0:T(8,128)(2,1)}, bf16[128,1152]{1,0:T(8,128)(2,1)S(1)}, u32[]{:S(2)}) copy-start(bf16[128,1152]{1,0:T(8,128)(2,1)S(1)} %collective-permute-done.7.b1_ref) | copy-start | bytes 884740
  86.3 3.7 %copy-start.7 = (bf16[128,1152]{1,0:T(8,128)(2,1)}, bf16[128,1152]{1,0:T(8,128)(2,1)S(1)}, u32[]{:S(2)}) copy-start(bf16[128,1152]{1,0:T(8,128)(2,1)S(1)} %collective-permute-done.8.b2_ref) | copy-start | bytes 884740
  88.3 1.7 %collective-permute-start.9 = (bf16[384,384]{1,0:T(8,128)(2,1)S(1)}, bf16[384,384]{1,0:T(8,128)(2,1)S(1)}, u32[]{:S(2)}, u32[]{:S(2)}) collective-permute-start(bf16[384,384]{1,0:T(8,128)(2,1)S(1)} %get-tuple-element.75), channel_id=1, source_target_pairs={{0,1},{1,0},{2,3},{3,2},{4,5},{5,4},{6,7},{7,6},{8,9},{9,8},{10,11... | collective-permute-start | bytes 884744 | tf_op jit(solution)/shard_map/ppermute | solution.py:449
  92.6 4.3 %copy-start.17 = (f32[1,768]{1,0:T(1,128)S(1)}, f32[1,768]{1,0:T(1,128)}, u32[]{:S(2)}) copy-start(f32[1,768]{1,0:T(1,128)} %copy-done.16) | copy-start | bytes 9220
  92.6 9.6 %copy-start.1 = (bf16[8,8,8,768]{3,2,1,0:T(8,128)(2,1)S(1)}, bf16[8,8,8,768]{3,2,1,0:T(8,128)(2,1)}, u32[]{:S(2)}) copy-start(bf16[8,8,8,768]{3,2,1,0:T(8,128)(2,1)} %tok_ref.3) | copy-start | bytes 2359300
  92.6 23.4 %all-to-all-start.2 = ((bf16[16,24,1792]{2,1,0:T(8,128)(2,1)}), bf16[16,24,1792]{2,1,0:T(8,128)(2,1)S(1)}, u32[]{:S(2)}, u32[]{:S(2)}) async-start(bf16[16,24,1792]{2,1,0:T(8,128)(2,1)} %shard_map.107), calls=%async_computation.2 | async-start | bytes 2752512 | tf_op jit(solution)/shard_map/all_to_all | solution.py:457
  96.9 16.6 %copy-start.3 = (bf16[768,768]{1,0:T(8,128)(2,1)S(1)}, bf16[768,768]{1,0:T(8,128)(2,1)}, u32[]{:S(2)}) copy-start(bf16[768,768]{1,0:T(8,128)(2,1)} %wc_ref.1) | copy-start | bytes 3538948
  96.9 16.6 %collective-permute-start.10 = (f32[1,768]{1,0:T(1,128)S(1)}, f32[1,768]{1,0:T(1,128)S(1)}, u32[]{:S(2)}, u32[]{:S(2)}) collective-permute-start(f32[1,768]{1,0:T(1,128)S(1)} %copy-done.17), channel_id=1, source_target_pairs={{0,224},{1,225},{2,226},{3,227},{4,228},{5,229},{6,230},{7,231},{8... | collective-permute-start | bytes 9224 | tf_op jit(solution)/shard_map/ppermute | solution.py:370
  105.2 8.2 %copy-start.6 = (bf16[128,1152]{1,0:T(8,128)(2,1)S(1)}, bf16[128,1152]{1,0:T(8,128)(2,1)}, u32[]{:S(2)}) copy-start(bf16[128,1152]{1,0:T(8,128)(2,1)} %copy-done.4) | copy-start | bytes 884740
  105.2 8.2 %copy-start.9 = (bf16[128,1152]{1,0:T(8,128)(2,1)S(1)}, bf16[128,1152]{1,0:T(8,128)(2,1)}, u32[]{:S(2)}) copy-start(bf16[128,1152]{1,0:T(8,128)(2,1)} %copy-done.7) | copy-start | bytes 884740
  (7 other events, 6.8 us)
